TPU v7x, 32 devices: a whole 2x2x4 slice. The times are simulated.
32 devices in a mesh: pipe: 8 (over z, y), tp: 4 (over x, core).
Axes of the slice: x: 2, y: 2, z: 4, core: 2. Of those that a mesh axis runs over, the one named last changes fastest.
Arguments:
- fwd_resid: bfloat16 [8, 512, 4096], P('pipe', 'tp'), may hold values from -6 to 6
- fwd_query: bfloat16 [8, 512, 4096], P('pipe', None, 'tp'), may hold values from -28 to 28
- fwd_keyval: bfloat16 [8, 2, 512, 1024], P('pipe', None, None, 'tp'), may hold values from -8 to 8
- fwd_micro: int32 [8], P('pipe'), may hold values from 0 to 3
- bwd_query: bfloat16 [8, 512, 4096], P('pipe', None, 'tp'), may hold values from -28 to 28
- bwd_keyval: bfloat16 [8, 2, 512, 1024], P('pipe', None, None, 'tp'), may hold values from -8 to 8
- grad_micro: int32 [8], P('pipe'), may hold values from 0 to 3
- grad_in: bfloat16 [8, 512, 4096], P('pipe', 'tp'), may hold values from -6 to 6
- out_weight: bfloat16 [8, 4096, 4096], P('pipe', 'tp'), may hold values from -0.09375 to 0.09375
- doc_starts: int32 [4, 4], replicated, may hold values from 0 to 511, as said below
Outputs:
- fwd_out: bfloat16 [8, 512, 4096], P('pipe', 'tp')
- grad_query: bfloat16 [8, 512, 4096], P('pipe', None, 'tp')
- grad_keyval: bfloat16 [8, 2, 512, 1024], P('pipe', None, None, 'tp')
- grad_weight: bfloat16 [8, 4096, 4096], P('pipe', 'tp')
Inputs may be any that keep to these rules, and one draw needn't show every extreme that they name: `doc_starts`: row m holds the first rows of the 4 documents of micro-batch m: it begins with 0 and rises strictly.
All inputs are finite; a program needn't handle non-finite values.
Results may differ from a plain program's by a relative error of at most 0.007.
Values may be sent and summed in bfloat16 or wider, within the bound.
No kernel may reach another device: no remote copies, remote signals or barrier semaphores. Data moves between devices by JAX's collectives and lax.ppermute only.
A program may use at most 128 MiB of HBM per device.

v0:
```python
import math

import jax
import jax.numpy as jnp
from jax import lax
from jax.sharding import PartitionSpec as P

HD = 128


def from_behind(value, axis, steps):
    count = lax.axis_size(axis)
    pairs = [(source, (source + steps) % count) for source in range(count)]
    return lax.ppermute(value, axis, pairs)


def doc_allowed(starts, row_count):
    position = jnp.arange(row_count, dtype=jnp.int32)
    segment = jnp.sum((starts[None, :] <= position[:, None]).astype(jnp.int32), axis=1)
    causal = position[None, :] <= position[:, None]
    return causal & (segment[:, None] == segment[None, :])


def pick_starts(start_table, micro_index):
    chosen = jnp.arange(start_table.shape[0], dtype=jnp.int32) == micro_index
    return jnp.sum(jnp.where(chosen[:, None], start_table, 0), axis=0)


def head_forward(query_head, key_head, value_head, allowed):
    score_scale = 1.0 / math.sqrt(query_head.shape[-1])
    scores = jnp.dot(query_head, key_head.T, preferred_element_type=jnp.float32) * score_scale
    scores = jnp.where(allowed, scores, -1e30)
    shifted = jnp.exp(scores - jnp.max(scores, axis=1, keepdims=True))
    attn_probs = shifted / jnp.sum(shifted, axis=1, keepdims=True)
    output = jnp.dot(
        attn_probs.astype(jnp.bfloat16), value_head, preferred_element_type=jnp.float32
    ).astype(jnp.bfloat16)
    return (output, attn_probs)


def split_heads(query, keyval):
    row_count = query.shape[0]
    heads_here = query.shape[1] // HD
    groups_here = keyval.shape[2] // HD
    group_size = heads_here // groups_here
    query_heads = query.reshape(row_count, heads_here, HD).transpose(1, 0, 2)
    key_heads = jnp.repeat(
        keyval[0].reshape(row_count, groups_here, HD).transpose(1, 0, 2), group_size, axis=0
    )
    value_heads = jnp.repeat(
        keyval[1].reshape(row_count, groups_here, HD).transpose(1, 0, 2), group_size, axis=0
    )
    return (query_heads, key_heads, value_heads)


def attend(query, keyval, allowed):
    head_parts = split_heads(query, keyval)
    outputs, attn_probs = jax.vmap(head_forward, in_axes=(0, 0, 0, None))(
        head_parts[0], head_parts[1], head_parts[2], allowed
    )
    merged = outputs.transpose(1, 0, 2).reshape(query.shape[0], query.shape[1])
    return (merged, attn_probs, head_parts)


def head_backward(query_head, key_head, value_head, attn_probs, grad_head):
    score_scale = 1.0 / math.sqrt(query_head.shape[-1])
    grad_probs = jnp.dot(grad_head, value_head.T, preferred_element_type=jnp.float32)
    center = jnp.sum(attn_probs * grad_probs, axis=1, keepdims=True)
    grad_scores = (attn_probs * (grad_probs - center) * score_scale).astype(jnp.bfloat16)
    grad_query = jnp.dot(grad_scores, key_head, preferred_element_type=jnp.float32).astype(
        jnp.bfloat16
    )
    grad_key = jnp.dot(grad_scores.T, query_head, preferred_element_type=jnp.float32)
    grad_value = jnp.dot(
        attn_probs.astype(jnp.bfloat16).T, grad_head, preferred_element_type=jnp.float32
    )
    return (grad_query, grad_key, grad_value)


def attend_back(head_parts, attn_probs, grad_attn, keyval):
    query_heads, key_heads, value_heads = head_parts
    heads_here, row_count, head_dim = query_heads.shape
    groups_here = keyval.shape[2] // head_dim
    grad_heads = grad_attn.reshape(row_count, heads_here, head_dim).transpose(1, 0, 2)
    grad_query, grad_key, grad_value = jax.vmap(head_backward)(
        query_heads, key_heads, value_heads, attn_probs, grad_heads
    )
    merged_query = grad_query.transpose(1, 0, 2).reshape(row_count, heads_here * head_dim)
    key_sum = grad_key.reshape(groups_here, heads_here // groups_here, row_count, head_dim).sum(
        axis=1
    )
    value_sum = grad_value.reshape(groups_here, heads_here // groups_here, row_count, head_dim).sum(
        axis=1
    )
    stacked = (
        jnp.stack([key_sum, value_sum])
        .transpose(0, 2, 1, 3)
        .reshape(2, row_count, groups_here * head_dim)
    )
    return (merged_query, stacked.astype(jnp.bfloat16))


def shards(
    fwd_resid,
    fwd_query,
    fwd_keyval,
    fwd_micro,
    bwd_query,
    bwd_keyval,
    grad_micro,
    grad_in,
    out_weight,
    doc_starts,
):
    resid_in, query_in, keyval_in, micro_in = from_behind(
        (fwd_resid[0], fwd_query[0], fwd_keyval[0], fwd_micro), "pipe", 1
    )
    weight = out_weight[0]
    row_count = query_in.shape[0]
    allowed = doc_allowed(pick_starts(doc_starts, micro_in[0]), row_count)
    attn_out, _, _ = attend(query_in, keyval_in, allowed)
    proj_sum = lax.psum_scatter(
        jnp.dot(attn_out, weight, preferred_element_type=jnp.float32).astype(jnp.bfloat16),
        "tp",
        scatter_dimension=0,
        tiled=True,
    ).astype(jnp.float32)
    phase_out = (resid_in.astype(jnp.float32) + proj_sum).astype(jnp.bfloat16)
    grad_share, micro_back = from_behind((grad_in[0], grad_micro), "pipe", -1)
    allowed_back = doc_allowed(pick_starts(doc_starts, micro_back[0]), row_count)
    back_attn, attn_probs, head_parts = attend(bwd_query[0], bwd_keyval[0], allowed_back)
    grad_block = lax.all_gather(grad_share, "tp", axis=0, tiled=True)
    weight_acc = jnp.dot(back_attn.T, grad_block, preferred_element_type=jnp.float32)
    block_grad = jnp.dot(grad_block, weight.T, preferred_element_type=jnp.float32)
    grad_attn = block_grad.astype(jnp.bfloat16)
    query_grad, keyval_grad = attend_back(head_parts, attn_probs, grad_attn, bwd_keyval[0])
    return (
        phase_out[None],
        query_grad[None],
        keyval_grad[None],
        weight_acc.astype(jnp.bfloat16)[None],
    )


def solution(mesh):
    return jax.shard_map(
        shards,
        mesh=mesh,
        in_specs=(
            P("pipe", "tp", None),
            P("pipe", None, "tp"),
            P("pipe", None, None, "tp"),
            P("pipe"),
            P("pipe", None, "tp"),
            P("pipe", None, None, "tp"),
            P("pipe"),
            P("pipe", "tp", None),
            P("pipe", "tp", None),
            P(),
        ),
        out_specs=(
            P("pipe", "tp", None),
            P("pipe", None, "tp"),
            P("pipe", None, None, "tp"),
            P("pipe", "tp", None),
        ),
        check_vma=False,
    )
```

profile of v0, /device:TPU:0, one launch (start us, length us, event | category | flops | bytes accessed | tf_op | source)
XLA Modules:
  0.0 180.3 jit_solution(1836812762314953627)
XLA Ops:
  7.2 6.1 %collective-permute-start.5 = (bf16[128,4096]{1,0:T(8,128)(2,1)}, bf16[128,4096]{1,0:T(8,128)(2,1)S(1)}, u32[]{:S(2)}, u32[]{:S(2)}) collective-permute-start(bf16[128,4096]{1,0:T(8,128)(2,1)} %bitcast.114), channel_id=1, source_target_pairs={{0,28},{4,0},{8,4},{12,8},{16,12},{20,16},{24,20},{28,24},{1,29},{... | collective-permute-start | bytes 3145736 | tf_op jit(solution)/shard_map/ppermute | solution.py:14
  13.3 22.7 %collective-permute-done.5 = bf16[128,4096]{1,0:T(8,128)(2,1)S(1)} collective-permute-done((bf16[128,4096]{1,0:T(8,128)(2,1)}, bf16[128,4096]{1,0:T(8,128)(2,1)S(1)}, u32[]{:S(2)}, u32[]{:S(2)}) %collective-permute-start.5) | collective-permute-done | bytes 1048608 | tf_op jit(solution)/shard_map/ppermute | solution.py:14
  37.0 1.5 copy.70
  38.8 4.9 %collective-permute-start.4 = (s32[1]{0:T(128)}, s32[1]{0:T(128)}, u32[]{:S(2)}, u32[]{:S(2)}) collective-permute-start(s32[1]{0:T(128)} %param.16), channel_id=1, source_target_pairs={{0,28},{4,0},{8,4},{12,8},{16,12},{20,16},{24,20},{28,24},{1,29},{... | collective-permute-start | bytes 20 | tf_op jit(solution)/shard_map/ppermute | solution.py:14
  43.7 1.4 collective-permute-done.4
  45.9 22.0 %collective-permute-done.1 = s32[1]{0:T(128)} collective-permute-done((s32[1]{0:T(128)}, s32[1]{0:T(128)}, u32[]{:S(2)}, u32[]{:S(2)}) %collective-permute-start.1) | collective-permute-done | bytes 36 | tf_op jit(solution)/shard_map/ppermute | solution.py:14
  69.5 7.7 %collective-permute-done.3 = bf16[2,512,256]{2,1,0:T(8,128)(2,1)S(1)} collective-permute-done((bf16[2,512,256]{2,1,0:T(8,128)(2,1)}, bf16[2,512,256]{2,1,0:T(8,128)(2,1)S(1)}, u32[]{:S(2)}, u32[]{:S(2)}) %collective-permute-start.3) | collective-permute-done | bytes 524320 | tf_op jit(solution)/shard_map/ppermute | solution.py:14
  78.5 1.3 fusion.50
  79.7 5.6 %fusion.74 = (f32[8,512]{1,0:T(8,128)S(1)}, f32[8,512,512]{1,2,0:T(8,128)}) fusion(f32[8,512,512]{1,2,0:T(8,128)S(1)} %fusion.50, pred[512,512]{0,1:T(8,128)(4,1)S(1)} %fusion.53), kind=kOutput, calls=%fused_computation.77 | output fusion | flops 12583423 | bytes 17055744 | tf_op jit(solution)/shard_map/vmap()/sub | solution.py:33
  85.5 4.3 %fusion.41 = bf16[8,512,128]{1,2,0:T(8,128)(2,1)S(1)} fusion(bf16[8,512,128]{1,2,0:T(8,128)(2,1)S(1)} %bitcast.101, f32[8,512,512]{1,2,0:T(8,128)} %get-tuple-element.31, f32[8,512]{1,0:T(8,128)S(1)} %get-tuple-element.30), kind=kOutput, calls=%fused_computation.39 | convolution fusion | flops 541589504 | bytes 10502144 | tf_op jit(solution)/shard_map/vmap()/dot_general | solution.py:35
  89.9 1.3 slice-done.1
  91.2 6.2 %fusion.10 = bf16[512,4096]{1,0:T(8,128)(2,1)} fusion(bf16[512,1024]{0,1:T(8,128)(2,1)S(1)} %bitcast.117, bf16[1,1024,4096]{2,1,0:T(8,128)(2,1)S(1)} %bitcast.113), kind=kOutput, calls=%fused_computation.18 | convolution fusion | flops 4297064448 | bytes 13631488 | tf_op jit(solution)/shard_map/dot_general | solution.py:123
  98.7 1.3 fusion.48
  100.3 5.7 %fusion.75 = (f32[8,512]{1,0:T(8,128)S(1)}, f32[8,512,512]{1,2,0:T(8,128)}) fusion(f32[8,512,512]{1,2,0:T(8,128)S(1)} %fusion.48, pred[512,512]{0,1:T(8,128)(4,1)S(1)} %fusion.52), kind=kOutput, calls=%fused_computation.78 | output fusion | flops 12583423 | bytes 17055744 | tf_op jit(solution)/shard_map/vmap()/sub | solution.py:33
  106.1 5.4 %fusion.32 = bf16[8,512,128]{1,2,0:T(8,128)(2,1)} fusion(bf16[8,512,128]{1,2,0:T(8,128)(2,1)S(1)} %bitcast.95, f32[8,512,512]{1,2,0:T(8,128)} %get-tuple-element.33, f32[8,512]{1,0:T(8,128)S(1)} %get-tuple-element.32), kind=kOutput, calls=%fused_computation.36 | convolution fusion | flops 541589504 | bytes 10502144 | tf_op jit(solution)/shard_map/vmap()/dot_general | solution.py:35
  111.5 9.9 %fusion.42 = bf16[64,8,8,128]{3,2,1,0:T(8,128)(2,1)S(1)} fusion(bf16[512,4096]{1,0:T(8,128)(2,1)} %all-gather.2.cloned.1.call-done, bf16[1,1024,4096]{2,1,0:T(8,128)(2,1)} %param.18), kind=kOutput, calls=%fused_computation.40 | convolution fusion | flops 4295491584 | bytes 13631488 | tf_op jit(solution)/shard_map/dot_general | solution.py:134
  122.3 4.7 %fusion.46 = f32[8,512,512]{1,2,0:T(8,128)} fusion(bf16[8,512,128]{1,2,0:T(8,128)(2,1)S(1)} %bitcast.96, bf16[64,8,8,128]{3,2,1,0:T(8,128)(2,1)S(1)} %fusion.42), kind=kOutput, calls=%fused_computation.43 | convolution fusion | flops 536870912 | bytes 10485760 | tf_op jit(solution)/shard_map/vmap()/dot_general | solution.py:67
  127.0 12.9 %bitcast_reduce_fusion.1 = bf16[2,512,128]{2,1,0:T(8,128)(2,1)S(1)} fusion(bf16[512,8,128]{2,1,0:T(8,128)(2,1)S(1)} %bitcast.99, f32[8,512,512]{1,2,0:T(8,128)} %fusion.46, f32[8,512,512]{1,2,0:T(8,128)} %get-tuple-element.33, f32[8,512]{1,0:T(8,128)S(1)} %get-tuple-element.32), kind=kOutput, calls=%fused_computation.30 | convolution fusion | flops 551948800 | bytes 18104320 | tf_op jit(solution)/shard_map/vmap()/dot_general | solution.py:73
  139.9 4.8 %bitcast_reduce_fusion = bf16[2,512,128]{2,1,0:T(8,128)(2,1)S(1)} fusion(bf16[64,8,8,128]{3,2,1,0:T(8,128)(2,1)S(1)} %copy-done.1, f32[8,512,512]{1,2,0:T(8,128)} %get-tuple-element.33, f32[8,512]{1,0:T(8,128)S(1)} %get-tuple-element.32), kind=kOutput, calls=%fused_computation.29 | convolution fusion | flops 541458432 | bytes 9715712 | tf_op jit(solution)/shard_map/vmap()/dot_general | solution.py:74
  145.0 1.0 copy.85
  146.0 14.3 %fusion.38 = bf16[8,512,128]{1,2,0:T(8,128)(2,1)S(1)} fusion(bf16[8,512,128]{1,2,0:T(8,128)(2,1)S(1)} %bitcast.94, f32[8,512,512]{1,2,0:T(8,128)} %fusion.46, f32[8,512,512]{1,2,0:T(8,128)} %get-tuple-element.33, f32[8,512]{1,0:T(8,128)S(1)} %get-tuple-element.32), kind=kOutput, calls=%fused_computation.38 | convolution fusion | flops 552079872 | bytes 18890752 | tf_op jit(solution)/shard_map/vmap()/dot_general | solution.py:70
  160.3 1.3 copy.84
  161.6 9.0 %convert_bitcast_fusion = bf16[1,1024,4096]{2,1,0:T(8,128)(2,1)} fusion(bf16[512,1024]{0,1:T(8,128)(2,1)S(1)} %bitcast.116, bf16[512,4096]{1,0:T(8,128)(2,1)} %all-gather.2.cloned.1.call-done), kind=kOutput, calls=%fused_computation.7 | convolution fusion | flops 4299161600 | bytes 13631488 | tf_op jit(solution)/shard_map/dot_general | solution.py:133
  170.7 2.8 %fusion.45 = bf16[1,128,4096]{2,1,0:T(8,128)(2,1)} fusion(bf16[128,4096]{1,0:T(8,128)(2,1)} %reduce-scatter.2.cloned.1.call-done, bf16[128,4096]{1,0:T(8,128)(2,1)} %collective-permute-done), kind=kLoop, calls=%fused_computation.41 | loop fusion | flops 2097152 | bytes 3145728 | tf_op jit(solution)/shard_map/broadcast_in_dim | solution.py:138
  (53 shorter events, 7.8 us)
Async XLA Ops:
  7.2 104.3 %all-gather.2.cloned.1.call-start = ((), (), s32[]{:S(2)}) async-start(), calls=%async_computation.2 | async-start | bytes 5242880 | tf_op jit(solution)/shard_map/all_gather | solution.py:132
  7.2 28.8 %collective-permute-start.5 = (bf16[128,4096]{1,0:T(8,128)(2,1)}, bf16[128,4096]{1,0:T(8,128)(2,1)S(1)}, u32[]{:S(2)}, u32[]{:S(2)}) collective-permute-start(bf16[128,4096]{1,0:T(8,128)(2,1)} %bitcast.114), channel_id=1, source_target_pairs={{0,28},{4,0},{8,4},{12,8},{16,12},{20,16},{24,20},{28,24},{1,29},{... | collective-permute-start | bytes 3145736 | tf_op jit(solution)/shard_map/ppermute | solution.py:14
  36.0 1.0 copy-start.3
  37.0 133.7 %reduce-scatter.2.cloned.1.call-start = ((), (), s32[]{:S(2)}) async-start(), calls=%async_computation.1 | async-start | bytes 5242880 | tf_op jit(solution)/shard_map/reduce_scatter | solution.py:122
  38.6 39.1 %collective-permute-start.2 = (bf16[512,1024]{0,1:T(8,128)(2,1)S(1)}, bf16[512,1024]{0,1:T(8,128)(2,1)S(1)}, u32[]{:S(2)}, u32[]{:S(2)}) collective-permute-start(bf16[512,1024]{0,1:T(8,128)(2,1)S(1)} %bitcast.104), channel_id=1, source_target_pairs={{0,4},{4,8},{8,12},{12,16},{16,20},{20,24},{24,28},{28,0},{1,5},{5... | collective-permute-start | bytes 3145736 | tf_op jit(solution)/shard_map/ppermute | solution.py:14
  38.8 6.3 %collective-permute-start.4 = (s32[1]{0:T(128)}, s32[1]{0:T(128)}, u32[]{:S(2)}, u32[]{:S(2)}) collective-permute-start(s32[1]{0:T(128)} %param.16), channel_id=1, source_target_pairs={{0,28},{4,0},{8,4},{12,8},{16,12},{20,16},{24,20},{28,24},{1,29},{... | collective-permute-start | bytes 20 | tf_op jit(solution)/shard_map/ppermute | solution.py:14
  43.7 24.1 %collective-permute-start.1 = (s32[1]{0:T(128)}, s32[1]{0:T(128)}, u32[]{:S(2)}, u32[]{:S(2)}) collective-permute-start(s32[1]{0:T(128)} %param.13), channel_id=1, source_target_pairs={{0,4},{4,8},{8,12},{12,16},{16,20},{20,24},{24,28},{28,0},{1,5},{5... | collective-permute-start | bytes 20 | tf_op jit(solution)/shard_map/ppermute | solution.py:14
  43.7 33.5 %collective-permute-start.3 = (bf16[2,512,256]{2,1,0:T(8,128)(2,1)}, bf16[2,512,256]{2,1,0:T(8,128)(2,1)S(1)}, u32[]{:S(2)}, u32[]{:S(2)}) collective-permute-start(bf16[2,512,256]{2,1,0:T(8,128)(2,1)} %bitcast.115), channel_id=1, source_target_pairs={{0,4},{4,8},{8,12},{12,16},{16,20},{20,24},{24,28},{28,0},{1,5},{5... | collective-permute-start | bytes 1572872 | tf_op jit(solution)/shard_map/ppermute | solution.py:14
  85.4 4.6 %slice-start = ((s8[8388608]{0:T(1024)(128)(4,1)}), s8[4194304]{0:T(1024)(128)(4,1)S(1)}, s32[]{:S(2)}) async-start(s8[8388608]{0:T(1024)(128)(4,1)} %bitcast.112), calls=%async_computation.3 | async-start | bytes 8388608
  85.5 5.8 %slice-start.1 = ((s8[8388608]{0:T(1024)(128)(4,1)}), s8[4194304]{0:T(1024)(128)(4,1)S(1)}, s32[]{:S(2)}) async-start(s8[8388608]{0:T(1024)(128)(4,1)} %bitcast.112), calls=%async_computation.4 | async-start | bytes 8388608
  91.2 6.5 %copy-start.4 = (bf16[1,2,512,256]{3,2,1,0:T(8,128)(2,1)S(1)}, bf16[1,2,512,256]{3,2,1,0:T(8,128)(2,1)}, u32[]{:S(2)}) copy-start(bf16[1,2,512,256]{3,2,1,0:T(8,128)(2,1)} %param.15) | copy-start | bytes 1572868
  91.2 6.8 %copy-start.2 = (bf16[1,512,1024]{2,1,0:T(8,128)(2,1)S(1)}, bf16[1,512,1024]{2,1,0:T(8,128)(2,1)}, u32[]{:S(2)}) copy-start(bf16[1,512,1024]{2,1,0:T(8,128)(2,1)} %param.14) | copy-start | bytes 3145732
  97.5 73.1 %collective-permute-start = (bf16[128,4096]{1,0:T(8,128)(2,1)}, bf16[128,4096]{1,0:T(8,128)(2,1)}, u32[]{:S(2)}, u32[]{:S(2)}) collective-permute-start(bf16[128,4096]{1,0:T(8,128)(2,1)} %bitcast), channel_id=1, source_target_pairs={{0,4},{4,8},{8,12},{12,16},{16,20},{20,24},{24,28},{28,0},{1,5},{5... | collective-permute-start | bytes 3145736 | tf_op jit(solution)/shard_map/ppermute | solution.py:14
  121.4 1.0 copy-start
  127.0 12.9 %copy-start.1 = (bf16[64,8,8,128]{3,2,1,0:T(8,128)(2,1)S(1)}, bf16[64,8,8,128]{3,2,1,0:T(8,128)(2,1)}, u32[]{:S(2)}) copy-start(bf16[64,8,8,128]{3,2,1,0:T(8,128)(2,1)} %copy-done) | copy-start | bytes 3145732
  146.0 15.7 %copy-start.5 = (bf16[8,512,128]{1,2,0:T(8,128)(2,1)S(1)}, bf16[8,512,128]{1,2,0:T(8,128)(2,1)}, u32[]{:S(2)}) copy-start(bf16[8,512,128]{1,2,0:T(8,128)(2,1)} %fusion.32) | copy-start | bytes 3145732
Sparse Core Ops, SparseCore 0:
  37.1 36.2 all-gather.1
  97.6 42.9 reduce-scatter.1
where the time goes:
time: 181 us; the launch traced here: 180 us
  matrix products  74.1 us (41%)
  waiting for transfers between devices  53.9 us (30%)
  other arithmetic  16.8 us (9%)
  between operations  14.3 us (8%)
  starting transfers between devices  11.6 us (6%)
  local copies, waits for them, and re-layouts  9.62 us (5%)
    ppermute x6, waiting for transfers between devices, from_behind(): return lax.ppermute(value, axis, pairs)  53.8 us
    dot_general x1, matrix products, head_backward(): jnp.dot(grad_scores, key_head, preferred_element_type=jnp.float32)  14.3 us
    dot_general x1, matrix products, head_backward(): jnp.dot(grad_scores.T, query_head, preferred_element_type=jnp.float32)  12.9 us
    ppermute x6, starting transfers between devices, from_behind(): return lax.ppermute(value, axis, pairs)  11.5 us
    sub x2, other arithmetic, head_forward(): shifted = jnp.exp(scores - jnp.max(scores, axis=1, keepdims=True))  11.3 us
    dot_general x1, matrix products, shards(): jnp.dot(grad_block, weight.T, preferred_element_type=jnp.float32)  9.88 us
    dot_general x2, matrix products, head_forward(): jnp.dot(attn_probs.astype(jnp.bfloat16), value_head, preferred_element_ty...  9.73 us
    dot_general x1, matrix products, shards(): jnp.dot(back_attn.T, grad_block, preferred_element_type=jnp.float32)  9.02 us
  transfers between devices with their start and end apart: 8, of which 4 were waited for; matrix products, arithmetic and copies ran while one was open for 52% of the time, Pallas kernels for 0%

commit v1 on v0

v1 whole, which is shorter than its diff:
```python
import functools
import math

import jax
import jax.numpy as jnp
from jax import lax
from jax.experimental import pallas as pl
from jax.experimental.pallas import tpu as pltpu
from jax.sharding import PartitionSpec as P

HD = 128
BLOCK = 128
F32 = jnp.float32
BF16 = jnp.bfloat16
SMEM = pl.BlockSpec(memory_space=pltpu.SMEM)
NT = (((1,), (1,)), ((), ()))
NN = (((1,), (0,)), ((), ()))
TN = (((0,), (0,)), ((), ()))


def dot(a, b, dims):
    return lax.dot_general(a, b, dims, preferred_element_type=F32)


def params(mib=48):
    return pltpu.CompilerParams(vmem_limit_bytes=mib * 1024 * 1024)


def cost(flops, moved, transcendentals=0):
    return pl.CostEstimate(
        flops=int(flops), bytes_accessed=int(moved), transcendentals=int(transcendentals)
    )


def after(value, *earlier):
    return lax.optimization_barrier((value, *earlier))[0]


def along_pipe(value, steps):
    count = lax.axis_size("pipe")
    return lax.ppermute(value, "pipe", [(i, (i + steps) % count) for i in range(count)])


def other_core(value):
    count = lax.axis_size("tp")
    return lax.ppermute(value, "tp", [(i, i ^ 1) for i in range(count)])


def along_chips(value, steps):
    count = lax.axis_size("tp")
    return lax.ppermute(value, "tp", [(i, (i + 2 * steps) % count) for i in range(count)])


def stack_heads(ref, first, heads):
    return jnp.concatenate(
        [ref[first : first + BLOCK, h * HD : (h + 1) * HD] for h in range(heads)], axis=0
    )


def block_probs(starts_ref, micro_ref, query, key, first, heads):
    extent = first + BLOCK
    micro = micro_ref[0]
    row = lax.broadcasted_iota(jnp.int32, (BLOCK, 1), 0) + first
    low = jnp.zeros((BLOCK, 1), jnp.int32)
    for doc in range(starts_ref.shape[1]):
        start = starts_ref[micro, doc]
        low = jnp.where(row >= start, start, low)
    column = lax.broadcasted_iota(jnp.int32, (BLOCK, extent), 1)
    allowed = (column >= low) & (column <= row)
    scores = dot(query, key, NT) * (1.0 / math.sqrt(HD))
    scores = scores.reshape(heads, BLOCK, extent)
    scores = jnp.where(allowed[None], scores, -1e30)
    shifted = jnp.exp(scores - jnp.max(scores, axis=2, keepdims=True))
    probs = shifted * (1.0 / jnp.sum(shifted, axis=2, keepdims=True))
    return probs.astype(BF16).reshape(heads * BLOCK, extent)


def forward_kernel(starts_ref, micro_ref, query_ref, keyval_ref, *out_refs):
    rows, width = query_ref.shape
    heads = width // HD
    parts = len(out_refs)
    owners, part_rows, _ = out_refs[0].shape
    for first in range(0, rows, BLOCK):
        extent = first + BLOCK
        query = stack_heads(query_ref, first, heads)
        probs = block_probs(starts_ref, micro_ref, query, keyval_ref[0, :extent], first, heads)
        out = dot(probs, keyval_ref[1, :extent], NN).astype(BF16)
        for h in range(heads):
            for low in range(0, BLOCK, part_rows):
                piece = (first + low) // part_rows
                out_refs[piece % parts][piece // parts, :, h * HD : (h + 1) * HD] = out[
                    h * BLOCK + low : h * BLOCK + low + part_rows
                ]


def forward_attention(starts, micro, query, keyval, owners, parts):
    rows, width = query.shape
    groups = keyval.shape[2] // HD
    span = width // groups
    part_rows = rows // owners // parts
    return pl.pallas_call(
        forward_kernel,
        grid=(groups,),
        in_specs=[
            SMEM,
            SMEM,
            pl.BlockSpec((rows, span), lambda g: (0, g)),
            pl.BlockSpec((2, rows, HD), lambda g: (0, 0, g)),
        ],
        out_specs=[pl.BlockSpec((owners, part_rows, span), lambda g: (0, 0, g))] * parts,
        out_shape=[jax.ShapeDtypeStruct((owners, part_rows, width), BF16)] * parts,
        compiler_params=params(),
        cost_estimate=cost(4 * rows * rows * width, 8 * rows * width),
        name="forward_attention",
    )(starts, micro, query, keyval)


def stored_kernel(starts_ref, micro_ref, query_ref, keyval_ref, out_ref, probs_ref):
    rows, width = query_ref.shape
    heads = width // HD
    for index, first in enumerate(range(0, rows, BLOCK)):
        extent = first + BLOCK
        query = stack_heads(query_ref, first, heads)
        probs = block_probs(starts_ref, micro_ref, query, keyval_ref[0, :extent], first, heads)
        probs_ref[0, index, :, :extent] = probs
        out = dot(probs, keyval_ref[1, :extent], NN)
        for h in range(heads):
            out_ref[h * HD : (h + 1) * HD, first:extent] = out[
                h * BLOCK : (h + 1) * BLOCK
            ].T.astype(BF16)


def stored_attention(starts, micro, query, keyval):
    rows, width = query.shape
    groups = keyval.shape[2] // HD
    span = width // groups
    blocks = rows // BLOCK
    stacked = span // HD * BLOCK
    return pl.pallas_call(
        stored_kernel,
        grid=(groups,),
        in_specs=[
            SMEM,
            SMEM,
            pl.BlockSpec((rows, span), lambda g: (0, g)),
            pl.BlockSpec((2, rows, HD), lambda g: (0, 0, g)),
        ],
        out_specs=[
            pl.BlockSpec((span, rows), lambda g: (g, 0)),
            pl.BlockSpec((1, blocks, stacked, rows), lambda g: (g, 0, 0, 0)),
        ],
        out_shape=[
            jax.ShapeDtypeStruct((width, rows), BF16),
            jax.ShapeDtypeStruct((groups, blocks, stacked, rows), BF16),
        ],
        compiler_params=params(),
        cost_estimate=cost(4 * rows * rows * width, 8 * rows * width),
        name="stored_attention",
    )(starts, micro, query, keyval)


def backward_kernel(query_ref, keyval_ref, grad_ref, probs_ref, dquery_ref, dkeyval_ref, dk, dv):
    rows, width = query_ref.shape
    heads = width // HD
    dk[...] = jnp.zeros_like(dk)
    dv[...] = jnp.zeros_like(dv)
    for index, first in enumerate(range(0, rows, BLOCK)):
        extent = first + BLOCK
        query = stack_heads(query_ref, first, heads)
        grad = stack_heads(grad_ref, first, heads)
        probs = probs_ref[0, index, :, :extent]
        wide = probs.astype(F32)
        dprobs = dot(grad, keyval_ref[1, :extent], NT)
        center = jnp.sum(wide * dprobs, axis=1, keepdims=True)
        dscores = (wide * (dprobs - center) * (1.0 / math.sqrt(HD))).astype(BF16)
        dquery = dot(dscores, keyval_ref[0, :extent], NN).astype(BF16)
        for h in range(heads):
            dquery_ref[first:extent, h * HD : (h + 1) * HD] = dquery[h * BLOCK : (h + 1) * BLOCK]
        dk[:extent] += dot(dscores, query, TN)
        dv[:extent] += dot(probs, grad, TN)
    dkeyval_ref[0] = dk[...].astype(BF16)
    dkeyval_ref[1] = dv[...].astype(BF16)


def backward_attention(query, keyval, grad, probs):
    rows, width = query.shape
    groups = keyval.shape[2] // HD
    span = width // groups
    wide = pl.BlockSpec((rows, span), lambda g: (0, g))
    narrow = pl.BlockSpec((2, rows, HD), lambda g: (0, 0, g))
    return pl.pallas_call(
        backward_kernel,
        grid=(groups,),
        in_specs=[
            wide,
            narrow,
            wide,
            pl.BlockSpec((1,) + probs.shape[1:], lambda g: (g, 0, 0, 0)),
        ],
        out_specs=[wide, narrow],
        out_shape=[
            jax.ShapeDtypeStruct(query.shape, BF16),
            jax.ShapeDtypeStruct(keyval.shape, BF16),
        ],
        scratch_shapes=[pltpu.VMEM((rows, HD), F32)] * 2,
        compiler_params=params(),
        cost_estimate=cost(8 * rows * rows * width, 16 * rows * width),
        name="backward_attention",
    )(query, keyval, grad, probs)


def grad_kernel(count, last, sources_ref, *refs):
    pieces = refs[:count]
    weight_ref, attn_ref = refs[count : count + 2]
    rest = refs[count + 2 :]
    total_ref = None
    if last:
        total_ref, _, dattn_ref, dweight_ref, whole, total = rest
    else:
        dattn_ref, dweight_ref, whole, total = rest
    step = pl.program_id(0)
    piece_rows = pieces[0].shape[0]
    for j in range(count):
        row = pl.multiple_of(sources_ref[j] * piece_rows, piece_rows)
        whole[pl.ds(row, piece_rows), :] = pieces[j][...]

    @pl.when(step == 0)
    def _():
        if last:
            total[...] = total_ref[...]
        else:
            total[...] = jnp.zeros_like(total)

    total[...] += dot(whole[...], weight_ref[...], NT)
    dweight_ref[...] = dot(attn_ref[...], whole[...], NN).astype(BF16)

    @pl.when(step == pl.num_programs(0) - 1)
    def _():
        dattn_ref[...] = total[...].astype(dattn_ref.dtype)


def grad_products(sources, pieces, weight, attn, part, earlier, last):
    piece_rows, columns = pieces[0].shape
    rows = attn.shape[1]
    heads_width, full = weight.shape
    block = min(512, columns)
    steps = columns // block
    offset = part * steps
    in_specs = [SMEM]
    in_specs += [pl.BlockSpec((piece_rows, block), lambda i: (0, i))] * len(pieces)
    in_specs += [
        pl.BlockSpec((heads_width, block), lambda i: (0, offset + i)),
        pl.BlockSpec((heads_width, rows), lambda i: (0, 0)),
    ]
    args = [sources, *pieces, weight, attn]
    aliases = {}
    if earlier is not None:
        in_specs += [
            pl.BlockSpec((rows, heads_width), lambda i: (0, 0)),
            pl.BlockSpec(memory_space=pl.ANY),
        ]
        args += list(earlier)
        aliases = {len(args) - 1: 1}
    return pl.pallas_call(
        functools.partial(grad_kernel, len(pieces), last),
        grid=(steps,),
        in_specs=in_specs,
        out_specs=[
            pl.BlockSpec((rows, heads_width), lambda i: (0, 0)),
            pl.BlockSpec((heads_width, block), lambda i: (0, offset + i)),
        ],
        out_shape=[
            jax.ShapeDtypeStruct((rows, heads_width), BF16 if last else F32),
            jax.ShapeDtypeStruct((heads_width, full), BF16),
        ],
        scratch_shapes=[
            pltpu.VMEM((rows, block), BF16),
            pltpu.VMEM((rows, heads_width), F32),
        ],
        input_output_aliases=aliases,
        compiler_params=params(),
        cost_estimate=cost(4 * rows * heads_width * columns, 4 * heads_width * columns),
        name="grad_products",
    )(*args)


def project_kernel(place_ref, attn_ref, weight_ref, send_ref, keep_ref, gathered):
    half, part_rows, block = send_ref.shape
    core = place_ref[0] % 2
    for j in range(half):
        gathered[j] = attn_ref[2 * j + 1 - core]
        gathered[half + j] = attn_ref[2 * j + core]
    stacked = gathered[...].reshape(2 * half * part_rows, attn_ref.shape[2])
    out = dot(stacked, weight_ref[...], NN).astype(BF16).reshape(2 * half, part_rows, block)
    send_ref[...] = out[:half]
    keep_ref[...] = out[half:]


def project(place, attn, weight):
    owners, part_rows, width = attn.shape
    columns = weight.shape[1]
    block = min(1024, columns)
    spec = pl.BlockSpec((owners // 2, part_rows, block), lambda i: (0, 0, i))
    shape = jax.ShapeDtypeStruct((owners // 2, part_rows, columns), BF16)
    return pl.pallas_call(
        project_kernel,
        grid=(columns // block,),
        in_specs=[
            SMEM,
            pl.BlockSpec((owners, part_rows, width), lambda i: (0, 0, 0)),
            pl.BlockSpec((width, block), lambda i: (0, i)),
        ],
        out_specs=[spec, spec],
        out_shape=[shape, shape],
        scratch_shapes=[pltpu.VMEM((owners, part_rows, width), BF16)],
        compiler_params=params(),
        cost_estimate=cost(2 * owners * part_rows * width * columns, 2 * width * columns),
        name="project",
    )(place, attn, weight)


def pair_sum_kernel(place_ref, keep_ref, got_ref, *out_refs):
    chips = keep_ref.shape[0]
    chip = place_ref[0] // 2
    for j, out_ref in enumerate(out_refs):
        index = (chip + j + 1) % chips
        out_ref[...] = (keep_ref[index].astype(F32) + got_ref[index].astype(F32)).astype(BF16)


def pair_sum(place, keep, got):
    chips, part_rows, columns = keep.shape
    block = min(2048, columns)
    spec = pl.BlockSpec((chips, part_rows, block), lambda i: (0, 0, i))
    return pl.pallas_call(
        pair_sum_kernel,
        grid=(columns // block,),
        in_specs=[SMEM, spec, spec],
        out_specs=[pl.BlockSpec((part_rows, block), lambda i: (0, i))] * (chips - 1),
        out_shape=[jax.ShapeDtypeStruct((part_rows, columns), BF16)] * (chips - 1),
        compiler_params=params(),
        cost_estimate=cost(chips * part_rows * columns, 6 * chips * part_rows * columns),
        name="pair_sum",
    )(place, keep, got)


def finish_kernel(parts, place_ref, resid_ref, *refs):
    out_ref = refs[-1]
    each = (len(refs) - 1) // parts
    part_rows = resid_ref.shape[0] // parts
    chip = place_ref[0] // 2
    for part in range(parts):
        keep_ref, got_ref, *far_refs = refs[part * each : (part + 1) * each]
        rows = slice(part * part_rows, (part + 1) * part_rows)
        total = keep_ref[chip].astype(F32) + got_ref[chip].astype(F32)
        for far_ref in far_refs:
            total += far_ref[...].astype(F32)
        out_ref[rows] = (resid_ref[rows].astype(F32) + total).astype(BF16)


def finish(place, resid, sums):
    rows, columns = resid.shape
    block = min(1024, columns)
    flat = [array for part in sums for array in part]
    specs = []
    for array in flat:
        if array.ndim == 3:
            specs.append(pl.BlockSpec(array.shape[:2] + (block,), lambda i: (0, 0, i)))
        else:
            specs.append(pl.BlockSpec(array.shape[:1] + (block,), lambda i: (0, i)))
    wide = pl.BlockSpec((rows, block), lambda i: (0, i))
    return pl.pallas_call(
        functools.partial(finish_kernel, len(sums)),
        grid=(columns // block,),
        in_specs=[SMEM, wide] + specs,
        out_specs=wide,
        out_shape=jax.ShapeDtypeStruct(resid.shape, BF16),
        compiler_params=params(),
        cost_estimate=cost(4 * rows * columns, 12 * rows * columns),
        name="finish",
    )(place, resid, *flat)


PARTS = 2


def shards(
    fwd_resid,
    fwd_query,
    fwd_keyval,
    fwd_micro,
    bwd_query,
    bwd_keyval,
    grad_micro,
    grad_in,
    out_weight,
    doc_starts,
):
    devices = lax.axis_size("tp")
    chips = devices // 2
    me = lax.axis_index("tp")
    place = me.astype(jnp.int32)[None]
    weight = out_weight[0]
    columns = weight.shape[1] // PARTS

    micro_back = along_pipe(grad_micro, -1)
    grads = [
        along_pipe(grad_in[0][:, part * columns : (part + 1) * columns], -1)
        for part in range(PARTS)
    ]

    attn = forward_attention(
        doc_starts, fwd_micro, fwd_query[0], fwd_keyval[0], devices, PARTS
    )
    attn_in = [along_pipe(after(attn[0], grads[0]), 1), along_pipe(after(attn[1], grads[0]), 1)]
    resid_in = along_pipe(after(fwd_resid[0], grads[1]), 1)

    back_attn, probs = stored_attention(doc_starts, micro_back, bwd_query[0], bwd_keyval[0])

    sources = [me, me ^ 1]
    for step in range(1, chips):
        sources += [(me - 2 * step) % devices, ((me ^ 1) - 2 * step) % devices]
    sources = jnp.stack(sources).astype(jnp.int32)

    pieces = []
    for part in range(PARTS):
        held = [grads[part], other_core(grads[part])]
        for step in range(1, chips):
            far = along_chips(grads[part], step)
            held += [far, other_core(far)]
        pieces.append(held)

    earlier = None
    for part in range(PARTS):
        earlier = grad_products(
            sources, pieces[part], weight, back_attn, part, earlier, part == PARTS - 1
        )
    grad_attn, grad_weight = earlier

    sums = []
    for part in range(PARTS):
        send, keep = project(place, attn_in[part], weight)
        got = other_core(send)
        near = pair_sum(place, keep, got)
        far = [along_chips(near[step - 1], step) for step in range(1, chips)]
        sums.append((keep, got, *far))

    query_grad, keyval_grad = backward_attention(bwd_query[0], bwd_keyval[0], grad_attn, probs)
    phase_out = finish(place, resid_in, sums)
    return (phase_out[None], query_grad[None], keyval_grad[None], grad_weight[None])


def solution(mesh):
    return jax.shard_map(
        shards,
        mesh=mesh,
        in_specs=(
            P("pipe", "tp", None),
            P("pipe", None, "tp"),
            P("pipe", None, None, "tp"),
            P("pipe"),
            P("pipe", None, "tp"),
            P("pipe", None, None, "tp"),
            P("pipe"),
            P("pipe", "tp", None),
            P("pipe", "tp", None),
            P(),
        ),
        out_specs=(
            P("pipe", "tp", None),
            P("pipe", None, "tp"),
            P("pipe", None, None, "tp"),
            P("pipe", "tp", None),
        ),
        check_vma=False,
    )
```

time: 181 us -> 121 us (0.67)
  matrix products: 74.1 us -> 0 us
  Pallas kernels: 0 us -> 55.5 us
  waiting for transfers between devices: 53.9 us -> 35.4 us
  other arithmetic: 16.8 us -> 0.08 us
  between operations: 14.3 us -> 1.38 us
  starting transfers between devices: 11.6 us -> 18.5 us
    dot_general x11 -> x0, matrix products: 74.1 us -> none  [the longest x1 14.3 us: head_backward(): jnp.dot(grad_scores, key_head, preferred_element_type=jnp.float32)]
    pallas_call x0 -> x10, Pallas kernels: none -> 55.5 us  [the longest x2 17.9 us: grad_products(): pl.pallas_call(functools.partial(grad_kernel, len(pieces), last), grid=(s...]
    ppermute x6 -> x16, waiting for transfers between devices: 53.8 us -> 35.4 us  [the longest x6 26.7 us: along_pipe(): lax.ppermute(value, 'pipe', [(i, (i + steps) % count) for i in range(coun...]
    sub x2 -> x0, other arithmetic: 11.3 us -> none  [head_forward(): shifted = jnp.exp(scores - jnp.max(scores, axis=1, keepdims=True))]
    ppermute x6 -> x16, starting transfers between devices: 11.5 us -> 18.5 us  [the longest x6 11.9 us: along_pipe(): lax.ppermute(value, 'pipe', [(i, (i + steps) % count) for i in range(coun...]
    broadcast_in_dim x1 -> x0, other arithmetic: 2.76 us -> none  [shards(): phase_out[None]]
    unnamed x20 -> x24, local copies, waits for them, and re-layouts: 7.45 us -> 8.43 us
  transfers between devices with their start and end apart: 8 -> 16, of which waited for: 4 -> 4; matrix products, arithmetic and copies ran while one was open for 52% -> 0% of each run, Pallas kernels for 0% -> 43%
where the time goes in v1:
time: 121 us; the launch traced here: 120 us
  Pallas kernels  55.5 us (46%)
  waiting for transfers between devices  35.4 us (29%)
  starting transfers between devices  18.5 us (15%)
  local copies, waits for them, and re-layouts  9.73 us (8%)
  between operations  1.38 us (1%)
    ppermute x6, waiting for transfers between devices, along_pipe(): lax.ppermute(value, 'pipe', [(i, (i + steps) % count) for i in range(coun...  26.7 us
    pallas_call x2, Pallas kernels, grad_products(): pl.pallas_call(functools.partial(grad_kernel, len(pieces), last), grid=(s...  17.9 us
    pallas_call x2, Pallas kernels, project(): pl.pallas_call(project_kernel, grid=(columns // block,), in_specs=[SMEM,...  12.5 us
    ppermute x6, starting transfers between devices, along_pipe(): lax.ppermute(value, 'pipe', [(i, (i + steps) % count) for i in range(coun...  11.9 us
    unnamed x24, local copies, waits for them, and re-layouts  8.43 us
    pallas_call x1, Pallas kernels, backward_attention(): pl.pallas_call(backward_kernel, grid=(groups,), in_specs=[wide, narrow, w...  7.34 us
    pallas_call x1, Pallas kernels, stored_attention(): pl.pallas_call(stored_kernel, grid=(groups,), in_specs=[SMEM, SMEM, pl.Bl...  7.02 us
    ppermute x4, starting transfers between devices, along_chips(): lax.ppermute(value, 'tp', [(i, (i + 2 * steps) % count) for i in range(co...  5.36 us
  transfers between devices with their start and end apart: 16, of which 4 were waited for; matrix products, arithmetic and copies ran while one was open for 0% of the time, Pallas kernels for 43%

profile of v1, /device:TPU:0, one launch (start us, length us, event | category | flops | bytes accessed | tf_op | source)
XLA Modules:
  0.0 120.5 jit_solution(9811938703630205320)
XLA Ops:
  0.6 1.3 %fusion = (bf16[128,2048]{1,0:T(8,128)(2,1)S(1)}, bf16[128,2048]{1,0:T(8,128)(2,1)S(1)}) fusion(bf16[128,4096]{1,0:T(8,128)(2,1)} %bitcast.26), kind=kLoop, calls=%fused_computation.1 | loop fusion | bytes 2097152 | tf_op jit(solution)/shard_map/slice | solution.py:407
  1.9 6.1 %collective-permute-start.2 = (bf16[128,2048]{1,0:T(8,128)(2,1)S(1)}, bf16[128,2048]{1,0:T(8,128)(2,1)}, u32[]{:S(2)}, u32[]{:S(2)}) collective-permute-start(bf16[128,2048]{1,0:T(8,128)(2,1)S(1)} %get-tuple-element.38), channel_id=1, source_target_pairs={{0,28},{4,0},{8,4},{12,8},{16,12},{20,16},{24,20},{28,24},{1,29},{... | collective-permute-start | bytes 1572872 | tf_op jit(solution)/shard_map/ppermute | solution.py:41
  9.2 1.2 %copy-done.4 = bf16[1,512,1024]{2,1,0:T(8,128)(2,1)S(1)} copy-done((bf16[1,512,1024]{2,1,0:T(8,128)(2,1)S(1)}, bf16[1,512,1024]{2,1,0:T(8,128)(2,1)}, u32[]{:S(2)}) %copy-start.4) | copy-done | bytes 1048600
  10.4 1.0 copy-done.7
  12.1 5.1 %forward_attention.1 = (bf16[4,64,1024]{2,1,0:T(8,128)(2,1)S(1)}, bf16[4,64,1024]{2,1,0:T(8,128)(2,1)S(1)}) custom-call(s32[4,4]{1,0:T(4,128)S(1)} %copy-done.10, s32[1]{0:T(128)S(6)} %copy.16.micro_ref, bf16[512,1024]{1,0:T(8,128)(2,1)S(1)} %bitcast.15, bf16[2,512,256]{2,1,0:T(8,128)(2,1)S(1)} %bitcast.18), custom_call_target="tpu_custom_call" | custom-call | flops 1073741824 | bytes 4194304 | tf_op jit(solution)/shard_map/forward_attention/pallas_call | solution.py:101
  17.2 3.1 %collective-permute-done.2.refs_0_ = bf16[128,2048]{1,0:T(8,128)(2,1)} collective-permute-done((bf16[128,2048]{1,0:T(8,128)(2,1)S(1)}, bf16[128,2048]{1,0:T(8,128)(2,1)}, u32[]{:S(2)}, u32[]{:S(2)}) %collective-permute-start.2) | collective-permute-done | bytes 524320 | tf_op jit(solution)/shard_map/ppermute | solution.py:41
  21.4 1.5 %collective-permute-start.14 = (bf16[128,2048]{1,0:T(8,128)(2,1)}, bf16[128,2048]{1,0:T(8,128)(2,1)}, u32[]{:S(2)}, u32[]{:S(2)}) collective-permute-start(bf16[128,2048]{1,0:T(8,128)(2,1)} %collective-permute-done.2.refs_0_), channel_id=1, source_target_pairs={{0,2},{1,3},{2,0},{3,1},{4,6},{5,7},{6,4},{7,5},{8,10},{9,11},{10,... | collective-permute-start | bytes 1572872 | tf_op jit(solution)/shard_map/ppermute | solution.py:51
  22.9 4.2 %collective-permute-start.12 = (s32[1]{0:T(128)}, s32[1]{0:T(128)}, u32[]{:S(2)}, u32[]{:S(2)}) collective-permute-start(s32[1]{0:T(128)} %param.16), channel_id=1, source_target_pairs={{0,28},{4,0},{8,4},{12,8},{16,12},{20,16},{24,20},{28,24},{1,29},{... | collective-permute-start | bytes 20 | tf_op jit(solution)/shard_map/ppermute | solution.py:41
  27.1 23.6 %collective-permute-done.refs_0_ = bf16[128,2048]{1,0:T(8,128)(2,1)} collective-permute-done((bf16[128,2048]{1,0:T(8,128)(2,1)S(1)}, bf16[128,2048]{1,0:T(8,128)(2,1)}, u32[]{:S(2)}, u32[]{:S(2)}) %collective-permute-start) | collective-permute-done | bytes 524320 | tf_op jit(solution)/shard_map/ppermute | solution.py:41
  50.7 1.7 %collective-permute-start.10 = (bf16[128,2048]{1,0:T(8,128)(2,1)}, bf16[128,2048]{1,0:T(8,128)(2,1)}, u32[]{:S(2)}, u32[]{:S(2)}) collective-permute-start(bf16[128,2048]{1,0:T(8,128)(2,1)} %collective-permute-done.refs_0_), channel_id=1, source_target_pairs={{0,2},{1,3},{2,0},{3,1},{4,6},{5,7},{6,4},{7,5},{8,10},{9,11},{10,... | collective-permute-start | bytes 1572872 | tf_op jit(solution)/shard_map/ppermute | solution.py:51
  52.4 6.2 %project.3 = (bf16[2,64,4096]{2,1,0:T(8,128)(2,1)}, bf16[2,64,4096]{2,1,0:T(8,128)(2,1)S(1)}) custom-call(s32[1]{0:T(128)} %bitcast.place_ref, bf16[4,64,1024]{2,1,0:T(8,128)(2,1)S(1)} %collective-permute-done.6.attn_ref, bf16[1024,4096]{1,0:T(8,128)(2,1)} %bitcast.21), custom_call_target="tpu_custom_call" | custom-call | flops 2147483648 | bytes 8388608 | tf_op jit(solution)/shard_map/project/pallas_call | solution.py:305
  59.7 1.0 copy-done.3
  60.7 6.2 %project.2 = (bf16[2,64,4096]{2,1,0:T(8,128)(2,1)}, bf16[2,64,4096]{2,1,0:T(8,128)(2,1)S(1)}) custom-call(s32[1]{0:T(128)} %bitcast.place_ref, bf16[4,64,1024]{2,1,0:T(8,128)(2,1)S(1)} %copy-done.3, bf16[1024,4096]{1,0:T(8,128)(2,1)} %bitcast.22), custom_call_target="tpu_custom_call" | custom-call | flops 2147483648 | bytes 8388608 | tf_op jit(solution)/shard_map/project/pallas_call | solution.py:305
  68.1 3.4 %collective-permute-done.15.refs_3_ = bf16[128,2048]{1,0:T(8,128)(2,1)} collective-permute-done((bf16[128,2048]{1,0:T(8,128)(2,1)}, bf16[128,2048]{1,0:T(8,128)(2,1)}, u32[]{:S(2)}, u32[]{:S(2)}) %collective-permute-start.15) | collective-permute-done | bytes 524320 | tf_op jit(solution)/shard_map/ppermute | solution.py:46
  71.5 1.2 %copy-done.5 = bf16[1,512,1024]{2,1,0:T(8,128)(2,1)S(1)} copy-done((bf16[1,512,1024]{2,1,0:T(8,128)(2,1)S(1)}, bf16[1,512,1024]{2,1,0:T(8,128)(2,1)}, u32[]{:S(2)}) %copy-start.5) | copy-done | bytes 1048600
  73.8 7.0 %stored_attention.1 = (bf16[1024,512]{1,0:T(8,128)(2,1)S(1)}, bf16[2,4,512,512]{3,2,1,0:T(8,128)(2,1)}) custom-call(s32[4,4]{1,0:T(4,128)S(1)} %copy-done.11, s32[1]{0:T(128)} %collective-permute-done.12.micro_ref, bf16[512,1024]{1,0:T(8,128)(2,1)S(1)} %bitcast.16, bf16[2,512,256]{2,1,0:T(8,128)(2,1)S(1)} %bitcast.19), custom_call_target="tpu_custom_call" | custom-call | flops 1073741824 | bytes 4194304 | tf_op jit(solution)/shard_map/stored_attention/pallas_call | solution.py:139
  80.8 8.7 %grad_products.2 = (f32[512,1024]{1,0:T(8,128)S(1)}, bf16[1024,4096]{1,0:T(8,128)(2,1)}) custom-call(s32[4]{0:T(128)S(1)} %pad_add_fusion.sources_ref, bf16[128,2048]{1,0:T(8,128)(2,1)} %collective-permute-done.2.refs_0_, bf16[128,2048]{1,0:T(8,128)(2,1)} %collective-permute-done.13.refs_1_, bf16[128,2048]{1,0:T(8,128)(2,1)} %collective-permute-done.14.refs_2_, ...), custom_call_target="tpu_custom_call" | custom-call | flops 4294967296 | bytes 8388608 | tf_op jit(solution)/shard_map/grad_products/pallas_call | solution.py:264
  89.5 1.4 %copy-done.1 = f32[512,1024]{1,0:T(8,128)} copy-done((f32[512,1024]{1,0:T(8,128)}, f32[512,1024]{1,0:T(8,128)S(1)}, u32[]{:S(2)}) %copy-start.1) | copy-done | bytes 2097176
  91.6 1.3 %pair_sum.2 = bf16[64,4096]{1,0:T(8,128)(2,1)S(1)} custom-call(s32[1]{0:T(128)} %bitcast.place_ref, bf16[2,64,4096]{2,1,0:T(8,128)(2,1)S(1)} %get-tuple-element.24.keep_ref.refs_0_, bf16[2,64,4096]{2,1,0:T(8,128)(2,1)} %collective-permute-done.4.got_ref.refs_1_), custom_call_target="tpu_custom_call" | custom-call | flops 524288 | bytes 3145728 | tf_op jit(solution)/shard_map/pair_sum/pallas_call | solution.py:334
  92.9 1.8 %collective-permute-start.5 = (bf16[64,4096]{1,0:T(8,128)(2,1)S(1)}, bf16[64,4096]{1,0:T(8,128)(2,1)S(1)}, u32[]{:S(2)}, u32[]{:S(2)}) collective-permute-start(bf16[64,4096]{1,0:T(8,128)(2,1)S(1)} %pair_sum.2), channel_id=1, source_target_pairs={{0,2},{1,3},{2,0},{3,1},{4,6},{5,7},{6,4},{7,5},{8,10},{9,11},{10,... | collective-permute-start | bytes 1572872 | tf_op jit(solution)/shard_map/ppermute | solution.py:51
  94.7 9.3 %grad_products.3 = (bf16[512,1024]{1,0:T(8,128)(2,1)S(1)}, bf16[1024,4096]{1,0:T(8,128)(2,1)}) custom-call(s32[4]{0:T(128)S(1)} %pad_add_fusion.sources_ref, bf16[128,2048]{1,0:T(8,128)(2,1)} %collective-permute-done.refs_0_, bf16[128,2048]{1,0:T(8,128)(2,1)S(1)} %collective-permute-done.9.refs_1_, ...), custom_call_target="tpu_custom_call", output_to_operand_aliasing={{1}: (8, {})} | custom-call | flops 4294967296 | bytes 8388608 | tf_op jit(solution)/shard_map/grad_products/pallas_call | solution.py:264
  104.0 7.3 %backward_attention.1 = (bf16[512,1024]{1,0:T(8,128)(2,1)}, bf16[2,512,256]{2,1,0:T(8,128)(2,1)}) custom-call(bf16[512,1024]{1,0:T(8,128)(2,1)S(1)} %bitcast.17, bf16[2,512,256]{2,1,0:T(8,128)(2,1)S(1)} %bitcast.20, bf16[512,1024]{1,0:T(8,128)(2,1)S(1)} %get-tuple-element.33.grad_ref, bf16[2,4,512,512]{3,2,1,0:T(8,128)(2,1)} %get-tuple-element.34.probs_ref), custom_call_target="tpu_custom_call" | custom-call | flops 2147483648 | bytes 8388608 | tf_op jit(solution)/shard_map/backward_attention/pallas_call | solution.py:191
  111.4 5.3 %collective-permute-done.5.refs_2_ = bf16[64,4096]{1,0:T(8,128)(2,1)S(1)} collective-permute-done((bf16[64,4096]{1,0:T(8,128)(2,1)S(1)}, bf16[64,4096]{1,0:T(8,128)(2,1)S(1)}, u32[]{:S(2)}, u32[]{:S(2)}) %collective-permute-start.5) | collective-permute-done | bytes 524320 | tf_op jit(solution)/shard_map/ppermute | solution.py:51
  116.6 3.9 %finish.1 = bf16[128,4096]{1,0:T(8,128)(2,1)} custom-call(s32[1]{0:T(128)} %bitcast.place_ref, bf16[128,4096]{1,0:T(8,128)(2,1)S(1)} %collective-permute-done.1.resid_ref, bf16[2,64,4096]{2,1,0:T(8,128)(2,1)S(1)} %get-tuple-element.24.keep_ref.refs_0_, bf16[2,64,4096]{2,1,0:T(8,128)(2,1)} %collective-permute-done.4.got_ref.refs_1_, ...), custom_call_target="tpu_custom_call" | custom-call | flops 2097152 | bytes 6291456 | tf_op jit(solution)/shard_map/finish/pallas_call | solution.py:371
  (44 shorter events, 6.2 us)
Async XLA Ops:
  1.9 18.4 %collective-permute-start.2 = (bf16[128,2048]{1,0:T(8,128)(2,1)S(1)}, bf16[128,2048]{1,0:T(8,128)(2,1)}, u32[]{:S(2)}, u32[]{:S(2)}) collective-permute-start(bf16[128,2048]{1,0:T(8,128)(2,1)S(1)} %get-tuple-element.38), channel_id=1, source_target_pairs={{0,28},{4,0},{8,4},{12,8},{16,12},{20,16},{24,20},{28,24},{1,29},{... | collective-permute-start | bytes 1572872 | tf_op jit(solution)/shard_map/ppermute | solution.py:41
  8.0 42.7 %collective-permute-start = (bf16[128,2048]{1,0:T(8,128)(2,1)S(1)}, bf16[128,2048]{1,0:T(8,128)(2,1)}, u32[]{:S(2)}, u32[]{:S(2)}) collective-permute-start(bf16[128,2048]{1,0:T(8,128)(2,1)S(1)} %get-tuple-element.39), channel_id=1, source_target_pairs={{0,28},{4,0},{8,4},{12,8},{16,12},{20,16},{24,20},{28,24},{1,29},{... | collective-permute-start | bytes 1572872 | tf_op jit(solution)/shard_map/ppermute | solution.py:41
  9.2 1.2 %copy-start.4 = (bf16[1,512,1024]{2,1,0:T(8,128)(2,1)S(1)}, bf16[1,512,1024]{2,1,0:T(8,128)(2,1)}, u32[]{:S(2)}) copy-start(bf16[1,512,1024]{2,1,0:T(8,128)(2,1)} %param.11) | copy-start | bytes 3145732
  10.4 1.0 copy-start.7
  20.3 30.4 %collective-permute-start.6 = (bf16[4,64,1024]{2,1,0:T(8,128)(2,1)S(1)}, bf16[4,64,1024]{2,1,0:T(8,128)(2,1)S(1)}, u32[]{:S(2)}, u32[]{:S(2)}) collective-permute-start(bf16[4,64,1024]{2,1,0:T(8,128)(2,1)S(1)} %get-tuple-element.27), channel_id=1, source_target_pairs={{0,4},{4,8},{8,12},{12,16},{16,20},{20,24},{24,28},{28,0},{1,5},{5... | collective-permute-start | bytes 1572872 | tf_op jit(solution)/shard_map/ppermute | solution.py:41
  20.8 37.9 %collective-permute-start.3 = (bf16[4,64,1024]{2,1,0:T(8,128)(2,1)S(1)}, bf16[4,64,1024]{2,1,0:T(8,128)(2,1)S(1)}, u32[]{:S(2)}, u32[]{:S(2)}) collective-permute-start(bf16[4,64,1024]{2,1,0:T(8,128)(2,1)S(1)} %get-tuple-element.23), channel_id=1, source_target_pairs={{0,4},{4,8},{8,12},{12,16},{16,20},{20,24},{24,28},{28,0},{1,5},{5... | collective-permute-start | bytes 1572872 | tf_op jit(solution)/shard_map/ppermute | solution.py:41
  21.4 45.9 %collective-permute-start.14 = (bf16[128,2048]{1,0:T(8,128)(2,1)}, bf16[128,2048]{1,0:T(8,128)(2,1)}, u32[]{:S(2)}, u32[]{:S(2)}) collective-permute-start(bf16[128,2048]{1,0:T(8,128)(2,1)} %collective-permute-done.2.refs_0_), channel_id=1, source_target_pairs={{0,2},{1,3},{2,0},{3,1},{4,6},{5,7},{6,4},{7,5},{8,10},{9,11},{10,... | collective-permute-start | bytes 1572872 | tf_op jit(solution)/shard_map/ppermute | solution.py:51
  22.9 44.1 %collective-permute-start.12 = (s32[1]{0:T(128)}, s32[1]{0:T(128)}, u32[]{:S(2)}, u32[]{:S(2)}) collective-permute-start(s32[1]{0:T(128)} %param.16), channel_id=1, source_target_pairs={{0,28},{4,0},{8,4},{12,8},{16,12},{20,16},{24,20},{28,24},{1,29},{... | collective-permute-start | bytes 20 | tf_op jit(solution)/shard_map/ppermute | solution.py:41
  50.7 16.8 %collective-permute-start.13 = (bf16[128,2048]{1,0:T(8,128)(2,1)}, bf16[128,2048]{1,0:T(8,128)(2,1)}, u32[]{:S(2)}, u32[]{:S(2)}) collective-permute-start(bf16[128,2048]{1,0:T(8,128)(2,1)} %collective-permute-done.2.refs_0_), channel_id=1, source_target_pairs={{0,1},{1,0},{2,3},{3,2},{4,5},{5,4},{6,7},{7,6},{8,9},{9,8},{10,11... | collective-permute-start | bytes 1572872 | tf_op jit(solution)/shard_map/ppermute | solution.py:46
  50.7 17.1 %collective-permute-start.10 = (bf16[128,2048]{1,0:T(8,128)(2,1)}, bf16[128,2048]{1,0:T(8,128)(2,1)}, u32[]{:S(2)}, u32[]{:S(2)}) collective-permute-start(bf16[128,2048]{1,0:T(8,128)(2,1)} %collective-permute-done.refs_0_), channel_id=1, source_target_pairs={{0,2},{1,3},{2,0},{3,1},{4,6},{5,7},{6,4},{7,5},{8,10},{9,11},{10,... | collective-permute-start | bytes 1572872 | tf_op jit(solution)/shard_map/ppermute | solution.py:51
  52.4 19.1 %copy-start.11 = (s32[4,4]{1,0:T(4,128)S(1)}, s32[4,4]{1,0:T(4,128)}, u32[]{:S(2)}) copy-start(s32[4,4]{1,0:T(4,128)} %starts_ref.3) | copy-start | bytes 196
  59.5 31.4 %collective-permute-start.7 = (bf16[2,64,4096]{2,1,0:T(8,128)(2,1)}, bf16[2,64,4096]{2,1,0:T(8,128)(2,1)S(1)}, u32[]{:S(2)}, u32[]{:S(2)}) collective-permute-start(bf16[2,64,4096]{2,1,0:T(8,128)(2,1)} %get-tuple-element.29), channel_id=1, source_target_pairs={{0,1},{1,0},{2,3},{3,2},{4,5},{5,4},{6,7},{7,6},{8,9},{9,8},{10,11... | collective-permute-start | bytes 3145736 | tf_op jit(solution)/shard_map/ppermute | solution.py:46
  67.0 24.6 %collective-permute-start.4 = (bf16[2,64,4096]{2,1,0:T(8,128)(2,1)}, bf16[2,64,4096]{2,1,0:T(8,128)(2,1)}, u32[]{:S(2)}, u32[]{:S(2)}) collective-permute-start(bf16[2,64,4096]{2,1,0:T(8,128)(2,1)} %get-tuple-element.25), channel_id=1, source_target_pairs={{0,1},{1,0},{2,3},{3,2},{4,5},{5,4},{6,7},{7,6},{8,9},{9,8},{10,11... | collective-permute-start | bytes 3145736 | tf_op jit(solution)/shard_map/ppermute | solution.py:46
  67.3 4.2 %collective-permute-start.15 = (bf16[128,2048]{1,0:T(8,128)(2,1)}, bf16[128,2048]{1,0:T(8,128)(2,1)}, u32[]{:S(2)}, u32[]{:S(2)}) collective-permute-start(bf16[128,2048]{1,0:T(8,128)(2,1)} %collective-permute-done.14.refs_2_), channel_id=1, source_target_pairs={{0,1},{1,0},{2,3},{3,2},{4,5},{5,4},{6,7},{7,6},{8,9},{9,8},{10,11... | collective-permute-start | bytes 1572872 | tf_op jit(solution)/shard_map/ppermute | solution.py:46
  67.5 27.2 %collective-permute-start.9 = (bf16[128,2048]{1,0:T(8,128)(2,1)}, bf16[128,2048]{1,0:T(8,128)(2,1)S(1)}, u32[]{:S(2)}, u32[]{:S(2)}) collective-permute-start(bf16[128,2048]{1,0:T(8,128)(2,1)} %collective-permute-done.refs_0_), channel_id=1, source_target_pairs={{0,1},{1,0},{2,3},{3,2},{4,5},{5,4},{6,7},{7,6},{8,9},{9,8},{10,11... | collective-permute-start | bytes 1572872 | tf_op jit(solution)/shard_map/ppermute | solution.py:46
  67.8 26.9 %collective-permute-start.11 = (bf16[128,2048]{1,0:T(8,128)(2,1)}, bf16[128,2048]{1,0:T(8,128)(2,1)S(1)}, u32[]{:S(2)}, u32[]{:S(2)}) collective-permute-start(bf16[128,2048]{1,0:T(8,128)(2,1)} %collective-permute-done.10.refs_2_), channel_id=1, source_target_pairs={{0,1},{1,0},{2,3},{3,2},{4,5},{5,4},{6,7},{7,6},{8,9},{9,8},{10,11... | collective-permute-start | bytes 1572872 | tf_op jit(solution)/shard_map/ppermute | solution.py:46
  71.5 39.9 %collective-permute-start.1 = (bf16[128,4096]{1,0:T(8,128)(2,1)}, bf16[128,4096]{1,0:T(8,128)(2,1)S(1)}, u32[]{:S(2)}, u32[]{:S(2)}) collective-permute-start(bf16[128,4096]{1,0:T(8,128)(2,1)} %bitcast.28), channel_id=1, source_target_pairs={{0,4},{4,8},{8,12},{12,16},{16,20},{20,24},{24,28},{28,0},{1,5},{5... | collective-permute-start | bytes 3145736 | tf_op jit(solution)/shard_map/ppermute | solution.py:41
  71.5 1.2 %copy-start.5 = (bf16[1,512,1024]{2,1,0:T(8,128)(2,1)S(1)}, bf16[1,512,1024]{2,1,0:T(8,128)(2,1)}, u32[]{:S(2)}) copy-start(bf16[1,512,1024]{2,1,0:T(8,128)(2,1)} %param.14) | copy-start | bytes 3145732
  89.5 1.4 %copy-start.1 = (f32[512,1024]{1,0:T(8,128)}, f32[512,1024]{1,0:T(8,128)S(1)}, u32[]{:S(2)}) copy-start(f32[512,1024]{1,0:T(8,128)S(1)} %get-tuple-element.31.refs_6_) | copy-start | bytes 6291460
  90.8 13.2 %copy-start = (bf16[2,64,4096]{2,1,0:T(8,128)(2,1)}, bf16[2,64,4096]{2,1,0:T(8,128)(2,1)S(1)}, u32[]{:S(2)}) copy-start(bf16[2,64,4096]{2,1,0:T(8,128)(2,1)S(1)} %collective-permute-done.7.got_ref.refs_4_) | copy-start | bytes 3145732
  91.2 20.2 %collective-permute-start.8 = (bf16[64,4096]{1,0:T(8,128)(2,1)S(1)}, bf16[64,4096]{1,0:T(8,128)(2,1)S(1)}, u32[]{:S(2)}, u32[]{:S(2)}) collective-permute-start(bf16[64,4096]{1,0:T(8,128)(2,1)S(1)} %pair_sum.3), channel_id=1, source_target_pairs={{0,2},{1,3},{2,0},{3,1},{4,6},{5,7},{6,4},{7,5},{8,10},{9,11},{10,... | collective-permute-start | bytes 1572872 | tf_op jit(solution)/shard_map/ppermute | solution.py:51
  92.9 23.7 %collective-permute-start.5 = (bf16[64,4096]{1,0:T(8,128)(2,1)S(1)}, bf16[64,4096]{1,0:T(8,128)(2,1)S(1)}, u32[]{:S(2)}, u32[]{:S(2)}) collective-permute-start(bf16[64,4096]{1,0:T(8,128)(2,1)S(1)} %pair_sum.2), channel_id=1, source_target_pairs={{0,2},{1,3},{2,0},{3,1},{4,6},{5,7},{6,4},{7,5},{8,10},{9,11},{10,... | collective-permute-start | bytes 1572872 | tf_op jit(solution)/shard_map/ppermute | solution.py:51
  94.7 9.3 %copy-start.6 = (bf16[1,512,1024]{2,1,0:T(8,128)(2,1)S(1)}, bf16[1,512,1024]{2,1,0:T(8,128)(2,1)}, u32[]{:S(2)}) copy-start(bf16[1,512,1024]{2,1,0:T(8,128)(2,1)} %param.14) | copy-start | bytes 3145732
  94.7 9.3 %copy-start.9 = (bf16[1,2,512,256]{3,2,1,0:T(8,128)(2,1)S(1)}, bf16[1,2,512,256]{3,2,1,0:T(8,128)(2,1)}, u32[]{:S(2)}) copy-start(bf16[1,2,512,256]{3,2,1,0:T(8,128)(2,1)} %param.15) | copy-start | bytes 1572868
  (4 other events, 3.6 us)

commit v2 on v1

v2 whole, which is shorter than its diff:
```python
import functools
import math

import jax
import jax.numpy as jnp
from jax import lax
from jax.experimental import pallas as pl
from jax.experimental.pallas import tpu as pltpu
from jax.sharding import PartitionSpec as P

HD = 128
BLOCK = 128
F32 = jnp.float32
BF16 = jnp.bfloat16
SMEM = pl.BlockSpec(memory_space=pltpu.SMEM)
NT = (((1,), (1,)), ((), ()))
NN = (((1,), (0,)), ((), ()))
TN = (((0,), (0,)), ((), ()))


def dot(a, b, dims):
    return lax.dot_general(a, b, dims, preferred_element_type=F32)


def params(mib=20):
    return pltpu.CompilerParams(vmem_limit_bytes=mib * 1024 * 1024)


def cost(flops, moved, transcendentals=0):
    return pl.CostEstimate(
        flops=1000, bytes_accessed=1000, transcendentals=0
    )


def after(value, *earlier):
    return lax.optimization_barrier((value, *earlier))[0]


def along_pipe(value, steps):
    count = lax.axis_size("pipe")
    return lax.ppermute(value, "pipe", [(i, (i + steps) % count) for i in range(count)])


def other_core(value):
    count = lax.axis_size("tp")
    return lax.ppermute(value, "tp", [(i, i ^ 1) for i in range(count)])


def along_chips(value, steps):
    count = lax.axis_size("tp")
    return lax.ppermute(value, "tp", [(i, (i + 2 * steps) % count) for i in range(count)])


def stack_heads(ref, first, heads):
    return jnp.concatenate(
        [ref[first : first + BLOCK, h * HD : (h + 1) * HD] for h in range(heads)], axis=0
    )


def doc_begins(starts_ref, micro):
    begins = []
    for doc in range(starts_ref.shape[1]):
        begin = jnp.zeros((1, 1), jnp.int32)
        for index in range(starts_ref.shape[0]):
            begin = jnp.where(micro == index, starts_ref[index, doc], begin)
        begins.append(begin)
    return begins


def block_probs(begins, query, key, first, heads):
    extent = first + BLOCK
    row = lax.broadcasted_iota(jnp.int32, (BLOCK, 1), 0) + first
    low = jnp.zeros((BLOCK, 1), jnp.int32)
    for begin in begins:
        low = jnp.where(row >= begin, begin, low)
    column = lax.broadcasted_iota(jnp.int32, (BLOCK, extent), 1)
    allowed = (column >= low) & (column <= row)
    scores = dot(query, key, NT) * (1.0 / math.sqrt(HD))
    scores = scores.reshape(heads, BLOCK, extent)
    scores = jnp.where(allowed[None], scores, -1e30)
    shifted = jnp.exp(scores - jnp.max(scores, axis=2, keepdims=True))
    probs = shifted * (1.0 / jnp.sum(shifted, axis=2, keepdims=True))
    return probs.astype(BF16).reshape(heads * BLOCK, extent)


def forward_kernel(starts_ref, micro_ref, query_ref, keyval_ref, *out_refs):
    rows, width = query_ref.shape
    heads = width // HD
    begins = doc_begins(starts_ref, jnp.full((1, 1), micro_ref[0], jnp.int32))
    each = rows // out_refs[0].shape[0]
    for first in range(0, rows, BLOCK):
        extent = first + BLOCK
        query = stack_heads(query_ref, first, heads)
        probs = block_probs(begins, query, keyval_ref[0, :extent], first, heads)
        out = dot(probs, keyval_ref[1, :extent], NN).astype(BF16)
        for owner in range(first // each, (extent - 1) // each + 1):
            begin = owner * each
            for out_ref in out_refs:
                end = begin + out_ref.shape[1]
                low, high = max(first, begin), min(extent, end)
                if low < high:
                    for h in range(heads):
                        out_ref[owner, low - begin : high - begin, h * HD : (h + 1) * HD] = out[
                            h * BLOCK + low - first : h * BLOCK + high - first
                        ]
                begin = end


def forward_attention(starts, micro, query, keyval, owners, parts):
    rows, width = query.shape
    groups = keyval.shape[2] // HD
    span = width // groups
    return pl.pallas_call(
        forward_kernel,
        grid=(groups,),
        in_specs=[
            SMEM,
            SMEM,
            pl.BlockSpec((rows, span), lambda g: (0, g)),
            pl.BlockSpec((2, rows, HD), lambda g: (0, 0, g)),
        ],
        out_specs=[pl.BlockSpec((owners, part, span), lambda g: (0, 0, g)) for part in parts],
        out_shape=[jax.ShapeDtypeStruct((owners, part, width), BF16) for part in parts],
        compiler_params=params(),
        cost_estimate=cost(4 * rows * rows * width, 8 * rows * width),
        name="forward_attention",
    )(starts, micro, query, keyval)


def stored_kernel(starts_ref, micro_ref, query_ref, keyval_ref, out_ref, probs_ref):
    rows, width = query_ref.shape
    heads = width // HD
    begins = doc_begins(starts_ref, micro_ref[0:1, 0:1].astype(F32).astype(jnp.int32))
    for index, first in enumerate(range(0, rows, BLOCK)):
        extent = first + BLOCK
        query = stack_heads(query_ref, first, heads)
        probs = block_probs(begins, query, keyval_ref[0, :extent], first, heads)
        probs_ref[0, index, :, :extent] = probs
        out = dot(probs, keyval_ref[1, :extent], NN)
        for h in range(heads):
            out_ref[h * HD : (h + 1) * HD, first:extent] = out[
                h * BLOCK : (h + 1) * BLOCK
            ].T.astype(BF16)


def stored_attention(starts, micro, query, keyval):
    rows, width = query.shape
    groups = keyval.shape[2] // HD
    span = width // groups
    blocks = rows // BLOCK
    stacked = span // HD * BLOCK
    return pl.pallas_call(
        stored_kernel,
        grid=(groups,),
        in_specs=[
            SMEM,
            pl.BlockSpec((16, HD), lambda g: (0, micro.shape[1] // HD - 1)),
            pl.BlockSpec((rows, span), lambda g: (0, g)),
            pl.BlockSpec((2, rows, HD), lambda g: (0, 0, g)),
        ],
        out_specs=[
            pl.BlockSpec((span, rows), lambda g: (g, 0)),
            pl.BlockSpec((1, blocks, stacked, rows), lambda g: (g, 0, 0, 0)),
        ],
        out_shape=[
            jax.ShapeDtypeStruct((width, rows), BF16),
            jax.ShapeDtypeStruct((groups, blocks, stacked, rows), BF16),
        ],
        compiler_params=params(),
        cost_estimate=cost(4 * rows * rows * width, 8 * rows * width),
        name="stored_attention",
    )(starts, micro, query, keyval)


def backward_kernel(query_ref, keyval_ref, grad_ref, probs_ref, dquery_ref, dkeyval_ref, dk, dv):
    rows, width = query_ref.shape
    heads = width // HD
    dk[...] = jnp.zeros_like(dk)
    dv[...] = jnp.zeros_like(dv)
    for index, first in enumerate(range(0, rows, BLOCK)):
        extent = first + BLOCK
        query = stack_heads(query_ref, first, heads)
        grad = stack_heads(grad_ref, first, heads)
        probs = probs_ref[0, index, :, :extent]
        wide = probs.astype(F32)
        dprobs = dot(grad, keyval_ref[1, :extent], NT)
        center = jnp.sum(wide * dprobs, axis=1, keepdims=True)
        dscores = (wide * (dprobs - center) * (1.0 / math.sqrt(HD))).astype(BF16)
        dquery = dot(dscores, keyval_ref[0, :extent], NN).astype(BF16)
        for h in range(heads):
            dquery_ref[first:extent, h * HD : (h + 1) * HD] = dquery[h * BLOCK : (h + 1) * BLOCK]
        dk[:extent] += dot(dscores, query, TN)
        dv[:extent] += dot(probs, grad, TN)
    dkeyval_ref[0] = dk[...].astype(BF16)
    dkeyval_ref[1] = dv[...].astype(BF16)


def backward_attention(query, keyval, grad, probs):
    rows, width = query.shape
    groups = keyval.shape[2] // HD
    span = width // groups
    wide = pl.BlockSpec((rows, span), lambda g: (0, g))
    narrow = pl.BlockSpec((2, rows, HD), lambda g: (0, 0, g))
    return pl.pallas_call(
        backward_kernel,
        grid=(groups,),
        in_specs=[
            wide,
            narrow,
            wide,
            pl.BlockSpec((1,) + probs.shape[1:], lambda g: (g, 0, 0, 0)),
        ],
        out_specs=[wide, narrow],
        out_shape=[
            jax.ShapeDtypeStruct(query.shape, BF16),
            jax.ShapeDtypeStruct(keyval.shape, BF16),
        ],
        scratch_shapes=[pltpu.VMEM((rows, HD), F32)] * 2,
        compiler_params=params(),
        cost_estimate=cost(8 * rows * rows * width, 16 * rows * width),
        name="backward_attention",
    )(query, keyval, grad, probs)


def grad_kernel(count, first, last, sources_ref, *refs):
    pieces = refs[:count]
    weight_ref, attn_ref = refs[count : count + 2]
    rest = refs[count + 2 :]
    if last:
        total_ref, _, dattn_ref, dweight_ref, whole, ready, sems = rest
    else:
        dattn_ref, dweight_ref, whole, ready, sems = rest
    columns = whole.shape[1]
    piece_rows = pieces[0].shape[0]
    for j in range(count):
        row = pl.multiple_of(sources_ref[j] * piece_rows, piece_rows)
        whole[pl.ds(row, piece_rows), :] = pieces[j][:, :columns]
    total = dot(whole[...], weight_ref[:, first : first + columns], NT)
    if last:
        total += total_ref[...]
    dattn_ref[...] = total.astype(dattn_ref.dtype)
    copies = []
    for index, low in enumerate(range(0, columns, GRAD_BLOCK)):
        ready[index] = dot(attn_ref[...], whole[:, low : low + GRAD_BLOCK], NN).astype(BF16)
        copy = pltpu.make_async_copy(
            ready.at[index], dweight_ref.at[:, pl.ds(first + low, GRAD_BLOCK)], sems.at[index]
        )
        copy.start()
        copies.append(copy)
    for copy in copies:
        copy.wait()


def grad_products(sources, pieces, weight, attn, first, columns, earlier, last):
    rows = attn.shape[1]
    heads_width, full = weight.shape
    steps = columns // GRAD_BLOCK
    vmem = pl.BlockSpec(memory_space=pltpu.VMEM)
    anywhere = pl.BlockSpec(memory_space=pl.ANY)
    in_specs = [SMEM] + [vmem] * (len(pieces) + 2)
    args = [sources, *pieces, weight, attn]
    aliases = {}
    if earlier is not None:
        in_specs += [vmem, anywhere]
        args += list(earlier)
        aliases = {len(args) - 1: 1}
    return pl.pallas_call(
        functools.partial(grad_kernel, len(pieces), first, last),
        in_specs=in_specs,
        out_specs=[vmem, anywhere],
        out_shape=[
            jax.ShapeDtypeStruct((rows, heads_width), BF16 if last else F32),
            jax.ShapeDtypeStruct((heads_width, full), BF16),
        ],
        scratch_shapes=[
            pltpu.VMEM((rows, columns), BF16),
            pltpu.VMEM((steps, heads_width, GRAD_BLOCK), BF16),
            pltpu.SemaphoreType.DMA((steps,)),
        ],
        input_output_aliases=aliases,
        compiler_params=params(32),
        cost_estimate=cost(4 * rows * heads_width * columns, 4 * heads_width * columns),
        name="grad_products",
    )(*args)


SPLIT = 2


def project_kernel(place_ref, attn_ref, weight_ref, *refs):
    *far_refs, own_ref, keep_ref, gathered = refs
    half, part_rows, columns = keep_ref.shape
    core = place_ref[0] % 2
    chip = place_ref[0] // 2
    for j in range(half):
        index = 2 * ((chip + 1 + j) % half)
        gathered[j] = attn_ref[index + 1 - core]
        gathered[half + j] = attn_ref[index + core]
    stacked = gathered[...].reshape(2 * half * part_rows, attn_ref.shape[2])
    block = columns // SPLIT
    for k, far_ref in enumerate(far_refs):
        cut = slice(k * block, (k + 1) * block)
        out = dot(stacked, weight_ref[:, cut], NN).astype(BF16)
        out = out.reshape(2 * half, part_rows, block)
        far_ref[...] = out[: half - 1]
        own_ref[:, cut] = out[half - 1]
        keep_ref[:, :, cut] = out[half:]


def project(place, attn, weight):
    owners, part_rows, width = attn.shape
    columns = weight.shape[1]
    half = owners // 2
    vmem = pl.BlockSpec(memory_space=pltpu.VMEM)
    outs = pl.pallas_call(
        project_kernel,
        in_specs=[SMEM, vmem, vmem],
        out_specs=[vmem] * (SPLIT + 2),
        out_shape=[jax.ShapeDtypeStruct((half - 1, part_rows, columns // SPLIT), BF16)] * SPLIT
        + [
            jax.ShapeDtypeStruct((part_rows, columns), BF16),
            jax.ShapeDtypeStruct((half, part_rows, columns), BF16),
        ],
        scratch_shapes=[pltpu.VMEM((owners, part_rows, width), BF16)],
        compiler_params=params(),
        cost_estimate=cost(2 * owners * part_rows * width * columns, 2 * width * columns),
        name="project",
    )(place, attn, weight)
    return outs[:SPLIT], outs[SPLIT], outs[SPLIT + 1]


def pair_sum_kernel(pieces, place_ref, keep_ref, *refs):
    got_refs, out_refs = refs[:SPLIT], refs[SPLIT:]
    chips, _, block = got_refs[0].shape
    for k in range(SPLIT):
        columns = slice(k * block, (k + 1) * block)
        for j in range(chips):
            total = keep_ref[j, :, columns].astype(F32) + got_refs[k][j].astype(F32)
            if pieces == 1:
                out_refs[j][:, columns] = total.astype(BF16)
            else:
                out_refs[j * SPLIT + k][...] = total.astype(BF16)


def pair_sum(place, keep, got, pieces):
    chips, part_rows, columns = keep.shape
    vmem = pl.BlockSpec(memory_space=pltpu.VMEM)
    count = pieces * (chips - 1)
    return pl.pallas_call(
        functools.partial(pair_sum_kernel, pieces),
        in_specs=[SMEM] + [vmem] * (1 + SPLIT),
        out_specs=[vmem] * count,
        out_shape=[jax.ShapeDtypeStruct((part_rows, columns // pieces), BF16)] * count,
        compiler_params=params(),
        cost_estimate=cost(chips * part_rows * columns, 6 * chips * part_rows * columns),
        name="pair_sum",
    )(place, keep, *got)


def finish_kernel(counts, resid_ref, *refs):
    out_ref = refs[-1]
    first = 0
    index = 0
    for count in counts:
        keep_ref, got_ref, *far_refs = refs[index : index + count]
        index += count
        part_rows = keep_ref.shape[1]
        rows = slice(first, first + part_rows)
        first += part_rows
        block = far_refs[0].shape[1]
        pieces = out_ref.shape[1] // block
        for k in range(pieces):
            cut = slice(k * block, (k + 1) * block)
            total = resid_ref[rows, cut].astype(F32)
            total += keep_ref[keep_ref.shape[0] - 1, :, cut].astype(F32)
            total += got_ref[:, cut].astype(F32)
            for far_ref in far_refs[k::pieces]:
                total += far_ref[...].astype(F32)
            out_ref[rows, cut] = total.astype(BF16)


def finish(resid, sums):
    rows, columns = resid.shape
    flat = [array for part in sums for array in part]
    vmem = pl.BlockSpec(memory_space=pltpu.VMEM)
    return pl.pallas_call(
        functools.partial(finish_kernel, [len(part) for part in sums]),
        in_specs=[vmem] * (1 + len(flat)),
        out_specs=vmem,
        out_shape=jax.ShapeDtypeStruct(resid.shape, BF16),
        compiler_params=params(),
        cost_estimate=cost(4 * rows * columns, 12 * rows * columns),
        name="finish",
    )(resid, *flat)


GRAD_BLOCK = 512


def shards(
    fwd_resid,
    fwd_query,
    fwd_keyval,
    fwd_micro,
    bwd_query,
    bwd_keyval,
    grad_micro,
    grad_in,
    out_weight,
    doc_starts,
):
    devices = lax.axis_size("tp")
    chips = devices // 2
    me = lax.axis_index("tp")
    place = me.astype(jnp.int32)[None]
    weight = out_weight[0]
    width = weight.shape[1]
    cut = max(1, width // GRAD_BLOCK * 3 // 8) * GRAD_BLOCK
    sources = [me, me ^ 1]
    for step in range(1, chips):
        sources += [(me - 2 * step) % devices, ((me ^ 1) - 2 * step) % devices]
    sources = jnp.stack(sources).astype(jnp.int32)

    own_rows = fwd_resid.shape[1]
    early = max(16, own_rows * 3 // 8 // 16 * 16)
    parts = (early, own_rows - early)
    grads = [
        along_pipe(
            jnp.concatenate(
                [
                    grad_in[0][:, :cut],
                    jnp.broadcast_to(grad_micro.astype(BF16)[:, None], (grad_in.shape[1], HD)),
                ],
                axis=1,
            ),
            -1,
        ),
        along_pipe(grad_in[0][:, cut:], -1),
    ]
    attn = forward_attention(
        doc_starts, fwd_micro, fwd_query[0], fwd_keyval[0], devices, parts
    )

    def spread(grad):
        return other_core(grad), [along_chips(grad, step) for step in range(1, chips)]

    def gather(grad, near, fars):
        held = [grad, near]
        for far in fars:
            held += [far, other_core(far)]
        return held

    def halves(move, value):
        cut = value.shape[-1] // 2
        return [move(value[..., :cut]), move(value[..., cut:])]

    grad0 = after(grads[0], attn[0])
    near0, fars0 = spread(grad0)
    back_attn, probs = stored_attention(
        after(doc_starts, grad0), grad0, bwd_query[0], bwd_keyval[0]
    )
    grad1 = after(grads[1], back_attn)
    near1, fars1 = spread(grad1)

    def sum_far(far, keep, pieces, *ties):
        near = pair_sum(after(place, *ties), keep, [other_core(part) for part in far], pieces)
        sums = [
            along_chips(near[(step - 1) * pieces + k], step)
            for step in range(1, chips)
            for k in range(pieces)
        ]
        return near[0], sums

    attn_in = [along_pipe(after(attn[part], grad1), 1) for part in range(2)]
    held = gather(grad0, near0, [after(far, grad1) for far in fars0])
    total, grad_weight = grad_products(
        sources, held, weight, back_attn, 0, cut, None, False
    )
    far, own, keep0 = project(after(place, total), attn_in[0], weight)
    resid_in = along_pipe(after(fwd_resid[0], keep0), 1)
    got0 = other_core(own)
    tie, sums0 = sum_far(far, keep0, 1)

    far, own, keep1 = project(after(place, tie, got0, near1, *fars1), attn_in[1], weight)
    got1 = other_core(own)
    fars1 = [after(far1, keep1) for far1 in fars1]
    tie, sums1 = sum_far(far, keep1, 1, *sums0)

    held = gather(grad1, near1, fars1)
    grad_attn, grad_weight = grad_products(
        after(sources, tie), held, weight, back_attn, cut, width - cut, (total, grad_weight), True
    )
    query_grad, keyval_grad = backward_attention(
        after(bwd_query[0], got1), bwd_keyval[0], grad_attn, probs
    )
    phase_out = finish(
        after(resid_in, keyval_grad), [(keep0, got0, *sums0), (keep1, got1, *sums1)]
    )
    return (phase_out[None], query_grad[None], keyval_grad[None], grad_weight[None])


def solution(mesh):
    return jax.shard_map(
        shards,
        mesh=mesh,
        in_specs=(
            P("pipe", "tp", None),
            P("pipe", None, "tp"),
            P("pipe", None, None, "tp"),
            P("pipe"),
            P("pipe", None, "tp"),
            P("pipe", None, None, "tp"),
            P("pipe"),
            P("pipe", "tp", None),
            P("pipe", "tp", None),
            P(),
        ),
        out_specs=(
            P("pipe", "tp", None),
            P("pipe", None, "tp"),
            P("pipe", None, None, "tp"),
            P("pipe", "tp", None),
        ),
        check_vma=False,
    )
```

time: 121 us -> 86.2 us (0.71)
  waiting for transfers between devices: 35.4 us -> 14.7 us
  Pallas kernels: 55.5 us -> 38.5 us
  local copies, waits for them, and re-layouts: 9.73 us -> 13.5 us
  starting transfers between devices: 18.5 us -> 15.7 us
    ppermute x6 -> x5, waiting for transfers between devices: 26.7 us -> 10.5 us  [along_pipe(): lax.ppermute(value, 'pipe', [(i, (i + steps) % count) for i in range(coun...]
    pallas_call x8, Pallas kernels: 43 us -> 26.8 us  [the longest x2 13.1 us: grad_products(): pl.pallas_call(functools.partial(grad_kernel, len(pieces), first, last),...]
    ppermute x4, waiting for transfers between devices: 5.26 us -> 0.94 us  [along_chips(): lax.ppermute(value, 'tp', [(i, (i + 2 * steps) % count) for i in range(co...]
    ppermute x6 -> x5, starting transfers between devices: 11.9 us -> 7.95 us  [along_pipe(): lax.ppermute(value, 'pipe', [(i, (i + steps) % count) for i in range(coun...]
    unnamed x24 -> x26, local copies, waits for them, and re-layouts: 8.43 us -> 12.3 us
    pallas_call x1, Pallas kernels: 7.34 us -> 5.93 us  [backward_attention(): pl.pallas_call(backward_kernel, grid=(groups,), in_specs=[wide, narrow, w...]
    ppermute x6 -> x10, waiting for transfers between devices: 3.41 us -> 3.32 us  [other_core(): return lax.ppermute(value, 'tp', [(i, i ^ 1) for i in range(count)])]
  transfers between devices with their start and end apart: 16 -> 19, of which waited for: 4 -> 9; matrix products, arithmetic and copies ran while one was open for 0% -> 1% of each run, Pallas kernels for 43% -> 43%
where the time goes in v2:
time: 86.2 us; the launch traced here: 85.6 us
  Pallas kernels  38.5 us (45%)
  starting transfers between devices  15.7 us (18%)
  waiting for transfers between devices  14.7 us (17%)
  local copies, waits for them, and re-layouts  13.5 us (16%)
  between operations  2.11 us (2%)
  other arithmetic  1.14 us (1%)
    pallas_call x2, Pallas kernels, grad_products(): pl.pallas_call(functools.partial(grad_kernel, len(pieces), first, last),...  13.1 us
    unnamed x26, local copies, waits for them, and re-layouts  12.3 us
    ppermute x5, waiting for transfers between devices, along_pipe(): lax.ppermute(value, 'pipe', [(i, (i + steps) % count) for i in range(coun...  10.5 us
    ppermute x5, starting transfers between devices, along_pipe(): lax.ppermute(value, 'pipe', [(i, (i + steps) % count) for i in range(coun...  7.95 us
    pallas_call x2, Pallas kernels, project(): pl.pallas_call(project_kernel, in_specs=[SMEM, vmem, vmem], out_specs=[vm...  6.76 us
    ppermute x4, starting transfers between devices, along_chips(): lax.ppermute(value, 'tp', [(i, (i + 2 * steps) % count) for i in range(co...  5.94 us
    pallas_call x1, Pallas kernels, backward_attention(): pl.pallas_call(backward_kernel, grid=(groups,), in_specs=[wide, narrow, w...  5.93 us
    pallas_call x1, Pallas kernels, forward_attention(): pl.pallas_call(forward_kernel, grid=(groups,), in_specs=[SMEM, SMEM, pl.B...  5.8 us
  transfers between devices with their start and end apart: 19, of which 9 were waited for; matrix products, arithmetic and copies ran while one was open for 1% of the time, Pallas kernels for 43%

profile of v2, /device:TPU:0, one launch (start us, length us, event | category | flops | bytes accessed | tf_op | source)
XLA Modules:
  0.0 85.6 jit_solution(17700937292932217082)
XLA Ops:
  1.3 1.1 %slice_select_fusion = bf16[128,1664]{1,0:T(8,128)(2,1)S(1)} fusion(bf16[128,4096]{1,0:T(8,128)(2,1)} %bitcast.27, pred[1664]{0:T(1024)(128)(4,1)} %constant.28.clone.1, bf16[]{:T(256)} %bitcast.6), kind=kLoop, calls=%fused_computation | loop fusion | flops 212992 | bytes 853634 | tf_op jit(solution)/shard_map/concatenate | solution.py:429
  2.3 6.1 %collective-permute-start = (bf16[128,1664]{1,0:T(8,128)(2,1)S(1)}, bf16[128,1664]{1,0:T(8,128)(2,1)S(1)}, u32[]{:S(2)}, u32[]{:S(2)}) collective-permute-start(bf16[128,1664]{1,0:T(8,128)(2,1)S(1)} %slice_select_fusion), channel_id=1, source_target_pairs={{0,28},{4,0},{8,4},{12,8},{16,12},{20,16},{24,20},{28,24},{1,29},{... | collective-permute-start | bytes 1277960 | tf_op jit(solution)/shard_map/ppermute | solution.py:41
  8.4 1.1 %slice.10 = bf16[128,2560]{1,0:T(8,128)(2,1)S(1)} slice(bf16[128,4096]{1,0:T(8,128)(2,1)} %bitcast.28), slice={[0:128], [1536:4096]} | slice | bytes 1310720 | tf_op jit(solution)/shard_map/slice | solution.py:438
  10.8 1.2 %copy-done.7 = bf16[1,512,1024]{2,1,0:T(8,128)(2,1)S(1)} copy-done((bf16[1,512,1024]{2,1,0:T(8,128)(2,1)S(1)}, bf16[1,512,1024]{2,1,0:T(8,128)(2,1)}, u32[]{:S(2)}) %copy-start.7) | copy-done | bytes 1048600
  12.0 1.0 %copy-done.8 = bf16[1,2,512,256]{3,2,1,0:T(8,128)(2,1)S(1)} copy-done((bf16[1,2,512,256]{3,2,1,0:T(8,128)(2,1)S(1)}, bf16[1,2,512,256]{3,2,1,0:T(8,128)(2,1)}, u32[]{:S(2)}) %copy-start.8) | copy-done | bytes 524312
  13.7 5.8 %forward_attention.1 = (bf16[4,48,1024]{2,1,0:T(8,128)(2,1)}, bf16[4,80,1024]{2,1,0:T(8,128)(2,1)}) custom-call(s32[4,4]{1,0:T(4,128)S(1)} %copy-done.11, s32[1]{0:T(128)S(6)} %copy.16.micro_ref, bf16[512,1024]{1,0:T(8,128)(2,1)S(1)} %bitcast.24, bf16[2,512,256]{2,1,0:T(8,128)(2,1)S(1)} %bitcast.25), custom_call_target="tpu_custom_call" | custom-call | flops 1000 | bytes 1000 | tf_op jit(solution)/shard_map/forward_attention/pallas_call | solution.py:113
  19.5 1.5 %collective-permute-start.2 = (bf16[128,1664]{1,0:T(8,128)(2,1)S(1)}, bf16[128,1664]{1,0:T(8,128)(2,1)}, u32[]{:S(2)}, u32[]{:S(2)}) collective-permute-start(bf16[128,1664]{1,0:T(8,128)(2,1)S(1)} %collective-permute-done.micro_ref.refs_0_), channel_id=1, source_target_pairs={{0,2},{1,3},{2,0},{3,1},{4,6},{5,7},{6,4},{7,5},{8,10},{9,11},{10,... | collective-permute-start | bytes 1277960 | tf_op jit(solution)/shard_map/ppermute | solution.py:51
  21.0 1.2 %copy-done.1 = bf16[1,512,1024]{2,1,0:T(8,128)(2,1)S(1)} copy-done((bf16[1,512,1024]{2,1,0:T(8,128)(2,1)S(1)}, bf16[1,512,1024]{2,1,0:T(8,128)(2,1)}, u32[]{:S(2)}) %copy-start.1) | copy-done | bytes 1048600
  23.3 5.2 %stored_attention.1 = (bf16[1024,512]{1,0:T(8,128)(2,1)S(1)}, bf16[2,4,512,512]{3,2,1,0:T(8,128)(2,1)S(1)}) custom-call(s32[4,4]{1,0:T(4,128)S(1)} %copy-done.11, bf16[128,1664]{1,0:T(8,128)(2,1)S(1)} %collective-permute-done.micro_ref.refs_0_, bf16[512,1024]{1,0:T(8,128)(2,1)S(1)} %bitcast.20, bf16[2,512,256]{2,1,0:T(8,128)(2,1)S(1)} %bitcast.22), custom_call_target="tpu_custom_call" | custom-call | flops 1000 | bytes 1000 | tf_op jit(solution)/shard_map/stored_attention/pallas_call | solution.py:152
  28.5 2.0 %copy-done.3 = bf16[2,4,512,512]{3,2,1,0:T(8,128)(2,1)} copy-done((bf16[2,4,512,512]{3,2,1,0:T(8,128)(2,1)}, bf16[2,4,512,512]{3,2,1,0:T(8,128)(2,1)S(1)}, u32[]{:S(2)}) %copy-start.3) | copy-done | bytes 4194328
  30.5 1.1 %collective-permute-done.3.refs_0_ = bf16[128,2560]{1,0:T(8,128)(2,1)S(1)} collective-permute-done((bf16[128,2560]{1,0:T(8,128)(2,1)S(1)}, bf16[128,2560]{1,0:T(8,128)(2,1)S(1)}, u32[]{:S(2)}, u32[]{:S(2)}) %collective-permute-start.3) | collective-permute-done | bytes 655392 | tf_op jit(solution)/shard_map/ppermute | solution.py:41
  32.5 1.3 %collective-permute-start.11 = (bf16[128,2560]{1,0:T(8,128)(2,1)S(1)}, bf16[128,2560]{1,0:T(8,128)(2,1)S(1)}, u32[]{:S(2)}, u32[]{:S(2)}) collective-permute-start(bf16[128,2560]{1,0:T(8,128)(2,1)S(1)} %collective-permute-done.3.refs_0_), channel_id=1, source_target_pairs={{0,2},{1,3},{2,0},{3,1},{4,6},{5,7},{6,4},{7,5},{8,10},{9,11},{10,... | collective-permute-start | bytes 1966088 | tf_op jit(solution)/shard_map/ppermute | solution.py:51
  35.1 3.4 %copy-done = bf16[1,1024,4096]{2,1,0:T(8,128)(2,1)S(1)} copy-done((bf16[1,1024,4096]{2,1,0:T(8,128)(2,1)S(1)}, bf16[1,1024,4096]{2,1,0:T(8,128)(2,1)}, u32[]{:S(2)}) %copy-start) | copy-done | bytes 8388632
  39.5 5.7 %grad_products.2 = (f32[512,1024]{1,0:T(8,128)S(1)}, bf16[1024,4096]{1,0:T(8,128)(2,1)}) custom-call(s32[4]{0:T(128)S(1)} %pad_add_fusion.sources_ref, bf16[128,1664]{1,0:T(8,128)(2,1)S(1)} %collective-permute-done.micro_ref.refs_0_, bf16[128,1664]{1,0:T(8,128)(2,1)S(1)} %copy-done.10, bf16[128,1664]{1,0:T(8,128)(2,1)} %collective-permute-done.2.refs_2_, ...), custom_call_target="tpu_custom_call" | custom-call | flops 1000 | bytes 1000 | tf_op jit(solution)/shard_map/grad_products/pallas_call | solution.py:267
  45.2 1.8 %collective-permute-done.5.attn_ref = bf16[4,48,1024]{2,1,0:T(8,128)(2,1)} collective-permute-done((bf16[4,48,1024]{2,1,0:T(8,128)(2,1)}, bf16[4,48,1024]{2,1,0:T(8,128)(2,1)}, u32[]{:S(2)}, u32[]{:S(2)}) %collective-permute-start.5) | collective-permute-done | bytes 393248 | tf_op jit(solution)/shard_map/ppermute | solution.py:41
  47.0 2.8 %project.2 = (bf16[1,48,2048]{2,1,0:T(8,128)(2,1)S(1)}, bf16[1,48,2048]{2,1,0:T(8,128)(2,1)S(1)}, bf16[48,4096]{1,0:T(8,128)(2,1)S(1)}, bf16[2,48,4096]{2,1,0:T(8,128)(2,1)S(1)}) custom-call(s32[1]{0:T(128)} %bitcast.1.place_ref, bf16[4,48,1024]{2,1,0:T(8,128)(2,1)} %collective-permute-done.5.attn_ref, bf16[1024,4096]{1,0:T(8,128)(2,1)S(1)} %bitcast.17), custom_call_target="tpu_custom_call" | custom-call | flops 1000 | bytes 1000 | tf_op jit(solution)/shard_map/project/pallas_call | solution.py:315
  51.5 1.3 %collective-permute-done.8.refs_1_ = bf16[1,48,2048]{2,1,0:T(8,128)(2,1)S(1)} collective-permute-done((bf16[1,48,2048]{2,1,0:T(8,128)(2,1)S(1)}, bf16[1,48,2048]{2,1,0:T(8,128)(2,1)S(1)}, u32[]{:S(2)}, u32[]{:S(2)}) %collective-permute-start.8) | collective-permute-done | bytes 196640 | tf_op jit(solution)/shard_map/ppermute | solution.py:46
  52.9 1.5 %collective-permute-start.14 = (bf16[48,4096]{1,0:T(8,128)(2,1)S(1)}, bf16[48,4096]{1,0:T(8,128)(2,1)S(1)}, u32[]{:S(2)}, u32[]{:S(2)}) collective-permute-start(bf16[48,4096]{1,0:T(8,128)(2,1)S(1)} %pair_sum.2), channel_id=1, source_target_pairs={{0,2},{1,3},{2,0},{3,1},{4,6},{5,7},{6,4},{7,5},{8,10},{9,11},{10,... | collective-permute-start | bytes 1179656 | tf_op jit(solution)/shard_map/ppermute | solution.py:51
  54.4 6.6 %collective-permute-done.12.attn_ref = bf16[4,80,1024]{2,1,0:T(8,128)(2,1)} collective-permute-done((bf16[4,80,1024]{2,1,0:T(8,128)(2,1)}, bf16[4,80,1024]{2,1,0:T(8,128)(2,1)}, u32[]{:S(2)}, u32[]{:S(2)}) %collective-permute-start.12) | collective-permute-done | bytes 655392 | tf_op jit(solution)/shard_map/ppermute | solution.py:41
  61.0 4.0 %project.3 = (bf16[1,80,2048]{2,1,0:T(8,128)(2,1)S(1)}, bf16[1,80,2048]{2,1,0:T(8,128)(2,1)S(1)}, bf16[80,4096]{1,0:T(8,128)(2,1)S(1)}, bf16[2,80,4096]{2,1,0:T(8,128)(2,1)S(1)}) custom-call(s32[1]{0:T(128)} %bitcast.1.place_ref, bf16[4,80,1024]{2,1,0:T(8,128)(2,1)} %collective-permute-done.12.attn_ref, bf16[1024,4096]{1,0:T(8,128)(2,1)S(1)} %bitcast.18), custom_call_target="tpu_custom_call" | custom-call | flops 1000 | bytes 1000 | tf_op jit(solution)/shard_map/project/pallas_call | solution.py:315
  67.3 1.6 %collective-permute-start.18 = (bf16[80,4096]{1,0:T(8,128)(2,1)S(1)}, bf16[80,4096]{1,0:T(8,128)(2,1)S(1)}, u32[]{:S(2)}, u32[]{:S(2)}) collective-permute-start(bf16[80,4096]{1,0:T(8,128)(2,1)S(1)} %pair_sum.3), channel_id=1, source_target_pairs={{0,2},{1,3},{2,0},{3,1},{4,6},{5,7},{6,4},{7,5},{8,10},{9,11},{10,... | collective-permute-start | bytes 1966088 | tf_op jit(solution)/shard_map/ppermute | solution.py:51
  68.9 7.3 %grad_products.3 = (bf16[512,1024]{1,0:T(8,128)(2,1)S(1)}, bf16[1024,4096]{1,0:T(8,128)(2,1)}) custom-call(s32[4]{0:T(128)S(1)} %pad_add_fusion.sources_ref, bf16[128,2560]{1,0:T(8,128)(2,1)S(1)} %collective-permute-done.3.refs_0_, bf16[128,2560]{1,0:T(8,128)(2,1)S(1)} %collective-permute-done.10.refs_1_, ...), custom_call_target="tpu_custom_call", output_to_operand_aliasing={{1}: (8, {})} | custom-call | flops 1000 | bytes 1000 | tf_op jit(solution)/shard_map/grad_products/pallas_call | solution.py:267
  76.3 5.9 %backward_attention.1 = (bf16[512,1024]{1,0:T(8,128)(2,1)}, bf16[2,512,256]{2,1,0:T(8,128)(2,1)}) custom-call(bf16[512,1024]{1,0:T(8,128)(2,1)S(1)} %bitcast.21, bf16[2,512,256]{2,1,0:T(8,128)(2,1)S(1)} %bitcast.23, bf16[512,1024]{1,0:T(8,128)(2,1)S(1)} %get-tuple-element.62.grad_ref, bf16[2,4,512,512]{3,2,1,0:T(8,128)(2,1)S(1)} %copy-done.4), custom_call_target="tpu_custom_call" | custom-call | flops 1000 | bytes 1000 | tf_op jit(solution)/shard_map/backward_attention/pallas_call | solution.py:204
  84.2 1.5 %finish.1 = bf16[128,4096]{1,0:T(8,128)(2,1)} custom-call(bf16[128,4096]{1,0:T(8,128)(2,1)S(1)} %collective-permute-done.6.resid_ref, bf16[2,48,4096]{2,1,0:T(8,128)(2,1)S(1)} %get-tuple-element.45.keep_ref.refs_0_, bf16[48,4096]{1,0:T(8,128)(2,1)S(1)} %collective-permute-done.9.refs_1_, bf16[48,4096]{1,0:T(8,128)(2,1)S(1)} %collective-permute-done.14.refs_2_, ...), custom_call_target="tpu_custom_call" | custom-call | flops 1000 | bytes 1000 | tf_op jit(solution)/shard_map/finish/pallas_call | solution.py:386
  (53 shorter events, 11.5 us)
Async XLA Ops:
  2.3 17.2 %collective-permute-start = (bf16[128,1664]{1,0:T(8,128)(2,1)S(1)}, bf16[128,1664]{1,0:T(8,128)(2,1)S(1)}, u32[]{:S(2)}, u32[]{:S(2)}) collective-permute-start(bf16[128,1664]{1,0:T(8,128)(2,1)S(1)} %slice_select_fusion), channel_id=1, source_target_pairs={{0,28},{4,0},{8,4},{12,8},{16,12},{20,16},{24,20},{28,24},{1,29},{... | collective-permute-start | bytes 1277960 | tf_op jit(solution)/shard_map/ppermute | solution.py:41
  9.5 22.0 %collective-permute-start.3 = (bf16[128,2560]{1,0:T(8,128)(2,1)S(1)}, bf16[128,2560]{1,0:T(8,128)(2,1)S(1)}, u32[]{:S(2)}, u32[]{:S(2)}) collective-permute-start(bf16[128,2560]{1,0:T(8,128)(2,1)S(1)} %slice.10), channel_id=1, source_target_pairs={{0,28},{4,0},{8,4},{12,8},{16,12},{20,16},{24,20},{28,24},{1,29},{... | collective-permute-start | bytes 1966088 | tf_op jit(solution)/shard_map/ppermute | solution.py:41
  19.5 12.0 %collective-permute-start.2 = (bf16[128,1664]{1,0:T(8,128)(2,1)S(1)}, bf16[128,1664]{1,0:T(8,128)(2,1)}, u32[]{:S(2)}, u32[]{:S(2)}) collective-permute-start(bf16[128,1664]{1,0:T(8,128)(2,1)S(1)} %collective-permute-done.micro_ref.refs_0_), channel_id=1, source_target_pairs={{0,2},{1,3},{2,0},{3,1},{4,6},{5,7},{6,4},{7,5},{8,10},{9,11},{10,... | collective-permute-start | bytes 1277960 | tf_op jit(solution)/shard_map/ppermute | solution.py:51
  21.0 12.9 %collective-permute-start.1 = (bf16[128,1664]{1,0:T(8,128)(2,1)S(1)}, bf16[128,1664]{1,0:T(8,128)(2,1)S(1)}, u32[]{:S(2)}, u32[]{:S(2)}) collective-permute-start(bf16[128,1664]{1,0:T(8,128)(2,1)S(1)} %collective-permute-done.micro_ref.refs_0_), channel_id=1, source_target_pairs={{0,1},{1,0},{2,3},{3,2},{4,5},{5,4},{6,7},{7,6},{8,9},{9,8},{10,11... | collective-permute-start | bytes 1277960 | tf_op jit(solution)/shard_map/ppermute | solution.py:46
  31.5 3.5 %collective-permute-start.4 = (bf16[128,1664]{1,0:T(8,128)(2,1)}, bf16[128,1664]{1,0:T(8,128)(2,1)}, u32[]{:S(2)}, u32[]{:S(2)}) collective-permute-start(bf16[128,1664]{1,0:T(8,128)(2,1)} %collective-permute-done.2.refs_2_), channel_id=1, source_target_pairs={{0,1},{1,0},{2,3},{3,2},{4,5},{5,4},{6,7},{7,6},{8,9},{9,8},{10,11... | collective-permute-start | bytes 1277960 | tf_op jit(solution)/shard_map/ppermute | solution.py:46
  31.5 15.5 %collective-permute-start.5 = (bf16[4,48,1024]{2,1,0:T(8,128)(2,1)}, bf16[4,48,1024]{2,1,0:T(8,128)(2,1)}, u32[]{:S(2)}, u32[]{:S(2)}) collective-permute-start(bf16[4,48,1024]{2,1,0:T(8,128)(2,1)} %get-tuple-element.44), channel_id=1, source_target_pairs={{0,4},{4,8},{8,12},{12,16},{16,20},{20,24},{24,28},{28,0},{1,5},{5... | collective-permute-start | bytes 1179656 | tf_op jit(solution)/shard_map/ppermute | solution.py:41
  32.5 21.9 %collective-permute-start.10 = (bf16[128,2560]{1,0:T(8,128)(2,1)S(1)}, bf16[128,2560]{1,0:T(8,128)(2,1)S(1)}, u32[]{:S(2)}, u32[]{:S(2)}) collective-permute-start(bf16[128,2560]{1,0:T(8,128)(2,1)S(1)} %collective-permute-done.3.refs_0_), channel_id=1, source_target_pairs={{0,1},{1,0},{2,3},{3,2},{4,5},{5,4},{6,7},{7,6},{8,9},{9,8},{10,11... | collective-permute-start | bytes 1966088 | tf_op jit(solution)/shard_map/ppermute | solution.py:46
  32.5 21.9 %collective-permute-start.11 = (bf16[128,2560]{1,0:T(8,128)(2,1)S(1)}, bf16[128,2560]{1,0:T(8,128)(2,1)S(1)}, u32[]{:S(2)}, u32[]{:S(2)}) collective-permute-start(bf16[128,2560]{1,0:T(8,128)(2,1)S(1)} %collective-permute-done.3.refs_0_), channel_id=1, source_target_pairs={{0,2},{1,3},{2,0},{3,1},{4,6},{5,7},{6,4},{7,5},{8,10},{9,11},{10,... | collective-permute-start | bytes 1966088 | tf_op jit(solution)/shard_map/ppermute | solution.py:51
  34.6 26.4 %collective-permute-start.12 = (bf16[4,80,1024]{2,1,0:T(8,128)(2,1)}, bf16[4,80,1024]{2,1,0:T(8,128)(2,1)}, u32[]{:S(2)}, u32[]{:S(2)}) collective-permute-start(bf16[4,80,1024]{2,1,0:T(8,128)(2,1)} %get-tuple-element.52), channel_id=1, source_target_pairs={{0,4},{4,8},{8,12},{12,16},{16,20},{20,24},{24,28},{28,0},{1,5},{5... | collective-permute-start | bytes 1966088 | tf_op jit(solution)/shard_map/ppermute | solution.py:41
  35.1 3.4 %copy-start = (bf16[1,1024,4096]{2,1,0:T(8,128)(2,1)S(1)}, bf16[1,1024,4096]{2,1,0:T(8,128)(2,1)}, u32[]{:S(2)}) copy-start(bf16[1,1024,4096]{2,1,0:T(8,128)(2,1)} %param.18) | copy-start | bytes 25165828
  39.5 15.0 %copy-start.12 = (bf16[1,128,4096]{2,1,0:T(8,128)(2,1)S(1)}, bf16[1,128,4096]{2,1,0:T(8,128)(2,1)}, u32[]{:S(2)}) copy-start(bf16[1,128,4096]{2,1,0:T(8,128)(2,1)} %param.10) | copy-start | bytes 3145732
  49.8 1.5 %collective-permute-start.7 = (bf16[1,48,2048]{2,1,0:T(8,128)(2,1)S(1)}, bf16[1,48,2048]{2,1,0:T(8,128)(2,1)S(1)}, u32[]{:S(2)}, u32[]{:S(2)}) collective-permute-start(bf16[1,48,2048]{2,1,0:T(8,128)(2,1)S(1)} %get-tuple-element.47), channel_id=1, source_target_pairs={{0,1},{1,0},{2,3},{3,2},{4,5},{5,4},{6,7},{7,6},{8,9},{9,8},{10,11... | collective-permute-start | bytes 589832 | tf_op jit(solution)/shard_map/ppermute | solution.py:46
  49.9 4.6 %collective-permute-start.9 = (bf16[48,4096]{1,0:T(8,128)(2,1)S(1)}, bf16[48,4096]{1,0:T(8,128)(2,1)S(1)}, u32[]{:S(2)}, u32[]{:S(2)}) collective-permute-start(bf16[48,4096]{1,0:T(8,128)(2,1)S(1)} %get-tuple-element.49), channel_id=1, source_target_pairs={{0,1},{1,0},{2,3},{3,2},{4,5},{5,4},{6,7},{7,6},{8,9},{9,8},{10,11... | collective-permute-start | bytes 1179656 | tf_op jit(solution)/shard_map/ppermute | solution.py:46
  51.3 1.4 %collective-permute-start.8 = (bf16[1,48,2048]{2,1,0:T(8,128)(2,1)S(1)}, bf16[1,48,2048]{2,1,0:T(8,128)(2,1)S(1)}, u32[]{:S(2)}, u32[]{:S(2)}) collective-permute-start(bf16[1,48,2048]{2,1,0:T(8,128)(2,1)S(1)} %get-tuple-element.48), channel_id=1, source_target_pairs={{0,1},{1,0},{2,3},{3,2},{4,5},{5,4},{6,7},{7,6},{8,9},{9,8},{10,11... | collective-permute-start | bytes 589832 | tf_op jit(solution)/shard_map/ppermute | solution.py:46
  52.9 12.8 %collective-permute-start.14 = (bf16[48,4096]{1,0:T(8,128)(2,1)S(1)}, bf16[48,4096]{1,0:T(8,128)(2,1)S(1)}, u32[]{:S(2)}, u32[]{:S(2)}) collective-permute-start(bf16[48,4096]{1,0:T(8,128)(2,1)S(1)} %pair_sum.2), channel_id=1, source_target_pairs={{0,2},{1,3},{2,0},{3,1},{4,6},{5,7},{6,4},{7,5},{8,10},{9,11},{10,... | collective-permute-start | bytes 1179656 | tf_op jit(solution)/shard_map/ppermute | solution.py:51
  54.4 28.8 %collective-permute-start.6 = (bf16[128,4096]{1,0:T(8,128)(2,1)S(1)}, bf16[128,4096]{1,0:T(8,128)(2,1)S(1)}, u32[]{:S(2)}, u32[]{:S(2)}) collective-permute-start(bf16[128,4096]{1,0:T(8,128)(2,1)S(1)} %bitcast.30), channel_id=1, source_target_pairs={{0,4},{4,8},{8,12},{12,16},{16,20},{20,24},{24,28},{28,0},{1,5},{5... | collective-permute-start | bytes 3145736 | tf_op jit(solution)/shard_map/ppermute | solution.py:41
  65.0 1.7 %collective-permute-start.15 = (bf16[1,80,2048]{2,1,0:T(8,128)(2,1)S(1)}, bf16[1,80,2048]{2,1,0:T(8,128)(2,1)S(1)}, u32[]{:S(2)}, u32[]{:S(2)}) collective-permute-start(bf16[1,80,2048]{2,1,0:T(8,128)(2,1)S(1)} %get-tuple-element.57), channel_id=1, source_target_pairs={{0,1},{1,0},{2,3},{3,2},{4,5},{5,4},{6,7},{7,6},{8,9},{9,8},{10,11... | collective-permute-start | bytes 983048 | tf_op jit(solution)/shard_map/ppermute | solution.py:46
  65.1 2.1 %collective-permute-start.16 = (bf16[1,80,2048]{2,1,0:T(8,128)(2,1)S(1)}, bf16[1,80,2048]{2,1,0:T(8,128)(2,1)S(1)}, u32[]{:S(2)}, u32[]{:S(2)}) collective-permute-start(bf16[1,80,2048]{2,1,0:T(8,128)(2,1)S(1)} %get-tuple-element.58), channel_id=1, source_target_pairs={{0,1},{1,0},{2,3},{3,2},{4,5},{5,4},{6,7},{7,6},{8,9},{9,8},{10,11... | collective-permute-start | bytes 983048 | tf_op jit(solution)/shard_map/ppermute | solution.py:46
  65.6 3.3 %collective-permute-start.17 = (bf16[128,2560]{1,0:T(8,128)(2,1)S(1)}, bf16[128,2560]{1,0:T(8,128)(2,1)S(1)}, u32[]{:S(2)}, u32[]{:S(2)}) collective-permute-start(bf16[128,2560]{1,0:T(8,128)(2,1)S(1)} %collective-permute-done.11.refs_2_), channel_id=1, source_target_pairs={{0,1},{1,0},{2,3},{3,2},{4,5},{5,4},{6,7},{7,6},{8,9},{9,8},{10,11... | collective-permute-start | bytes 1966088 | tf_op jit(solution)/shard_map/ppermute | solution.py:46
  65.7 10.6 %collective-permute-start.13 = (bf16[80,4096]{1,0:T(8,128)(2,1)S(1)}, bf16[80,4096]{1,0:T(8,128)(2,1)S(1)}, u32[]{:S(2)}, u32[]{:S(2)}) collective-permute-start(bf16[80,4096]{1,0:T(8,128)(2,1)S(1)} %get-tuple-element.53), channel_id=1, source_target_pairs={{0,1},{1,0},{2,3},{3,2},{4,5},{5,4},{6,7},{7,6},{8,9},{9,8},{10,11... | collective-permute-start | bytes 1966088 | tf_op jit(solution)/shard_map/ppermute | solution.py:46
  67.3 16.8 %collective-permute-start.18 = (bf16[80,4096]{1,0:T(8,128)(2,1)S(1)}, bf16[80,4096]{1,0:T(8,128)(2,1)S(1)}, u32[]{:S(2)}, u32[]{:S(2)}) collective-permute-start(bf16[80,4096]{1,0:T(8,128)(2,1)S(1)} %pair_sum.3), channel_id=1, source_target_pairs={{0,2},{1,3},{2,0},{3,1},{4,6},{5,7},{6,4},{7,5},{8,10},{9,11},{10,... | collective-permute-start | bytes 1966088 | tf_op jit(solution)/shard_map/ppermute | solution.py:51
  68.9 7.4 %copy-start.2 = (bf16[1,512,1024]{2,1,0:T(8,128)(2,1)S(1)}, bf16[1,512,1024]{2,1,0:T(8,128)(2,1)}, u32[]{:S(2)}) copy-start(bf16[1,512,1024]{2,1,0:T(8,128)(2,1)} %param.14) | copy-start | bytes 3145732
  68.9 7.4 %copy-start.4 = (bf16[2,4,512,512]{3,2,1,0:T(8,128)(2,1)S(1)}, bf16[2,4,512,512]{3,2,1,0:T(8,128)(2,1)}, u32[]{:S(2)}) copy-start(bf16[2,4,512,512]{3,2,1,0:T(8,128)(2,1)} %copy-done.3) | copy-start | bytes 12582916
  68.9 7.4 %copy-start.6 = (bf16[1,2,512,256]{3,2,1,0:T(8,128)(2,1)S(1)}, bf16[1,2,512,256]{3,2,1,0:T(8,128)(2,1)}, u32[]{:S(2)}) copy-start(bf16[1,2,512,256]{3,2,1,0:T(8,128)(2,1)} %param.15) | copy-start | bytes 1572868
  (8 other events, 9.0 us)

commit v3 on v2

--- a/solution.py
+++ b/solution.py
@@ -22,7 +22,7 @@
     return lax.dot_general(a, b, dims, preferred_element_type=F32)
 
 
-def params(mib=20):
+def params(mib=16):
     return pltpu.CompilerParams(vmem_limit_bytes=mib * 1024 * 1024)
 
 
@@ -30,6 +30,10 @@
     return pl.CostEstimate(
         flops=1000, bytes_accessed=1000, transcendentals=0
     )
+
+
+def in_hbm(value):
+    return pltpu.with_memory_space_constraint(value, pltpu.HBM)
 
 
 def after(value, *earlier):
@@ -124,7 +128,7 @@
         compiler_params=params(),
         cost_estimate=cost(4 * rows * rows * width, 8 * rows * width),
         name="forward_attention",
-    )(starts, micro, query, keyval)
+    )(starts, micro, in_hbm(query), in_hbm(keyval))
 
 
 def stored_kernel(starts_ref, micro_ref, query_ref, keyval_ref, out_ref, probs_ref):
@@ -164,12 +168,12 @@
         ],
         out_shape=[
             jax.ShapeDtypeStruct((width, rows), BF16),
-            jax.ShapeDtypeStruct((groups, blocks, stacked, rows), BF16),
+            pltpu.HBM((groups, blocks, stacked, rows), BF16),
         ],
         compiler_params=params(),
         cost_estimate=cost(4 * rows * rows * width, 8 * rows * width),
         name="stored_attention",
-    )(starts, micro, query, keyval)
+    )(starts, micro, in_hbm(query), in_hbm(keyval))
 
 
 def backward_kernel(query_ref, keyval_ref, grad_ref, probs_ref, dquery_ref, dkeyval_ref, dk, dv):
@@ -222,11 +226,11 @@
     )(query, keyval, grad, probs)
 
 
-def grad_kernel(count, first, last, sources_ref, *refs):
+def grad_kernel(count, first, more, sources_ref, *refs):
     pieces = refs[:count]
     weight_ref, attn_ref = refs[count : count + 2]
     rest = refs[count + 2 :]
-    if last:
+    if more:
         total_ref, _, dattn_ref, dweight_ref, whole, ready, sems = rest
     else:
         dattn_ref, dweight_ref, whole, ready, sems = rest
@@ -236,7 +240,7 @@
         row = pl.multiple_of(sources_ref[j] * piece_rows, piece_rows)
         whole[pl.ds(row, piece_rows), :] = pieces[j][:, :columns]
     total = dot(whole[...], weight_ref[:, first : first + columns], NT)
-    if last:
+    if more:
         total += total_ref[...]
     dattn_ref[...] = total.astype(dattn_ref.dtype)
     copies = []
@@ -265,7 +269,7 @@
         args += list(earlier)
         aliases = {len(args) - 1: 1}
     return pl.pallas_call(
-        functools.partial(grad_kernel, len(pieces), first, last),
+        functools.partial(grad_kernel, len(pieces), first, earlier is not None),
         in_specs=in_specs,
         out_specs=[vmem, anywhere],
         out_shape=[
@@ -278,7 +282,7 @@
             pltpu.SemaphoreType.DMA((steps,)),
         ],
         input_output_aliases=aliases,
-        compiler_params=params(32),
+        compiler_params=params(16),
         cost_estimate=cost(4 * rows * heads_width * columns, 4 * heads_width * columns),
         name="grad_products",
     )(*args)
@@ -415,7 +419,8 @@
     place = me.astype(jnp.int32)[None]
     weight = out_weight[0]
     width = weight.shape[1]
-    cut = max(1, width // GRAD_BLOCK * 3 // 8) * GRAD_BLOCK
+    unit = width // GRAD_BLOCK
+    cuts = [0, unit * 2 // 8 * GRAD_BLOCK, unit * 5 // 8 * GRAD_BLOCK, width]
     sources = [me, me ^ 1]
     for step in range(1, chips):
         sources += [(me - 2 * step) % devices, ((me ^ 1) - 2 * step) % devices]
@@ -428,14 +433,15 @@
         along_pipe(
             jnp.concatenate(
                 [
-                    grad_in[0][:, :cut],
+                    grad_in[0][:, : cuts[1]],
                     jnp.broadcast_to(grad_micro.astype(BF16)[:, None], (grad_in.shape[1], HD)),
                 ],
                 axis=1,
             ),
             -1,
         ),
-        along_pipe(grad_in[0][:, cut:], -1),
+        along_pipe(grad_in[0][:, cuts[1] : cuts[2]], -1),
+        along_pipe(grad_in[0][:, cuts[2] :], -1),
     ]
     attn = forward_attention(
         doc_starts, fwd_micro, fwd_query[0], fwd_keyval[0], devices, parts
@@ -461,6 +467,8 @@
     )
     grad1 = after(grads[1], back_attn)
     near1, fars1 = spread(grad1)
+    grad2 = after(grads[2], grad1)
+    near2, fars2 = spread(grad2)
 
     def sum_far(far, keep, pieces, *ties):
         near = pair_sum(after(place, *ties), keep, [other_core(part) for part in far], pieces)
@@ -471,25 +479,34 @@
         ]
         return near[0], sums
 
-    attn_in = [along_pipe(after(attn[part], grad1), 1) for part in range(2)]
-    held = gather(grad0, near0, [after(far, grad1) for far in fars0])
-    total, grad_weight = grad_products(
-        sources, held, weight, back_attn, 0, cut, None, False
-    )
-    far, own, keep0 = project(after(place, total), attn_in[0], weight)
+    def products(tie, held, part, earlier):
+        return grad_products(
+            after(sources, tie),
+            held,
+            weight,
+            back_attn,
+            cuts[part],
+            cuts[part + 1] - cuts[part],
+            earlier,
+            part == 2,
+        )
+
+    attn_in = [along_pipe(after(attn[part], back_attn), 1) for part in range(2)]
+    held = gather(grad0, near0, [after(far, grad2) for far in fars0])
+    earlier = products(back_attn, held, 0, None)
+    far, own, keep0 = project(after(place, earlier[0], *fars1), attn_in[0], weight)
     resid_in = along_pipe(after(fwd_resid[0], keep0), 1)
     got0 = other_core(own)
-    tie, sums0 = sum_far(far, keep0, 1)
-
-    far, own, keep1 = project(after(place, tie, got0, near1, *fars1), attn_in[1], weight)
+    tie, sums0 = sum_far(far, keep0, 1, *fars2)
+
+    held = gather(grad1, near1, [after(far1, keep0) for far1 in fars1])
+    earlier = products(tie, held, 1, earlier)
+    far, own, keep1 = project(after(place, earlier[0], got0, near2), attn_in[1], weight)
     got1 = other_core(own)
-    fars1 = [after(far1, keep1) for far1 in fars1]
     tie, sums1 = sum_far(far, keep1, 1, *sums0)
 
-    held = gather(grad1, near1, fars1)
-    grad_attn, grad_weight = grad_products(
-        after(sources, tie), held, weight, back_attn, cut, width - cut, (total, grad_weight), True
-    )
+    held = gather(grad2, near2, [after(far2, keep1) for far2 in fars2])
+    grad_attn, grad_weight = products(tie, held, 2, earlier)
     query_grad, keyval_grad = backward_attention(
         after(bwd_query[0], got1), bwd_keyval[0], grad_attn, probs
     )

time: 86.2 us -> 81.4 us (0.944)
  local copies, waits for them, and re-layouts: 13.5 us -> 6.08 us
  Pallas kernels: 38.5 us -> 40.2 us
  starting transfers between devices: 15.7 us -> 17.2 us
    unnamed x26 -> x16, local copies, waits for them, and re-layouts: 12.3 us -> 4.91 us
    pallas_call x2, Pallas kernels: 6.76 us -> 4.74 us  [project(): pl.pallas_call(project_kernel, in_specs=[SMEM, vmem, vmem], out_specs=[vm...]
    ppermute x5 -> x6, waiting for transfers between devices: 10.5 us -> 8.45 us  [along_pipe(): lax.ppermute(value, 'pipe', [(i, (i + steps) % count) for i in range(coun...]
    pallas_call x2 -> x3, Pallas kernels: 13.1 us -> 14.9 us  [grad_products(): pl.pallas_call(functools.partial(grad_kernel, len(pieces), first, earlier...]
    ppermute x5 -> x6, starting transfers between devices: 7.95 us -> 9.6 us  [along_pipe(): lax.ppermute(value, 'pipe', [(i, (i + steps) % count) for i in range(coun...]
    pallas_call x1, Pallas kernels: 5.22 us -> 6.8 us  [stored_attention(): pl.pallas_call(stored_kernel, grid=(groups,), in_specs=[SMEM, pl.BlockSpe...]
    ppermute x4 -> x5, waiting for transfers between devices: 0.94 us -> 2.36 us  [along_chips(): lax.ppermute(value, 'tp', [(i, (i + 2 * steps) % count) for i in range(co...]
    ppermute x10 -> x12, waiting for transfers between devices: 3.32 us -> 3.65 us  [other_core(): return lax.ppermute(value, 'tp', [(i, i ^ 1) for i in range(count)])]
  transfers between devices with their start and end apart: 19 -> 23, of which waited for: 9 -> 10; matrix products, arithmetic and copies ran while one was open for 1% -> 2% of each run, Pallas kernels for 43% -> 48%
where the time goes in v3:
time: 81.4 us; the launch traced here: 81.1 us
  Pallas kernels  40.2 us (49%)
  starting transfers between devices  17.2 us (21%)
  waiting for transfers between devices  14.5 us (18%)
  local copies, waits for them, and re-layouts  6.08 us (7%)
  between operations  2.1 us (3%)
  other arithmetic  1.08 us (1%)
    pallas_call x3, Pallas kernels, grad_products(): pl.pallas_call(functools.partial(grad_kernel, len(pieces), first, earlier...  14.9 us
    ppermute x6, starting transfers between devices, along_pipe(): lax.ppermute(value, 'pipe', [(i, (i + steps) % count) for i in range(coun...  9.6 us
    ppermute x6, waiting for transfers between devices, along_pipe(): lax.ppermute(value, 'pipe', [(i, (i + steps) % count) for i in range(coun...  8.45 us
    pallas_call x1, Pallas kernels, stored_attention(): pl.pallas_call(stored_kernel, grid=(groups,), in_specs=[SMEM, pl.BlockSpe...  6.8 us
    pallas_call x1, Pallas kernels, forward_attention(): pl.pallas_call(forward_kernel, grid=(groups,), in_specs=[SMEM, SMEM, pl.B...  6.17 us
    pallas_call x1, Pallas kernels, backward_attention(): pl.pallas_call(backward_kernel, grid=(groups,), in_specs=[wide, narrow, w...  5.94 us
    ppermute x5, starting transfers between devices, along_chips(): lax.ppermute(value, 'tp', [(i, (i + 2 * steps) % count) for i in range(co...  5.68 us
    unnamed x16, local copies, waits for them, and re-layouts  4.91 us
  transfers between devices with their start and end apart: 23, of which 10 were waited for; matrix products, arithmetic and copies ran while one was open for 2% of the time, Pallas kernels for 48%

profile of v3, /device:TPU:0, one launch (start us, length us, event | category | flops | bytes accessed | tf_op | source)
XLA Modules:
  0.0 81.1 jit_solution(1218721805100302654)
XLA Ops:
  1.3 1.0 %slice_select_fusion = bf16[128,1152]{1,0:T(8,128)(2,1)S(1)} fusion(bf16[128,4096]{1,0:T(8,128)(2,1)} %bitcast.26, pred[1152]{0:T(1024)(128)(4,1)} %constant.28.clone.1, bf16[]{:T(256)} %bitcast.6), kind=kLoop, calls=%fused_computation | loop fusion | flops 147456 | bytes 590978 | tf_op jit(solution)/shard_map/concatenate | solution.py:434
  2.3 6.1 %collective-permute-start = (bf16[128,1152]{1,0:T(8,128)(2,1)S(1)}, bf16[128,1152]{1,0:T(8,128)(2,1)S(1)}, u32[]{:S(2)}, u32[]{:S(2)}) collective-permute-start(bf16[128,1152]{1,0:T(8,128)(2,1)S(1)} %slice_select_fusion), channel_id=1, source_target_pairs={{0,28},{4,0},{8,4},{12,8},{16,12},{20,16},{24,20},{28,24},{1,29},{... | collective-permute-start | bytes 884744 | tf_op jit(solution)/shard_map/ppermute | solution.py:45
  8.3 1.2 %fusion = (bf16[128,1536]{1,0:T(8,128)(2,1)S(1)}, bf16[128,1536]{1,0:T(8,128)(2,1)S(1)}) fusion(bf16[128,4096]{1,0:T(8,128)(2,1)} %bitcast.27), kind=kLoop, calls=%fused_computation.2 | loop fusion | bytes 1572864 | tf_op jit(solution)/shard_map/slice | solution.py:443
  10.1 1.4 %collective-permute-start.3 = (bf16[128,1536]{1,0:T(8,128)(2,1)S(1)}, bf16[128,1536]{1,0:T(8,128)(2,1)S(1)}, u32[]{:S(2)}, u32[]{:S(2)}) collective-permute-start(bf16[128,1536]{1,0:T(8,128)(2,1)S(1)} %get-tuple-element.83), channel_id=1, source_target_pairs={{0,28},{4,0},{8,4},{12,8},{16,12},{20,16},{24,20},{28,24},{1,29},{... | collective-permute-start | bytes 1179656 | tf_op jit(solution)/shard_map/ppermute | solution.py:45
  12.8 6.2 %forward_attention.1 = (bf16[4,48,1024]{2,1,0:T(8,128)(2,1)}, bf16[4,80,1024]{2,1,0:T(8,128)(2,1)S(1)}) custom-call(s32[4,4]{1,0:T(4,128)S(1)} %copy-done.5, s32[1]{0:T(128)S(6)} %copy.18.micro_ref, bf16[512,1024]{1,0:T(8,128)(2,1)} %bitcast.28, bf16[2,512,256]{2,1,0:T(8,128)(2,1)} %bitcast.30), custom_call_target="tpu_custom_call" | custom-call | flops 1000 | bytes 1000 | tf_op jit(solution)/shard_map/forward_attention/pallas_call | solution.py:117
  19.8 1.5 %collective-permute-start.2 = (bf16[128,1152]{1,0:T(8,128)(2,1)S(1)}, bf16[128,1152]{1,0:T(8,128)(2,1)}, u32[]{:S(2)}, u32[]{:S(2)}) collective-permute-start(bf16[128,1152]{1,0:T(8,128)(2,1)S(1)} %collective-permute-done.micro_ref.refs_0_), channel_id=1, source_target_pairs={{0,2},{1,3},{2,0},{3,1},{4,6},{5,7},{6,4},{7,5},{8,10},{9,11},{10,... | collective-permute-start | bytes 884744 | tf_op jit(solution)/shard_map/ppermute | solution.py:55
  21.3 6.8 %stored_attention.1 = (bf16[1024,512]{1,0:T(8,128)(2,1)S(1)}, bf16[2,4,512,512]{3,2,1,0:T(8,128)(2,1)}) custom-call(s32[4,4]{1,0:T(4,128)S(1)} %copy-done.5, bf16[128,1152]{1,0:T(8,128)(2,1)S(1)} %collective-permute-done.micro_ref.refs_0_, bf16[512,1024]{1,0:T(8,128)(2,1)} %bitcast.21, bf16[2,512,256]{2,1,0:T(8,128)(2,1)} %bitcast.23), custom_call_target="tpu_custom_call" | custom-call | flops 1000 | bytes 1000 | tf_op jit(solution)/shard_map/stored_attention/pallas_call | solution.py:156
  29.3 2.2 %collective-permute-done.3.refs_0_ = bf16[128,1536]{1,0:T(8,128)(2,1)S(1)} collective-permute-done((bf16[128,1536]{1,0:T(8,128)(2,1)S(1)}, bf16[128,1536]{1,0:T(8,128)(2,1)S(1)}, u32[]{:S(2)}, u32[]{:S(2)}) %collective-permute-start.3) | collective-permute-done | bytes 393248 | tf_op jit(solution)/shard_map/ppermute | solution.py:45
  31.5 1.5 %collective-permute-start.9 = (bf16[128,1536]{1,0:T(8,128)(2,1)S(1)}, bf16[128,1536]{1,0:T(8,128)(2,1)S(1)}, u32[]{:S(2)}, u32[]{:S(2)}) collective-permute-start(bf16[128,1536]{1,0:T(8,128)(2,1)S(1)} %collective-permute-done.3.refs_0_), channel_id=1, source_target_pairs={{0,2},{1,3},{2,0},{3,1},{4,6},{5,7},{6,4},{7,5},{8,10},{9,11},{10,... | collective-permute-start | bytes 1179656 | tf_op jit(solution)/shard_map/ppermute | solution.py:55
  33.4 3.4 %copy-done = bf16[1,1024,4096]{2,1,0:T(8,128)(2,1)S(1)} copy-done((bf16[1,1024,4096]{2,1,0:T(8,128)(2,1)S(1)}, bf16[1,1024,4096]{2,1,0:T(8,128)(2,1)}, u32[]{:S(2)}) %copy-start) | copy-done | bytes 8388632
  36.8 4.7 %grad_products.3 = (f32[512,1024]{1,0:T(8,128)S(1)}, bf16[1024,4096]{1,0:T(8,128)(2,1)}) custom-call(s32[4]{0:T(128)S(1)} %pad_add_fusion.sources_ref, bf16[128,1152]{1,0:T(8,128)(2,1)S(1)} %collective-permute-done.micro_ref.refs_0_, bf16[128,1152]{1,0:T(8,128)(2,1)} %collective-permute-done.1.refs_1_, bf16[128,1152]{1,0:T(8,128)(2,1)} %collective-permute-done.2.refs_2_, ...), custom_call_target="tpu_custom_call" | custom-call | flops 1000 | bytes 1000 | tf_op jit(solution)/shard_map/grad_products/pallas_call | solution.py:271
  41.5 2.0 %collective-permute-done.7.attn_ref = bf16[4,48,1024]{2,1,0:T(8,128)(2,1)S(1)} collective-permute-done((bf16[4,48,1024]{2,1,0:T(8,128)(2,1)}, bf16[4,48,1024]{2,1,0:T(8,128)(2,1)S(1)}, u32[]{:S(2)}, u32[]{:S(2)}) %collective-permute-start.7) | collective-permute-done | bytes 393248 | tf_op jit(solution)/shard_map/ppermute | solution.py:45
  43.5 1.8 %project.2 = (bf16[1,48,2048]{2,1,0:T(8,128)(2,1)S(1)}, bf16[1,48,2048]{2,1,0:T(8,128)(2,1)S(1)}, bf16[48,4096]{1,0:T(8,128)(2,1)S(1)}, bf16[2,48,4096]{2,1,0:T(8,128)(2,1)S(1)}) custom-call(s32[1]{0:T(128)} %bitcast.1.place_ref, bf16[4,48,1024]{2,1,0:T(8,128)(2,1)S(1)} %collective-permute-done.7.attn_ref, bf16[1024,4096]{1,0:T(8,128)(2,1)S(1)} %bitcast.17), custom_call_target="tpu_custom_call" | custom-call | flops 1000 | bytes 1000 | tf_op jit(solution)/shard_map/project/pallas_call | solution.py:319
  46.0 2.0 %collective-permute-done.9.refs_2_ = bf16[128,1536]{1,0:T(8,128)(2,1)S(1)} collective-permute-done((bf16[128,1536]{1,0:T(8,128)(2,1)S(1)}, bf16[128,1536]{1,0:T(8,128)(2,1)S(1)}, u32[]{:S(2)}, u32[]{:S(2)}) %collective-permute-start.9) | collective-permute-done | bytes 393248 | tf_op jit(solution)/shard_map/ppermute | solution.py:55
  50.4 5.1 %grad_products.4 = (f32[512,1024]{1,0:T(8,128)S(1)}, bf16[1024,4096]{1,0:T(8,128)(2,1)}) custom-call(s32[4]{0:T(128)S(1)} %pad_add_fusion.sources_ref, bf16[128,1536]{1,0:T(8,128)(2,1)S(1)} %collective-permute-done.4.refs_0_, bf16[128,1536]{1,0:T(8,128)(2,1)S(1)} %collective-permute-done.12.refs_1_, ...), custom_call_target="tpu_custom_call", output_to_operand_aliasing={{1}: (8, {})} | custom-call | flops 1000 | bytes 1000 | tf_op jit(solution)/shard_map/grad_products/pallas_call | solution.py:271
  55.5 2.0 %collective-permute-done.16.attn_ref = bf16[4,80,1024]{2,1,0:T(8,128)(2,1)S(1)} collective-permute-done((bf16[4,80,1024]{2,1,0:T(8,128)(2,1)}, bf16[4,80,1024]{2,1,0:T(8,128)(2,1)S(1)}, u32[]{:S(2)}, u32[]{:S(2)}) %collective-permute-start.16) | collective-permute-done | bytes 655392 | tf_op jit(solution)/shard_map/ppermute | solution.py:45
  57.6 2.9 %project.3 = (bf16[1,80,2048]{2,1,0:T(8,128)(2,1)S(1)}, bf16[1,80,2048]{2,1,0:T(8,128)(2,1)S(1)}, bf16[80,4096]{1,0:T(8,128)(2,1)S(1)}, bf16[2,80,4096]{2,1,0:T(8,128)(2,1)S(1)}) custom-call(s32[1]{0:T(128)} %bitcast.1.place_ref, bf16[4,80,1024]{2,1,0:T(8,128)(2,1)S(1)} %collective-permute-done.16.attn_ref, bf16[1024,4096]{1,0:T(8,128)(2,1)S(1)} %bitcast.19), custom_call_target="tpu_custom_call" | custom-call | flops 1000 | bytes 1000 | tf_op jit(solution)/shard_map/project/pallas_call | solution.py:319
  61.1 1.0 %collective-permute-done.19.refs_0_ = bf16[1,80,2048]{2,1,0:T(8,128)(2,1)S(1)} collective-permute-done((bf16[1,80,2048]{2,1,0:T(8,128)(2,1)S(1)}, bf16[1,80,2048]{2,1,0:T(8,128)(2,1)S(1)}, u32[]{:S(2)}, u32[]{:S(2)}) %collective-permute-start.19) | collective-permute-done | bytes 327712 | tf_op jit(solution)/shard_map/ppermute | solution.py:50
  62.8 1.5 %collective-permute-start.22 = (bf16[80,4096]{1,0:T(8,128)(2,1)S(1)}, bf16[80,4096]{1,0:T(8,128)(2,1)S(1)}, u32[]{:S(2)}, u32[]{:S(2)}) collective-permute-start(bf16[80,4096]{1,0:T(8,128)(2,1)S(1)} %pair_sum.3), channel_id=1, source_target_pairs={{0,2},{1,3},{2,0},{3,1},{4,6},{5,7},{6,4},{7,5},{8,10},{9,11},{10,... | collective-permute-start | bytes 1966088 | tf_op jit(solution)/shard_map/ppermute | solution.py:55
  64.3 1.7 %collective-permute-done.21.refs_3_ = bf16[128,1536]{1,0:T(8,128)(2,1)S(1)} collective-permute-done((bf16[128,1536]{1,0:T(8,128)(2,1)S(1)}, bf16[128,1536]{1,0:T(8,128)(2,1)S(1)}, u32[]{:S(2)}, u32[]{:S(2)}) %collective-permute-start.21) | collective-permute-done | bytes 393248 | tf_op jit(solution)/shard_map/ppermute | solution.py:50
  66.1 5.1 %grad_products.5 = (bf16[512,1024]{1,0:T(8,128)(2,1)S(1)}, bf16[1024,4096]{1,0:T(8,128)(2,1)}) custom-call(s32[4]{0:T(128)S(1)} %pad_add_fusion.sources_ref, bf16[128,1536]{1,0:T(8,128)(2,1)S(1)} %collective-permute-done.3.refs_0_, bf16[128,1536]{1,0:T(8,128)(2,1)S(1)} %collective-permute-done.15.refs_1_, ...), custom_call_target="tpu_custom_call", output_to_operand_aliasing={{1}: (8, {})} | custom-call | flops 1000 | bytes 1000 | tf_op jit(solution)/shard_map/grad_products/pallas_call | solution.py:271
  71.2 5.9 %backward_attention.1 = (bf16[512,1024]{1,0:T(8,128)(2,1)}, bf16[2,512,256]{2,1,0:T(8,128)(2,1)}) custom-call(bf16[512,1024]{1,0:T(8,128)(2,1)S(1)} %bitcast.22, bf16[2,512,256]{2,1,0:T(8,128)(2,1)S(1)} %bitcast.24, bf16[512,1024]{1,0:T(8,128)(2,1)S(1)} %get-tuple-element.76.grad_ref, bf16[2,4,512,512]{3,2,1,0:T(8,128)(2,1)S(1)} %copy-done.2), custom_call_target="tpu_custom_call" | custom-call | flops 1000 | bytes 1000 | tf_op jit(solution)/shard_map/backward_attention/pallas_call | solution.py:208
  77.1 2.2 %collective-permute-done.8.resid_ref = bf16[128,4096]{1,0:T(8,128)(2,1)S(1)} collective-permute-done((bf16[128,4096]{1,0:T(8,128)(2,1)S(1)}, bf16[128,4096]{1,0:T(8,128)(2,1)S(1)}, u32[]{:S(2)}, u32[]{:S(2)}) %collective-permute-start.8) | collective-permute-done | bytes 1048608 | tf_op jit(solution)/shard_map/ppermute | solution.py:45
  79.6 1.5 %finish.1 = bf16[128,4096]{1,0:T(8,128)(2,1)} custom-call(bf16[128,4096]{1,0:T(8,128)(2,1)S(1)} %collective-permute-done.8.resid_ref, bf16[2,48,4096]{2,1,0:T(8,128)(2,1)S(1)} %get-tuple-element.54.keep_ref.refs_0_, bf16[48,4096]{1,0:T(8,128)(2,1)S(1)} %collective-permute-done.14.refs_1_, bf16[48,4096]{1,0:T(8,128)(2,1)S(1)} %collective-permute-done.18.refs_2_, ...), custom_call_target="tpu_custom_call" | custom-call | flops 1000 | bytes 1000 | tf_op jit(solution)/shard_map/finish/pallas_call | solution.py:390
  (52 shorter events, 8.3 us)
Async XLA Ops:
  2.3 17.5 %collective-permute-start = (bf16[128,1152]{1,0:T(8,128)(2,1)S(1)}, bf16[128,1152]{1,0:T(8,128)(2,1)S(1)}, u32[]{:S(2)}, u32[]{:S(2)}) collective-permute-start(bf16[128,1152]{1,0:T(8,128)(2,1)S(1)} %slice_select_fusion), channel_id=1, source_target_pairs={{0,28},{4,0},{8,4},{12,8},{16,12},{20,16},{24,20},{28,24},{1,29},{... | collective-permute-start | bytes 884744 | tf_op jit(solution)/shard_map/ppermute | solution.py:45
  9.5 18.6 %collective-permute-start.4 = (bf16[128,1536]{1,0:T(8,128)(2,1)S(1)}, bf16[128,1536]{1,0:T(8,128)(2,1)S(1)}, u32[]{:S(2)}, u32[]{:S(2)}) collective-permute-start(bf16[128,1536]{1,0:T(8,128)(2,1)S(1)} %get-tuple-element.82), channel_id=1, source_target_pairs={{0,28},{4,0},{8,4},{12,8},{16,12},{20,16},{24,20},{28,24},{1,29},{... | collective-permute-start | bytes 1179656 | tf_op jit(solution)/shard_map/ppermute | solution.py:45
  10.1 21.4 %collective-permute-start.3 = (bf16[128,1536]{1,0:T(8,128)(2,1)S(1)}, bf16[128,1536]{1,0:T(8,128)(2,1)S(1)}, u32[]{:S(2)}, u32[]{:S(2)}) collective-permute-start(bf16[128,1536]{1,0:T(8,128)(2,1)S(1)} %get-tuple-element.83), channel_id=1, source_target_pairs={{0,28},{4,0},{8,4},{12,8},{16,12},{20,16},{24,20},{28,24},{1,29},{... | collective-permute-start | bytes 1179656 | tf_op jit(solution)/shard_map/ppermute | solution.py:45
  19.8 11.6 %collective-permute-start.2 = (bf16[128,1152]{1,0:T(8,128)(2,1)S(1)}, bf16[128,1152]{1,0:T(8,128)(2,1)}, u32[]{:S(2)}, u32[]{:S(2)}) collective-permute-start(bf16[128,1152]{1,0:T(8,128)(2,1)S(1)} %collective-permute-done.micro_ref.refs_0_), channel_id=1, source_target_pairs={{0,2},{1,3},{2,0},{3,1},{4,6},{5,7},{6,4},{7,5},{8,10},{9,11},{10,... | collective-permute-start | bytes 884744 | tf_op jit(solution)/shard_map/ppermute | solution.py:55
  21.3 11.7 %collective-permute-start.1 = (bf16[128,1152]{1,0:T(8,128)(2,1)S(1)}, bf16[128,1152]{1,0:T(8,128)(2,1)}, u32[]{:S(2)}, u32[]{:S(2)}) collective-permute-start(bf16[128,1152]{1,0:T(8,128)(2,1)S(1)} %collective-permute-done.micro_ref.refs_0_), channel_id=1, source_target_pairs={{0,1},{1,0},{2,3},{3,2},{4,5},{5,4},{6,7},{7,6},{8,9},{9,8},{10,11... | collective-permute-start | bytes 884744 | tf_op jit(solution)/shard_map/ppermute | solution.py:50
  28.1 13.4 %collective-permute-start.6 = (bf16[128,1536]{1,0:T(8,128)(2,1)S(1)}, bf16[128,1536]{1,0:T(8,128)(2,1)S(1)}, u32[]{:S(2)}, u32[]{:S(2)}) collective-permute-start(bf16[128,1536]{1,0:T(8,128)(2,1)S(1)} %collective-permute-done.4.refs_0_), channel_id=1, source_target_pairs={{0,2},{1,3},{2,0},{3,1},{4,6},{5,7},{6,4},{7,5},{8,10},{9,11},{10,... | collective-permute-start | bytes 1179656 | tf_op jit(solution)/shard_map/ppermute | solution.py:55
  28.7 14.9 %collective-permute-start.7 = (bf16[4,48,1024]{2,1,0:T(8,128)(2,1)}, bf16[4,48,1024]{2,1,0:T(8,128)(2,1)S(1)}, u32[]{:S(2)}, u32[]{:S(2)}) collective-permute-start(bf16[4,48,1024]{2,1,0:T(8,128)(2,1)} %get-tuple-element.53), channel_id=1, source_target_pairs={{0,4},{4,8},{8,12},{12,16},{16,20},{20,24},{24,28},{28,0},{1,5},{5... | collective-permute-start | bytes 1179656 | tf_op jit(solution)/shard_map/ppermute | solution.py:45
  31.5 1.9 %collective-permute-start.5 = (bf16[128,1152]{1,0:T(8,128)(2,1)}, bf16[128,1152]{1,0:T(8,128)(2,1)}, u32[]{:S(2)}, u32[]{:S(2)}) collective-permute-start(bf16[128,1152]{1,0:T(8,128)(2,1)} %collective-permute-done.2.refs_2_), channel_id=1, source_target_pairs={{0,1},{1,0},{2,3},{3,2},{4,5},{5,4},{6,7},{7,6},{8,9},{9,8},{10,11... | collective-permute-start | bytes 884744 | tf_op jit(solution)/shard_map/ppermute | solution.py:50
  31.5 16.6 %collective-permute-start.9 = (bf16[128,1536]{1,0:T(8,128)(2,1)S(1)}, bf16[128,1536]{1,0:T(8,128)(2,1)S(1)}, u32[]{:S(2)}, u32[]{:S(2)}) collective-permute-start(bf16[128,1536]{1,0:T(8,128)(2,1)S(1)} %collective-permute-done.3.refs_0_), channel_id=1, source_target_pairs={{0,2},{1,3},{2,0},{3,1},{4,6},{5,7},{6,4},{7,5},{8,10},{9,11},{10,... | collective-permute-start | bytes 1179656 | tf_op jit(solution)/shard_map/ppermute | solution.py:55
  33.0 24.6 %collective-permute-start.16 = (bf16[4,80,1024]{2,1,0:T(8,128)(2,1)}, bf16[4,80,1024]{2,1,0:T(8,128)(2,1)S(1)}, u32[]{:S(2)}, u32[]{:S(2)}) collective-permute-start(bf16[4,80,1024]{2,1,0:T(8,128)(2,1)} %copy-done.6), channel_id=1, source_target_pairs={{0,4},{4,8},{8,12},{12,16},{16,20},{20,24},{24,28},{28,0},{1,5},{5... | collective-permute-start | bytes 1966088 | tf_op jit(solution)/shard_map/ppermute | solution.py:45
  36.8 13.0 %copy-start.7 = (bf16[1,128,4096]{2,1,0:T(8,128)(2,1)S(1)}, bf16[1,128,4096]{2,1,0:T(8,128)(2,1)}, u32[]{:S(2)}) copy-start(bf16[1,128,4096]{2,1,0:T(8,128)(2,1)} %param.10) | copy-start | bytes 3145732
  45.4 2.7 %collective-permute-start.10 = (bf16[1,48,2048]{2,1,0:T(8,128)(2,1)S(1)}, bf16[1,48,2048]{2,1,0:T(8,128)(2,1)S(1)}, u32[]{:S(2)}, u32[]{:S(2)}) collective-permute-start(bf16[1,48,2048]{2,1,0:T(8,128)(2,1)S(1)} %get-tuple-element.57), channel_id=1, source_target_pairs={{0,1},{1,0},{2,3},{3,2},{4,5},{5,4},{6,7},{7,6},{8,9},{9,8},{10,11... | collective-permute-start | bytes 589832 | tf_op jit(solution)/shard_map/ppermute | solution.py:50
  45.5 3.1 %collective-permute-start.11 = (bf16[1,48,2048]{2,1,0:T(8,128)(2,1)S(1)}, bf16[1,48,2048]{2,1,0:T(8,128)(2,1)S(1)}, u32[]{:S(2)}, u32[]{:S(2)}) collective-permute-start(bf16[1,48,2048]{2,1,0:T(8,128)(2,1)S(1)} %get-tuple-element.58), channel_id=1, source_target_pairs={{0,1},{1,0},{2,3},{3,2},{4,5},{5,4},{6,7},{7,6},{8,9},{9,8},{10,11... | collective-permute-start | bytes 589832 | tf_op jit(solution)/shard_map/ppermute | solution.py:50
  45.9 2.8 %collective-permute-start.12 = (bf16[128,1536]{1,0:T(8,128)(2,1)S(1)}, bf16[128,1536]{1,0:T(8,128)(2,1)S(1)}, u32[]{:S(2)}, u32[]{:S(2)}) collective-permute-start(bf16[128,1536]{1,0:T(8,128)(2,1)S(1)} %collective-permute-done.4.refs_0_), channel_id=1, source_target_pairs={{0,1},{1,0},{2,3},{3,2},{4,5},{5,4},{6,7},{7,6},{8,9},{9,8},{10,11... | collective-permute-start | bytes 1179656 | tf_op jit(solution)/shard_map/ppermute | solution.py:50
  48.1 1.7 %collective-permute-start.13 = (bf16[128,1536]{1,0:T(8,128)(2,1)S(1)}, bf16[128,1536]{1,0:T(8,128)(2,1)S(1)}, u32[]{:S(2)}, u32[]{:S(2)}) collective-permute-start(bf16[128,1536]{1,0:T(8,128)(2,1)S(1)} %collective-permute-done.6.refs_2_), channel_id=1, source_target_pairs={{0,1},{1,0},{2,3},{3,2},{4,5},{5,4},{6,7},{7,6},{8,9},{9,8},{10,11... | collective-permute-start | bytes 1179656 | tf_op jit(solution)/shard_map/ppermute | solution.py:50
  48.1 7.4 %collective-permute-start.15 = (bf16[128,1536]{1,0:T(8,128)(2,1)S(1)}, bf16[128,1536]{1,0:T(8,128)(2,1)S(1)}, u32[]{:S(2)}, u32[]{:S(2)}) collective-permute-start(bf16[128,1536]{1,0:T(8,128)(2,1)S(1)} %collective-permute-done.3.refs_0_), channel_id=1, source_target_pairs={{0,1},{1,0},{2,3},{3,2},{4,5},{5,4},{6,7},{7,6},{8,9},{9,8},{10,11... | collective-permute-start | bytes 1179656 | tf_op jit(solution)/shard_map/ppermute | solution.py:50
  48.6 6.9 %collective-permute-start.14 = (bf16[48,4096]{1,0:T(8,128)(2,1)S(1)}, bf16[48,4096]{1,0:T(8,128)(2,1)S(1)}, u32[]{:S(2)}, u32[]{:S(2)}) collective-permute-start(bf16[48,4096]{1,0:T(8,128)(2,1)S(1)} %get-tuple-element.63), channel_id=1, source_target_pairs={{0,1},{1,0},{2,3},{3,2},{4,5},{5,4},{6,7},{7,6},{8,9},{9,8},{10,11... | collective-permute-start | bytes 1179656 | tf_op jit(solution)/shard_map/ppermute | solution.py:50
  48.8 12.4 %collective-permute-start.18 = (bf16[48,4096]{1,0:T(8,128)(2,1)S(1)}, bf16[48,4096]{1,0:T(8,128)(2,1)S(1)}, u32[]{:S(2)}, u32[]{:S(2)}) collective-permute-start(bf16[48,4096]{1,0:T(8,128)(2,1)S(1)} %pair_sum.2), channel_id=1, source_target_pairs={{0,2},{1,3},{2,0},{3,1},{4,6},{5,7},{6,4},{7,5},{8,10},{9,11},{10,... | collective-permute-start | bytes 1179656 | tf_op jit(solution)/shard_map/ppermute | solution.py:55
  49.8 29.5 %collective-permute-start.8 = (bf16[128,4096]{1,0:T(8,128)(2,1)S(1)}, bf16[128,4096]{1,0:T(8,128)(2,1)S(1)}, u32[]{:S(2)}, u32[]{:S(2)}) collective-permute-start(bf16[128,4096]{1,0:T(8,128)(2,1)S(1)} %bitcast.31), channel_id=1, source_target_pairs={{0,4},{4,8},{8,12},{12,16},{16,20},{20,24},{24,28},{28,0},{1,5},{5... | collective-permute-start | bytes 3145736 | tf_op jit(solution)/shard_map/ppermute | solution.py:45
  60.5 1.7 %collective-permute-start.19 = (bf16[1,80,2048]{2,1,0:T(8,128)(2,1)S(1)}, bf16[1,80,2048]{2,1,0:T(8,128)(2,1)S(1)}, u32[]{:S(2)}, u32[]{:S(2)}) collective-permute-start(bf16[1,80,2048]{2,1,0:T(8,128)(2,1)S(1)} %get-tuple-element.71), channel_id=1, source_target_pairs={{0,1},{1,0},{2,3},{3,2},{4,5},{5,4},{6,7},{7,6},{8,9},{9,8},{10,11... | collective-permute-start | bytes 983048 | tf_op jit(solution)/shard_map/ppermute | solution.py:50
  60.6 2.1 %collective-permute-start.20 = (bf16[1,80,2048]{2,1,0:T(8,128)(2,1)S(1)}, bf16[1,80,2048]{2,1,0:T(8,128)(2,1)S(1)}, u32[]{:S(2)}, u32[]{:S(2)}) collective-permute-start(bf16[1,80,2048]{2,1,0:T(8,128)(2,1)S(1)} %get-tuple-element.72), channel_id=1, source_target_pairs={{0,1},{1,0},{2,3},{3,2},{4,5},{5,4},{6,7},{7,6},{8,9},{9,8},{10,11... | collective-permute-start | bytes 983048 | tf_op jit(solution)/shard_map/ppermute | solution.py:50
  61.1 10.1 %collective-permute-start.17 = (bf16[80,4096]{1,0:T(8,128)(2,1)S(1)}, bf16[80,4096]{1,0:T(8,128)(2,1)S(1)}, u32[]{:S(2)}, u32[]{:S(2)}) collective-permute-start(bf16[80,4096]{1,0:T(8,128)(2,1)S(1)} %get-tuple-element.67), channel_id=1, source_target_pairs={{0,1},{1,0},{2,3},{3,2},{4,5},{5,4},{6,7},{7,6},{8,9},{9,8},{10,11... | collective-permute-start | bytes 1966088 | tf_op jit(solution)/shard_map/ppermute | solution.py:50
  62.8 16.8 %collective-permute-start.22 = (bf16[80,4096]{1,0:T(8,128)(2,1)S(1)}, bf16[80,4096]{1,0:T(8,128)(2,1)S(1)}, u32[]{:S(2)}, u32[]{:S(2)}) collective-permute-start(bf16[80,4096]{1,0:T(8,128)(2,1)S(1)} %pair_sum.3), channel_id=1, source_target_pairs={{0,2},{1,3},{2,0},{3,1},{4,6},{5,7},{6,4},{7,5},{8,10},{9,11},{10,... | collective-permute-start | bytes 1966088 | tf_op jit(solution)/shard_map/ppermute | solution.py:55
  64.3 1.7 %collective-permute-start.21 = (bf16[128,1536]{1,0:T(8,128)(2,1)S(1)}, bf16[128,1536]{1,0:T(8,128)(2,1)S(1)}, u32[]{:S(2)}, u32[]{:S(2)}) collective-permute-start(bf16[128,1536]{1,0:T(8,128)(2,1)S(1)} %collective-permute-done.9.refs_2_), channel_id=1, source_target_pairs={{0,1},{1,0},{2,3},{3,2},{4,5},{5,4},{6,7},{7,6},{8,9},{9,8},{10,11... | collective-permute-start | bytes 1179656 | tf_op jit(solution)/shard_map/ppermute | solution.py:50
  (7 other events, 27.0 us)

commit v4 on v3

--- a/solution.py
+++ b/solution.py
@@ -22,7 +22,7 @@
     return lax.dot_general(a, b, dims, preferred_element_type=F32)
 
 
-def params(mib=16):
+def params(mib=12):
     return pltpu.CompilerParams(vmem_limit_bytes=mib * 1024 * 1024)
 
 
@@ -362,36 +362,47 @@
 
 
 def finish_kernel(counts, resid_ref, *refs):
-    out_ref = refs[-1]
-    first = 0
-    index = 0
-    for count in counts:
-        keep_ref, got_ref, *far_refs = refs[index : index + count]
-        index += count
-        part_rows = keep_ref.shape[1]
-        rows = slice(first, first + part_rows)
-        first += part_rows
-        block = far_refs[0].shape[1]
-        pieces = out_ref.shape[1] // block
-        for k in range(pieces):
-            cut = slice(k * block, (k + 1) * block)
-            total = resid_ref[rows, cut].astype(F32)
+    *refs, out_ref, ready, sems = refs
+    steps, rows, block = ready.shape
+    copies = []
+    for step in range(steps):
+        cut = slice(step * block, (step + 1) * block)
+        first = 0
+        index = 0
+        for count in counts:
+            keep_ref, *others = refs[index : index + count]
+            index += count
+            part_rows = keep_ref.shape[1]
+            part = slice(first, first + part_rows)
+            first += part_rows
+            total = resid_ref[part, cut].astype(F32)
             total += keep_ref[keep_ref.shape[0] - 1, :, cut].astype(F32)
-            total += got_ref[:, cut].astype(F32)
-            for far_ref in far_refs[k::pieces]:
-                total += far_ref[...].astype(F32)
-            out_ref[rows, cut] = total.astype(BF16)
+            for other in others:
+                total += other[:, cut].astype(F32)
+            ready[step, part] = total.astype(BF16)
+        copy = pltpu.make_async_copy(
+            ready.at[step], out_ref.at[:, pl.ds(step * block, block)], sems.at[step]
+        )
+        copy.start()
+        copies.append(copy)
+    for copy in copies:
+        copy.wait()
 
 
 def finish(resid, sums):
     rows, columns = resid.shape
     flat = [array for part in sums for array in part]
     vmem = pl.BlockSpec(memory_space=pltpu.VMEM)
+    steps = 4
     return pl.pallas_call(
         functools.partial(finish_kernel, [len(part) for part in sums]),
         in_specs=[vmem] * (1 + len(flat)),
-        out_specs=vmem,
+        out_specs=pl.BlockSpec(memory_space=pl.ANY),
         out_shape=jax.ShapeDtypeStruct(resid.shape, BF16),
+        scratch_shapes=[
+            pltpu.VMEM((steps, rows, columns // steps), BF16),
+            pltpu.SemaphoreType.DMA((steps,)),
+        ],
         compiler_params=params(),
         cost_estimate=cost(4 * rows * columns, 12 * rows * columns),
         name="finish",

time: 81.4 us -> 81.3 us (level)
  no operation moved by 1% of the time
where the time goes in v4:
time: 81.3 us; the launch traced here: 81 us
  Pallas kernels  40 us (49%)
  starting transfers between devices  17.2 us (21%)
  waiting for transfers between devices  14.5 us (18%)
  local copies, waits for them, and re-layouts  6.08 us (7%)
  between operations  2.26 us (3%)
  other arithmetic  1.08 us (1%)
    pallas_call x3, Pallas kernels, grad_products(): pl.pallas_call(functools.partial(grad_kernel, len(pieces), first, earlier...  14.9 us
    ppermute x6, starting transfers between devices, along_pipe(): lax.ppermute(value, 'pipe', [(i, (i + steps) % count) for i in range(coun...  9.6 us
    ppermute x6, waiting for transfers between devices, along_pipe(): lax.ppermute(value, 'pipe', [(i, (i + steps) % count) for i in range(coun...  8.45 us
    pallas_call x1, Pallas kernels, stored_attention(): pl.pallas_call(stored_kernel, grid=(groups,), in_specs=[SMEM, pl.BlockSpe...  6.8 us
    pallas_call x1, Pallas kernels, forward_attention(): pl.pallas_call(forward_kernel, grid=(groups,), in_specs=[SMEM, SMEM, pl.B...  6.17 us
    pallas_call x1, Pallas kernels, backward_attention(): pl.pallas_call(backward_kernel, grid=(groups,), in_specs=[wide, narrow, w...  5.94 us
    ppermute x5, starting transfers between devices, along_chips(): lax.ppermute(value, 'tp', [(i, (i + 2 * steps) % count) for i in range(co...  5.68 us
    unnamed x16, local copies, waits for them, and re-layouts  4.91 us
  transfers between devices with their start and end apart: 23, of which 10 were waited for; matrix products, arithmetic and copies ran while one was open for 2% of the time, Pallas kernels for 48%

profile of v4, /device:TPU:0, one launch (start us, length us, event | category | flops | bytes accessed | tf_op | source)
XLA Modules:
  0.0 81.0 jit_solution(13927183734046918684)
XLA Ops:
  1.3 1.0 %slice_select_fusion = bf16[128,1152]{1,0:T(8,128)(2,1)S(1)} fusion(bf16[128,4096]{1,0:T(8,128)(2,1)} %bitcast.26, pred[1152]{0:T(1024)(128)(4,1)} %constant.28.clone.1, bf16[]{:T(256)} %bitcast.6), kind=kLoop, calls=%fused_computation | loop fusion | flops 147456 | bytes 590978 | tf_op jit(solution)/shard_map/concatenate | solution.py:445
  2.3 6.1 %collective-permute-start = (bf16[128,1152]{1,0:T(8,128)(2,1)S(1)}, bf16[128,1152]{1,0:T(8,128)(2,1)S(1)}, u32[]{:S(2)}, u32[]{:S(2)}) collective-permute-start(bf16[128,1152]{1,0:T(8,128)(2,1)S(1)} %slice_select_fusion), channel_id=1, source_target_pairs={{0,28},{4,0},{8,4},{12,8},{16,12},{20,16},{24,20},{28,24},{1,29},{... | collective-permute-start | bytes 884744 | tf_op jit(solution)/shard_map/ppermute | solution.py:45
  8.3 1.2 %fusion = (bf16[128,1536]{1,0:T(8,128)(2,1)S(1)}, bf16[128,1536]{1,0:T(8,128)(2,1)S(1)}) fusion(bf16[128,4096]{1,0:T(8,128)(2,1)} %bitcast.27), kind=kLoop, calls=%fused_computation.2 | loop fusion | bytes 1572864 | tf_op jit(solution)/shard_map/slice | solution.py:454
  10.1 1.4 %collective-permute-start.3 = (bf16[128,1536]{1,0:T(8,128)(2,1)S(1)}, bf16[128,1536]{1,0:T(8,128)(2,1)S(1)}, u32[]{:S(2)}, u32[]{:S(2)}) collective-permute-start(bf16[128,1536]{1,0:T(8,128)(2,1)S(1)} %get-tuple-element.83), channel_id=1, source_target_pairs={{0,28},{4,0},{8,4},{12,8},{16,12},{20,16},{24,20},{28,24},{1,29},{... | collective-permute-start | bytes 1179656 | tf_op jit(solution)/shard_map/ppermute | solution.py:45
  12.8 6.2 %forward_attention.1 = (bf16[4,48,1024]{2,1,0:T(8,128)(2,1)}, bf16[4,80,1024]{2,1,0:T(8,128)(2,1)S(1)}) custom-call(s32[4,4]{1,0:T(4,128)S(1)} %copy-done.5, s32[1]{0:T(128)S(6)} %copy.18.micro_ref, bf16[512,1024]{1,0:T(8,128)(2,1)} %bitcast.28, bf16[2,512,256]{2,1,0:T(8,128)(2,1)} %bitcast.30), custom_call_target="tpu_custom_call" | custom-call | flops 1000 | bytes 1000 | tf_op jit(solution)/shard_map/forward_attention/pallas_call | solution.py:117
  19.8 1.5 %collective-permute-start.2 = (bf16[128,1152]{1,0:T(8,128)(2,1)S(1)}, bf16[128,1152]{1,0:T(8,128)(2,1)}, u32[]{:S(2)}, u32[]{:S(2)}) collective-permute-start(bf16[128,1152]{1,0:T(8,128)(2,1)S(1)} %collective-permute-done.micro_ref.refs_0_), channel_id=1, source_target_pairs={{0,2},{1,3},{2,0},{3,1},{4,6},{5,7},{6,4},{7,5},{8,10},{9,11},{10,... | collective-permute-start | bytes 884744 | tf_op jit(solution)/shard_map/ppermute | solution.py:55
  21.3 6.8 %stored_attention.1 = (bf16[1024,512]{1,0:T(8,128)(2,1)S(1)}, bf16[2,4,512,512]{3,2,1,0:T(8,128)(2,1)}) custom-call(s32[4,4]{1,0:T(4,128)S(1)} %copy-done.5, bf16[128,1152]{1,0:T(8,128)(2,1)S(1)} %collective-permute-done.micro_ref.refs_0_, bf16[512,1024]{1,0:T(8,128)(2,1)} %bitcast.21, bf16[2,512,256]{2,1,0:T(8,128)(2,1)} %bitcast.23), custom_call_target="tpu_custom_call" | custom-call | flops 1000 | bytes 1000 | tf_op jit(solution)/shard_map/stored_attention/pallas_call | solution.py:156
  29.3 2.2 %collective-permute-done.3.refs_0_ = bf16[128,1536]{1,0:T(8,128)(2,1)S(1)} collective-permute-done((bf16[128,1536]{1,0:T(8,128)(2,1)S(1)}, bf16[128,1536]{1,0:T(8,128)(2,1)S(1)}, u32[]{:S(2)}, u32[]{:S(2)}) %collective-permute-start.3) | collective-permute-done | bytes 393248 | tf_op jit(solution)/shard_map/ppermute | solution.py:45
  31.5 1.5 %collective-permute-start.9 = (bf16[128,1536]{1,0:T(8,128)(2,1)S(1)}, bf16[128,1536]{1,0:T(8,128)(2,1)S(1)}, u32[]{:S(2)}, u32[]{:S(2)}) collective-permute-start(bf16[128,1536]{1,0:T(8,128)(2,1)S(1)} %collective-permute-done.3.refs_0_), channel_id=1, source_target_pairs={{0,2},{1,3},{2,0},{3,1},{4,6},{5,7},{6,4},{7,5},{8,10},{9,11},{10,... | collective-permute-start | bytes 1179656 | tf_op jit(solution)/shard_map/ppermute | solution.py:55
  33.4 3.4 %copy-done = bf16[1,1024,4096]{2,1,0:T(8,128)(2,1)S(1)} copy-done((bf16[1,1024,4096]{2,1,0:T(8,128)(2,1)S(1)}, bf16[1,1024,4096]{2,1,0:T(8,128)(2,1)}, u32[]{:S(2)}) %copy-start) | copy-done | bytes 8388632
  36.8 4.7 %grad_products.3 = (f32[512,1024]{1,0:T(8,128)S(1)}, bf16[1024,4096]{1,0:T(8,128)(2,1)}) custom-call(s32[4]{0:T(128)S(1)} %pad_add_fusion.sources_ref, bf16[128,1152]{1,0:T(8,128)(2,1)S(1)} %collective-permute-done.micro_ref.refs_0_, bf16[128,1152]{1,0:T(8,128)(2,1)} %collective-permute-done.1.refs_1_, bf16[128,1152]{1,0:T(8,128)(2,1)} %collective-permute-done.2.refs_2_, ...), custom_call_target="tpu_custom_call" | custom-call | flops 1000 | bytes 1000 | tf_op jit(solution)/shard_map/grad_products/pallas_call | solution.py:271
  41.5 2.0 %collective-permute-done.7.attn_ref = bf16[4,48,1024]{2,1,0:T(8,128)(2,1)S(1)} collective-permute-done((bf16[4,48,1024]{2,1,0:T(8,128)(2,1)}, bf16[4,48,1024]{2,1,0:T(8,128)(2,1)S(1)}, u32[]{:S(2)}, u32[]{:S(2)}) %collective-permute-start.7) | collective-permute-done | bytes 393248 | tf_op jit(solution)/shard_map/ppermute | solution.py:45
  43.5 1.8 %project.2 = (bf16[1,48,2048]{2,1,0:T(8,128)(2,1)S(1)}, bf16[1,48,2048]{2,1,0:T(8,128)(2,1)S(1)}, bf16[48,4096]{1,0:T(8,128)(2,1)S(1)}, bf16[2,48,4096]{2,1,0:T(8,128)(2,1)S(1)}) custom-call(s32[1]{0:T(128)} %bitcast.1.place_ref, bf16[4,48,1024]{2,1,0:T(8,128)(2,1)S(1)} %collective-permute-done.7.attn_ref, bf16[1024,4096]{1,0:T(8,128)(2,1)S(1)} %bitcast.17), custom_call_target="tpu_custom_call" | custom-call | flops 1000 | bytes 1000 | tf_op jit(solution)/shard_map/project/pallas_call | solution.py:319
  46.0 2.0 %collective-permute-done.9.refs_2_ = bf16[128,1536]{1,0:T(8,128)(2,1)S(1)} collective-permute-done((bf16[128,1536]{1,0:T(8,128)(2,1)S(1)}, bf16[128,1536]{1,0:T(8,128)(2,1)S(1)}, u32[]{:S(2)}, u32[]{:S(2)}) %collective-permute-start.9) | collective-permute-done | bytes 393248 | tf_op jit(solution)/shard_map/ppermute | solution.py:55
  50.4 5.1 %grad_products.4 = (f32[512,1024]{1,0:T(8,128)S(1)}, bf16[1024,4096]{1,0:T(8,128)(2,1)}) custom-call(s32[4]{0:T(128)S(1)} %pad_add_fusion.sources_ref, bf16[128,1536]{1,0:T(8,128)(2,1)S(1)} %collective-permute-done.4.refs_0_, bf16[128,1536]{1,0:T(8,128)(2,1)S(1)} %collective-permute-done.12.refs_1_, ...), custom_call_target="tpu_custom_call", output_to_operand_aliasing={{1}: (8, {})} | custom-call | flops 1000 | bytes 1000 | tf_op jit(solution)/shard_map/grad_products/pallas_call | solution.py:271
  55.5 2.0 %collective-permute-done.16.attn_ref = bf16[4,80,1024]{2,1,0:T(8,128)(2,1)S(1)} collective-permute-done((bf16[4,80,1024]{2,1,0:T(8,128)(2,1)}, bf16[4,80,1024]{2,1,0:T(8,128)(2,1)S(1)}, u32[]{:S(2)}, u32[]{:S(2)}) %collective-permute-start.16) | collective-permute-done | bytes 655392 | tf_op jit(solution)/shard_map/ppermute | solution.py:45
  57.6 2.9 %project.3 = (bf16[1,80,2048]{2,1,0:T(8,128)(2,1)S(1)}, bf16[1,80,2048]{2,1,0:T(8,128)(2,1)S(1)}, bf16[80,4096]{1,0:T(8,128)(2,1)S(1)}, bf16[2,80,4096]{2,1,0:T(8,128)(2,1)S(1)}) custom-call(s32[1]{0:T(128)} %bitcast.1.place_ref, bf16[4,80,1024]{2,1,0:T(8,128)(2,1)S(1)} %collective-permute-done.16.attn_ref, bf16[1024,4096]{1,0:T(8,128)(2,1)S(1)} %bitcast.19), custom_call_target="tpu_custom_call" | custom-call | flops 1000 | bytes 1000 | tf_op jit(solution)/shard_map/project/pallas_call | solution.py:319
  61.1 1.0 %collective-permute-done.19.refs_0_ = bf16[1,80,2048]{2,1,0:T(8,128)(2,1)S(1)} collective-permute-done((bf16[1,80,2048]{2,1,0:T(8,128)(2,1)S(1)}, bf16[1,80,2048]{2,1,0:T(8,128)(2,1)S(1)}, u32[]{:S(2)}, u32[]{:S(2)}) %collective-permute-start.19) | collective-permute-done | bytes 327712 | tf_op jit(solution)/shard_map/ppermute | solution.py:50
  62.8 1.5 %collective-permute-start.22 = (bf16[80,4096]{1,0:T(8,128)(2,1)S(1)}, bf16[80,4096]{1,0:T(8,128)(2,1)S(1)}, u32[]{:S(2)}, u32[]{:S(2)}) collective-permute-start(bf16[80,4096]{1,0:T(8,128)(2,1)S(1)} %pair_sum.3), channel_id=1, source_target_pairs={{0,2},{1,3},{2,0},{3,1},{4,6},{5,7},{6,4},{7,5},{8,10},{9,11},{10,... | collective-permute-start | bytes 1966088 | tf_op jit(solution)/shard_map/ppermute | solution.py:55
  64.3 1.7 %collective-permute-done.21.refs_3_ = bf16[128,1536]{1,0:T(8,128)(2,1)S(1)} collective-permute-done((bf16[128,1536]{1,0:T(8,128)(2,1)S(1)}, bf16[128,1536]{1,0:T(8,128)(2,1)S(1)}, u32[]{:S(2)}, u32[]{:S(2)}) %collective-permute-start.21) | collective-permute-done | bytes 393248 | tf_op jit(solution)/shard_map/ppermute | solution.py:50
  66.1 5.1 %grad_products.5 = (bf16[512,1024]{1,0:T(8,128)(2,1)S(1)}, bf16[1024,4096]{1,0:T(8,128)(2,1)}) custom-call(s32[4]{0:T(128)S(1)} %pad_add_fusion.sources_ref, bf16[128,1536]{1,0:T(8,128)(2,1)S(1)} %collective-permute-done.3.refs_0_, bf16[128,1536]{1,0:T(8,128)(2,1)S(1)} %collective-permute-done.15.refs_1_, ...), custom_call_target="tpu_custom_call", output_to_operand_aliasing={{1}: (8, {})} | custom-call | flops 1000 | bytes 1000 | tf_op jit(solution)/shard_map/grad_products/pallas_call | solution.py:271
  71.2 5.9 %backward_attention.1 = (bf16[512,1024]{1,0:T(8,128)(2,1)}, bf16[2,512,256]{2,1,0:T(8,128)(2,1)}) custom-call(bf16[512,1024]{1,0:T(8,128)(2,1)S(1)} %bitcast.22, bf16[2,512,256]{2,1,0:T(8,128)(2,1)S(1)} %bitcast.24, bf16[512,1024]{1,0:T(8,128)(2,1)S(1)} %get-tuple-element.76.grad_ref, bf16[2,4,512,512]{3,2,1,0:T(8,128)(2,1)S(1)} %copy-done.2), custom_call_target="tpu_custom_call" | custom-call | flops 1000 | bytes 1000 | tf_op jit(solution)/shard_map/backward_attention/pallas_call | solution.py:208
  77.1 2.2 %collective-permute-done.8.resid_ref = bf16[128,4096]{1,0:T(8,128)(2,1)S(1)} collective-permute-done((bf16[128,4096]{1,0:T(8,128)(2,1)S(1)}, bf16[128,4096]{1,0:T(8,128)(2,1)S(1)}, u32[]{:S(2)}, u32[]{:S(2)}) %collective-permute-start.8) | collective-permute-done | bytes 1048608 | tf_op jit(solution)/shard_map/ppermute | solution.py:45
  79.6 1.2 %finish.1 = bf16[128,4096]{1,0:T(8,128)(2,1)} custom-call(bf16[128,4096]{1,0:T(8,128)(2,1)S(1)} %collective-permute-done.8.resid_ref, bf16[2,48,4096]{2,1,0:T(8,128)(2,1)S(1)} %get-tuple-element.54.keep_ref.refs_0_, bf16[48,4096]{1,0:T(8,128)(2,1)S(1)} %collective-permute-done.14.refs_1_, bf16[48,4096]{1,0:T(8,128)(2,1)S(1)} %collective-permute-done.18.refs_2_, ...), custom_call_target="tpu_custom_call" | custom-call | flops 1000 | bytes 1000 | tf_op jit(solution)/shard_map/finish/pallas_call | solution.py:397
  (52 shorter events, 8.3 us)
Async XLA Ops:
  2.3 17.5 %collective-permute-start = (bf16[128,1152]{1,0:T(8,128)(2,1)S(1)}, bf16[128,1152]{1,0:T(8,128)(2,1)S(1)}, u32[]{:S(2)}, u32[]{:S(2)}) collective-permute-start(bf16[128,1152]{1,0:T(8,128)(2,1)S(1)} %slice_select_fusion), channel_id=1, source_target_pairs={{0,28},{4,0},{8,4},{12,8},{16,12},{20,16},{24,20},{28,24},{1,29},{... | collective-permute-start | bytes 884744 | tf_op jit(solution)/shard_map/ppermute | solution.py:45
  9.5 18.6 %collective-permute-start.4 = (bf16[128,1536]{1,0:T(8,128)(2,1)S(1)}, bf16[128,1536]{1,0:T(8,128)(2,1)S(1)}, u32[]{:S(2)}, u32[]{:S(2)}) collective-permute-start(bf16[128,1536]{1,0:T(8,128)(2,1)S(1)} %get-tuple-element.82), channel_id=1, source_target_pairs={{0,28},{4,0},{8,4},{12,8},{16,12},{20,16},{24,20},{28,24},{1,29},{... | collective-permute-start | bytes 1179656 | tf_op jit(solution)/shard_map/ppermute | solution.py:45
  10.1 21.4 %collective-permute-start.3 = (bf16[128,1536]{1,0:T(8,128)(2,1)S(1)}, bf16[128,1536]{1,0:T(8,128)(2,1)S(1)}, u32[]{:S(2)}, u32[]{:S(2)}) collective-permute-start(bf16[128,1536]{1,0:T(8,128)(2,1)S(1)} %get-tuple-element.83), channel_id=1, source_target_pairs={{0,28},{4,0},{8,4},{12,8},{16,12},{20,16},{24,20},{28,24},{1,29},{... | collective-permute-start | bytes 1179656 | tf_op jit(solution)/shard_map/ppermute | solution.py:45
  19.8 11.6 %collective-permute-start.2 = (bf16[128,1152]{1,0:T(8,128)(2,1)S(1)}, bf16[128,1152]{1,0:T(8,128)(2,1)}, u32[]{:S(2)}, u32[]{:S(2)}) collective-permute-start(bf16[128,1152]{1,0:T(8,128)(2,1)S(1)} %collective-permute-done.micro_ref.refs_0_), channel_id=1, source_target_pairs={{0,2},{1,3},{2,0},{3,1},{4,6},{5,7},{6,4},{7,5},{8,10},{9,11},{10,... | collective-permute-start | bytes 884744 | tf_op jit(solution)/shard_map/ppermute | solution.py:55
  21.3 11.7 %collective-permute-start.1 = (bf16[128,1152]{1,0:T(8,128)(2,1)S(1)}, bf16[128,1152]{1,0:T(8,128)(2,1)}, u32[]{:S(2)}, u32[]{:S(2)}) collective-permute-start(bf16[128,1152]{1,0:T(8,128)(2,1)S(1)} %collective-permute-done.micro_ref.refs_0_), channel_id=1, source_target_pairs={{0,1},{1,0},{2,3},{3,2},{4,5},{5,4},{6,7},{7,6},{8,9},{9,8},{10,11... | collective-permute-start | bytes 884744 | tf_op jit(solution)/shard_map/ppermute | solution.py:50
  28.1 13.4 %collective-permute-start.6 = (bf16[128,1536]{1,0:T(8,128)(2,1)S(1)}, bf16[128,1536]{1,0:T(8,128)(2,1)S(1)}, u32[]{:S(2)}, u32[]{:S(2)}) collective-permute-start(bf16[128,1536]{1,0:T(8,128)(2,1)S(1)} %collective-permute-done.4.refs_0_), channel_id=1, source_target_pairs={{0,2},{1,3},{2,0},{3,1},{4,6},{5,7},{6,4},{7,5},{8,10},{9,11},{10,... | collective-permute-start | bytes 1179656 | tf_op jit(solution)/shard_map/ppermute | solution.py:55
  28.7 14.9 %collective-permute-start.7 = (bf16[4,48,1024]{2,1,0:T(8,128)(2,1)}, bf16[4,48,1024]{2,1,0:T(8,128)(2,1)S(1)}, u32[]{:S(2)}, u32[]{:S(2)}) collective-permute-start(bf16[4,48,1024]{2,1,0:T(8,128)(2,1)} %get-tuple-element.53), channel_id=1, source_target_pairs={{0,4},{4,8},{8,12},{12,16},{16,20},{20,24},{24,28},{28,0},{1,5},{5... | collective-permute-start | bytes 1179656 | tf_op jit(solution)/shard_map/ppermute | solution.py:45
  31.5 1.9 %collective-permute-start.5 = (bf16[128,1152]{1,0:T(8,128)(2,1)}, bf16[128,1152]{1,0:T(8,128)(2,1)}, u32[]{:S(2)}, u32[]{:S(2)}) collective-permute-start(bf16[128,1152]{1,0:T(8,128)(2,1)} %collective-permute-done.2.refs_2_), channel_id=1, source_target_pairs={{0,1},{1,0},{2,3},{3,2},{4,5},{5,4},{6,7},{7,6},{8,9},{9,8},{10,11... | collective-permute-start | bytes 884744 | tf_op jit(solution)/shard_map/ppermute | solution.py:50
  31.5 16.6 %collective-permute-start.9 = (bf16[128,1536]{1,0:T(8,128)(2,1)S(1)}, bf16[128,1536]{1,0:T(8,128)(2,1)S(1)}, u32[]{:S(2)}, u32[]{:S(2)}) collective-permute-start(bf16[128,1536]{1,0:T(8,128)(2,1)S(1)} %collective-permute-done.3.refs_0_), channel_id=1, source_target_pairs={{0,2},{1,3},{2,0},{3,1},{4,6},{5,7},{6,4},{7,5},{8,10},{9,11},{10,... | collective-permute-start | bytes 1179656 | tf_op jit(solution)/shard_map/ppermute | solution.py:55
  33.0 24.6 %collective-permute-start.16 = (bf16[4,80,1024]{2,1,0:T(8,128)(2,1)}, bf16[4,80,1024]{2,1,0:T(8,128)(2,1)S(1)}, u32[]{:S(2)}, u32[]{:S(2)}) collective-permute-start(bf16[4,80,1024]{2,1,0:T(8,128)(2,1)} %copy-done.6), channel_id=1, source_target_pairs={{0,4},{4,8},{8,12},{12,16},{16,20},{20,24},{24,28},{28,0},{1,5},{5... | collective-permute-start | bytes 1966088 | tf_op jit(solution)/shard_map/ppermute | solution.py:45
  36.8 13.0 %copy-start.7 = (bf16[1,128,4096]{2,1,0:T(8,128)(2,1)S(1)}, bf16[1,128,4096]{2,1,0:T(8,128)(2,1)}, u32[]{:S(2)}) copy-start(bf16[1,128,4096]{2,1,0:T(8,128)(2,1)} %param.10) | copy-start | bytes 3145732
  45.4 2.7 %collective-permute-start.10 = (bf16[1,48,2048]{2,1,0:T(8,128)(2,1)S(1)}, bf16[1,48,2048]{2,1,0:T(8,128)(2,1)S(1)}, u32[]{:S(2)}, u32[]{:S(2)}) collective-permute-start(bf16[1,48,2048]{2,1,0:T(8,128)(2,1)S(1)} %get-tuple-element.57), channel_id=1, source_target_pairs={{0,1},{1,0},{2,3},{3,2},{4,5},{5,4},{6,7},{7,6},{8,9},{9,8},{10,11... | collective-permute-start | bytes 589832 | tf_op jit(solution)/shard_map/ppermute | solution.py:50
  45.5 3.1 %collective-permute-start.11 = (bf16[1,48,2048]{2,1,0:T(8,128)(2,1)S(1)}, bf16[1,48,2048]{2,1,0:T(8,128)(2,1)S(1)}, u32[]{:S(2)}, u32[]{:S(2)}) collective-permute-start(bf16[1,48,2048]{2,1,0:T(8,128)(2,1)S(1)} %get-tuple-element.58), channel_id=1, source_target_pairs={{0,1},{1,0},{2,3},{3,2},{4,5},{5,4},{6,7},{7,6},{8,9},{9,8},{10,11... | collective-permute-start | bytes 589832 | tf_op jit(solution)/shard_map/ppermute | solution.py:50
  45.9 2.8 %collective-permute-start.12 = (bf16[128,1536]{1,0:T(8,128)(2,1)S(1)}, bf16[128,1536]{1,0:T(8,128)(2,1)S(1)}, u32[]{:S(2)}, u32[]{:S(2)}) collective-permute-start(bf16[128,1536]{1,0:T(8,128)(2,1)S(1)} %collective-permute-done.4.refs_0_), channel_id=1, source_target_pairs={{0,1},{1,0},{2,3},{3,2},{4,5},{5,4},{6,7},{7,6},{8,9},{9,8},{10,11... | collective-permute-start | bytes 1179656 | tf_op jit(solution)/shard_map/ppermute | solution.py:50
  48.1 1.7 %collective-permute-start.13 = (bf16[128,1536]{1,0:T(8,128)(2,1)S(1)}, bf16[128,1536]{1,0:T(8,128)(2,1)S(1)}, u32[]{:S(2)}, u32[]{:S(2)}) collective-permute-start(bf16[128,1536]{1,0:T(8,128)(2,1)S(1)} %collective-permute-done.6.refs_2_), channel_id=1, source_target_pairs={{0,1},{1,0},{2,3},{3,2},{4,5},{5,4},{6,7},{7,6},{8,9},{9,8},{10,11... | collective-permute-start | bytes 1179656 | tf_op jit(solution)/shard_map/ppermute | solution.py:50
  48.1 7.4 %collective-permute-start.15 = (bf16[128,1536]{1,0:T(8,128)(2,1)S(1)}, bf16[128,1536]{1,0:T(8,128)(2,1)S(1)}, u32[]{:S(2)}, u32[]{:S(2)}) collective-permute-start(bf16[128,1536]{1,0:T(8,128)(2,1)S(1)} %collective-permute-done.3.refs_0_), channel_id=1, source_target_pairs={{0,1},{1,0},{2,3},{3,2},{4,5},{5,4},{6,7},{7,6},{8,9},{9,8},{10,11... | collective-permute-start | bytes 1179656 | tf_op jit(solution)/shard_map/ppermute | solution.py:50
  48.6 6.9 %collective-permute-start.14 = (bf16[48,4096]{1,0:T(8,128)(2,1)S(1)}, bf16[48,4096]{1,0:T(8,128)(2,1)S(1)}, u32[]{:S(2)}, u32[]{:S(2)}) collective-permute-start(bf16[48,4096]{1,0:T(8,128)(2,1)S(1)} %get-tuple-element.63), channel_id=1, source_target_pairs={{0,1},{1,0},{2,3},{3,2},{4,5},{5,4},{6,7},{7,6},{8,9},{9,8},{10,11... | collective-permute-start | bytes 1179656 | tf_op jit(solution)/shard_map/ppermute | solution.py:50
  48.8 12.4 %collective-permute-start.18 = (bf16[48,4096]{1,0:T(8,128)(2,1)S(1)}, bf16[48,4096]{1,0:T(8,128)(2,1)S(1)}, u32[]{:S(2)}, u32[]{:S(2)}) collective-permute-start(bf16[48,4096]{1,0:T(8,128)(2,1)S(1)} %pair_sum.2), channel_id=1, source_target_pairs={{0,2},{1,3},{2,0},{3,1},{4,6},{5,7},{6,4},{7,5},{8,10},{9,11},{10,... | collective-permute-start | bytes 1179656 | tf_op jit(solution)/shard_map/ppermute | solution.py:55
  49.8 29.5 %collective-permute-start.8 = (bf16[128,4096]{1,0:T(8,128)(2,1)S(1)}, bf16[128,4096]{1,0:T(8,128)(2,1)S(1)}, u32[]{:S(2)}, u32[]{:S(2)}) collective-permute-start(bf16[128,4096]{1,0:T(8,128)(2,1)S(1)} %bitcast.31), channel_id=1, source_target_pairs={{0,4},{4,8},{8,12},{12,16},{16,20},{20,24},{24,28},{28,0},{1,5},{5... | collective-permute-start | bytes 3145736 | tf_op jit(solution)/shard_map/ppermute | solution.py:45
  60.5 1.7 %collective-permute-start.19 = (bf16[1,80,2048]{2,1,0:T(8,128)(2,1)S(1)}, bf16[1,80,2048]{2,1,0:T(8,128)(2,1)S(1)}, u32[]{:S(2)}, u32[]{:S(2)}) collective-permute-start(bf16[1,80,2048]{2,1,0:T(8,128)(2,1)S(1)} %get-tuple-element.71), channel_id=1, source_target_pairs={{0,1},{1,0},{2,3},{3,2},{4,5},{5,4},{6,7},{7,6},{8,9},{9,8},{10,11... | collective-permute-start | bytes 983048 | tf_op jit(solution)/shard_map/ppermute | solution.py:50
  60.6 2.1 %collective-permute-start.20 = (bf16[1,80,2048]{2,1,0:T(8,128)(2,1)S(1)}, bf16[1,80,2048]{2,1,0:T(8,128)(2,1)S(1)}, u32[]{:S(2)}, u32[]{:S(2)}) collective-permute-start(bf16[1,80,2048]{2,1,0:T(8,128)(2,1)S(1)} %get-tuple-element.72), channel_id=1, source_target_pairs={{0,1},{1,0},{2,3},{3,2},{4,5},{5,4},{6,7},{7,6},{8,9},{9,8},{10,11... | collective-permute-start | bytes 983048 | tf_op jit(solution)/shard_map/ppermute | solution.py:50
  61.1 10.1 %collective-permute-start.17 = (bf16[80,4096]{1,0:T(8,128)(2,1)S(1)}, bf16[80,4096]{1,0:T(8,128)(2,1)S(1)}, u32[]{:S(2)}, u32[]{:S(2)}) collective-permute-start(bf16[80,4096]{1,0:T(8,128)(2,1)S(1)} %get-tuple-element.67), channel_id=1, source_target_pairs={{0,1},{1,0},{2,3},{3,2},{4,5},{5,4},{6,7},{7,6},{8,9},{9,8},{10,11... | collective-permute-start | bytes 1966088 | tf_op jit(solution)/shard_map/ppermute | solution.py:50
  62.8 16.8 %collective-permute-start.22 = (bf16[80,4096]{1,0:T(8,128)(2,1)S(1)}, bf16[80,4096]{1,0:T(8,128)(2,1)S(1)}, u32[]{:S(2)}, u32[]{:S(2)}) collective-permute-start(bf16[80,4096]{1,0:T(8,128)(2,1)S(1)} %pair_sum.3), channel_id=1, source_target_pairs={{0,2},{1,3},{2,0},{3,1},{4,6},{5,7},{6,4},{7,5},{8,10},{9,11},{10,... | collective-permute-start | bytes 1966088 | tf_op jit(solution)/shard_map/ppermute | solution.py:55
  64.3 1.7 %collective-permute-start.21 = (bf16[128,1536]{1,0:T(8,128)(2,1)S(1)}, bf16[128,1536]{1,0:T(8,128)(2,1)S(1)}, u32[]{:S(2)}, u32[]{:S(2)}) collective-permute-start(bf16[128,1536]{1,0:T(8,128)(2,1)S(1)} %collective-permute-done.9.refs_2_), channel_id=1, source_target_pairs={{0,1},{1,0},{2,3},{3,2},{4,5},{5,4},{6,7},{7,6},{8,9},{9,8},{10,11... | collective-permute-start | bytes 1179656 | tf_op jit(solution)/shard_map/ppermute | solution.py:50
  (7 other events, 27.0 us)

commit v5 on v4

--- a/solution.py
+++ b/solution.py
@@ -85,6 +85,18 @@
     shifted = jnp.exp(scores - jnp.max(scores, axis=2, keepdims=True))
     probs = shifted * (1.0 / jnp.sum(shifted, axis=2, keepdims=True))
     return probs.astype(BF16).reshape(heads * BLOCK, extent)
+
+
+def in_turn(count, begin, middle, end):
+    started = begin(0)
+    waiting = None
+    for index in range(count):
+        following = begin(index + 1) if index + 1 < count else None
+        worked = middle(index, started)
+        if waiting is not None:
+            end(index - 1, waiting)
+        waiting, started = worked, following
+    end(count - 1, waiting)
 
 
 def forward_kernel(starts_ref, micro_ref, query_ref, keyval_ref, *out_refs):
@@ -181,20 +193,30 @@
     heads = width // HD
     dk[...] = jnp.zeros_like(dk)
     dv[...] = jnp.zeros_like(dv)
-    for index, first in enumerate(range(0, rows, BLOCK)):
+
+    def shares(index):
+        first = index * BLOCK
+        grad = stack_heads(grad_ref, first, heads)
+        return grad, dot(grad, keyval_ref[1, : first + BLOCK], NT)
+
+    def center(index, value):
+        grad, dprobs = value
+        probs = probs_ref[0, index, :, : (index + 1) * BLOCK]
+        wide = probs.astype(F32)
+        mean = jnp.sum(wide * dprobs, axis=1, keepdims=True)
+        return grad, (wide * (dprobs - mean) * (1.0 / math.sqrt(HD))).astype(BF16)
+
+    def collect(index, value):
+        first = index * BLOCK
         extent = first + BLOCK
-        query = stack_heads(query_ref, first, heads)
-        grad = stack_heads(grad_ref, first, heads)
-        probs = probs_ref[0, index, :, :extent]
-        wide = probs.astype(F32)
-        dprobs = dot(grad, keyval_ref[1, :extent], NT)
-        center = jnp.sum(wide * dprobs, axis=1, keepdims=True)
-        dscores = (wide * (dprobs - center) * (1.0 / math.sqrt(HD))).astype(BF16)
+        grad, dscores = value
         dquery = dot(dscores, keyval_ref[0, :extent], NN).astype(BF16)
         for h in range(heads):
             dquery_ref[first:extent, h * HD : (h + 1) * HD] = dquery[h * BLOCK : (h + 1) * BLOCK]
-        dk[:extent] += dot(dscores, query, TN)
-        dv[:extent] += dot(probs, grad, TN)
+        dk[:extent] += dot(dscores, stack_heads(query_ref, first, heads), TN)
+        dv[:extent] += dot(probs_ref[0, index, :, :extent], grad, TN)
+
+    in_turn(rows // BLOCK, shares, center, collect)
     dkeyval_ref[0] = dk[...].astype(BF16)
     dkeyval_ref[1] = dv[...].astype(BF16)
 

time: 81.3 us -> 81.3 us (level)
  waiting for transfers between devices: 14.5 us -> 15.4 us
  Pallas kernels: 40 us -> 39.1 us
    ppermute x6, waiting for transfers between devices: 8.45 us -> 9.37 us  [along_pipe(): lax.ppermute(value, 'pipe', [(i, (i + steps) % count) for i in range(coun...]
    pallas_call x1, Pallas kernels: 5.94 us -> 5.02 us  [backward_attention(): pl.pallas_call(backward_kernel, grid=(groups,), in_specs=[wide, narrow, w...]
  transfers between devices with their start and end apart: 23 -> 23, of which waited for: 10 -> 10; matrix products, arithmetic and copies ran while one was open for 2% -> 2% of each run, Pallas kernels for 48% -> 47%
where the time goes in v5:
time: 81.3 us; the launch traced here: 81 us
  Pallas kernels  39.1 us (48%)
  starting transfers between devices  17.2 us (21%)
  waiting for transfers between devices  15.4 us (19%)
  local copies, waits for them, and re-layouts  6.08 us (7%)
  between operations  2.26 us (3%)
  other arithmetic  1.08 us (1%)
    pallas_call x3, Pallas kernels, grad_products(): pl.pallas_call(functools.partial(grad_kernel, len(pieces), first, earlier...  14.9 us
    ppermute x6, starting transfers between devices, along_pipe(): lax.ppermute(value, 'pipe', [(i, (i + steps) % count) for i in range(coun...  9.6 us
    ppermute x6, waiting for transfers between devices, along_pipe(): lax.ppermute(value, 'pipe', [(i, (i + steps) % count) for i in range(coun...  9.37 us
    pallas_call x1, Pallas kernels, stored_attention(): pl.pallas_call(stored_kernel, grid=(groups,), in_specs=[SMEM, pl.BlockSpe...  6.8 us
    pallas_call x1, Pallas kernels, forward_attention(): pl.pallas_call(forward_kernel, grid=(groups,), in_specs=[SMEM, SMEM, pl.B...  6.17 us
    ppermute x5, starting transfers between devices, along_chips(): lax.ppermute(value, 'tp', [(i, (i + 2 * steps) % count) for i in range(co...  5.68 us
    pallas_call x1, Pallas kernels, backward_attention(): pl.pallas_call(backward_kernel, grid=(groups,), in_specs=[wide, narrow, w...  5.02 us
    unnamed x16, local copies, waits for them, and re-layouts  4.91 us
  transfers between devices with their start and end apart: 23, of which 10 were waited for; matrix products, arithmetic and copies ran while one was open for 2% of the time, Pallas kernels for 47%

profile of v5, /device:TPU:0, one launch (start us, length us, event | category | flops | bytes accessed | tf_op | source)
XLA Modules:
  0.0 81.0 jit_solution(8563906132092472002)
XLA Ops:
  1.3 1.0 %slice_select_fusion = bf16[128,1152]{1,0:T(8,128)(2,1)S(1)} fusion(bf16[128,4096]{1,0:T(8,128)(2,1)} %bitcast.26, pred[1152]{0:T(1024)(128)(4,1)} %constant.28.clone.1, bf16[]{:T(256)} %bitcast.6), kind=kLoop, calls=%fused_computation | loop fusion | flops 147456 | bytes 590978 | tf_op jit(solution)/shard_map/concatenate | solution.py:467
  2.3 6.1 %collective-permute-start = (bf16[128,1152]{1,0:T(8,128)(2,1)S(1)}, bf16[128,1152]{1,0:T(8,128)(2,1)S(1)}, u32[]{:S(2)}, u32[]{:S(2)}) collective-permute-start(bf16[128,1152]{1,0:T(8,128)(2,1)S(1)} %slice_select_fusion), channel_id=1, source_target_pairs={{0,28},{4,0},{8,4},{12,8},{16,12},{20,16},{24,20},{28,24},{1,29},{... | collective-permute-start | bytes 884744 | tf_op jit(solution)/shard_map/ppermute | solution.py:45
  8.3 1.2 %fusion = (bf16[128,1536]{1,0:T(8,128)(2,1)S(1)}, bf16[128,1536]{1,0:T(8,128)(2,1)S(1)}) fusion(bf16[128,4096]{1,0:T(8,128)(2,1)} %bitcast.27), kind=kLoop, calls=%fused_computation.2 | loop fusion | bytes 1572864 | tf_op jit(solution)/shard_map/slice | solution.py:476
  10.1 1.4 %collective-permute-start.3 = (bf16[128,1536]{1,0:T(8,128)(2,1)S(1)}, bf16[128,1536]{1,0:T(8,128)(2,1)S(1)}, u32[]{:S(2)}, u32[]{:S(2)}) collective-permute-start(bf16[128,1536]{1,0:T(8,128)(2,1)S(1)} %get-tuple-element.83), channel_id=1, source_target_pairs={{0,28},{4,0},{8,4},{12,8},{16,12},{20,16},{24,20},{28,24},{1,29},{... | collective-permute-start | bytes 1179656 | tf_op jit(solution)/shard_map/ppermute | solution.py:45
  12.8 6.2 %forward_attention.1 = (bf16[4,48,1024]{2,1,0:T(8,128)(2,1)}, bf16[4,80,1024]{2,1,0:T(8,128)(2,1)S(1)}) custom-call(s32[4,4]{1,0:T(4,128)S(1)} %copy-done.5, s32[1]{0:T(128)S(6)} %copy.18.micro_ref, bf16[512,1024]{1,0:T(8,128)(2,1)} %bitcast.28, bf16[2,512,256]{2,1,0:T(8,128)(2,1)} %bitcast.30), custom_call_target="tpu_custom_call" | custom-call | flops 1000 | bytes 1000 | tf_op jit(solution)/shard_map/forward_attention/pallas_call | solution.py:129
  19.8 1.5 %collective-permute-start.2 = (bf16[128,1152]{1,0:T(8,128)(2,1)S(1)}, bf16[128,1152]{1,0:T(8,128)(2,1)}, u32[]{:S(2)}, u32[]{:S(2)}) collective-permute-start(bf16[128,1152]{1,0:T(8,128)(2,1)S(1)} %collective-permute-done.micro_ref.refs_0_), channel_id=1, source_target_pairs={{0,2},{1,3},{2,0},{3,1},{4,6},{5,7},{6,4},{7,5},{8,10},{9,11},{10,... | collective-permute-start | bytes 884744 | tf_op jit(solution)/shard_map/ppermute | solution.py:55
  21.3 6.8 %stored_attention.1 = (bf16[1024,512]{1,0:T(8,128)(2,1)S(1)}, bf16[2,4,512,512]{3,2,1,0:T(8,128)(2,1)}) custom-call(s32[4,4]{1,0:T(4,128)S(1)} %copy-done.5, bf16[128,1152]{1,0:T(8,128)(2,1)S(1)} %collective-permute-done.micro_ref.refs_0_, bf16[512,1024]{1,0:T(8,128)(2,1)} %bitcast.21, bf16[2,512,256]{2,1,0:T(8,128)(2,1)} %bitcast.23), custom_call_target="tpu_custom_call" | custom-call | flops 1000 | bytes 1000 | tf_op jit(solution)/shard_map/stored_attention/pallas_call | solution.py:168
  29.3 2.2 %collective-permute-done.3.refs_0_ = bf16[128,1536]{1,0:T(8,128)(2,1)S(1)} collective-permute-done((bf16[128,1536]{1,0:T(8,128)(2,1)S(1)}, bf16[128,1536]{1,0:T(8,128)(2,1)S(1)}, u32[]{:S(2)}, u32[]{:S(2)}) %collective-permute-start.3) | collective-permute-done | bytes 393248 | tf_op jit(solution)/shard_map/ppermute | solution.py:45
  31.5 1.5 %collective-permute-start.9 = (bf16[128,1536]{1,0:T(8,128)(2,1)S(1)}, bf16[128,1536]{1,0:T(8,128)(2,1)S(1)}, u32[]{:S(2)}, u32[]{:S(2)}) collective-permute-start(bf16[128,1536]{1,0:T(8,128)(2,1)S(1)} %collective-permute-done.3.refs_0_), channel_id=1, source_target_pairs={{0,2},{1,3},{2,0},{3,1},{4,6},{5,7},{6,4},{7,5},{8,10},{9,11},{10,... | collective-permute-start | bytes 1179656 | tf_op jit(solution)/shard_map/ppermute | solution.py:55
  33.4 3.4 %copy-done = bf16[1,1024,4096]{2,1,0:T(8,128)(2,1)S(1)} copy-done((bf16[1,1024,4096]{2,1,0:T(8,128)(2,1)S(1)}, bf16[1,1024,4096]{2,1,0:T(8,128)(2,1)}, u32[]{:S(2)}) %copy-start) | copy-done | bytes 8388632
  36.8 4.7 %grad_products.3 = (f32[512,1024]{1,0:T(8,128)S(1)}, bf16[1024,4096]{1,0:T(8,128)(2,1)}) custom-call(s32[4]{0:T(128)S(1)} %pad_add_fusion.sources_ref, bf16[128,1152]{1,0:T(8,128)(2,1)S(1)} %collective-permute-done.micro_ref.refs_0_, bf16[128,1152]{1,0:T(8,128)(2,1)} %collective-permute-done.1.refs_1_, bf16[128,1152]{1,0:T(8,128)(2,1)} %collective-permute-done.2.refs_2_, ...), custom_call_target="tpu_custom_call" | custom-call | flops 1000 | bytes 1000 | tf_op jit(solution)/shard_map/grad_products/pallas_call | solution.py:293
  41.5 2.0 %collective-permute-done.7.attn_ref = bf16[4,48,1024]{2,1,0:T(8,128)(2,1)S(1)} collective-permute-done((bf16[4,48,1024]{2,1,0:T(8,128)(2,1)}, bf16[4,48,1024]{2,1,0:T(8,128)(2,1)S(1)}, u32[]{:S(2)}, u32[]{:S(2)}) %collective-permute-start.7) | collective-permute-done | bytes 393248 | tf_op jit(solution)/shard_map/ppermute | solution.py:45
  43.5 1.8 %project.2 = (bf16[1,48,2048]{2,1,0:T(8,128)(2,1)S(1)}, bf16[1,48,2048]{2,1,0:T(8,128)(2,1)S(1)}, bf16[48,4096]{1,0:T(8,128)(2,1)S(1)}, bf16[2,48,4096]{2,1,0:T(8,128)(2,1)S(1)}) custom-call(s32[1]{0:T(128)} %bitcast.1.place_ref, bf16[4,48,1024]{2,1,0:T(8,128)(2,1)S(1)} %collective-permute-done.7.attn_ref, bf16[1024,4096]{1,0:T(8,128)(2,1)S(1)} %bitcast.17), custom_call_target="tpu_custom_call" | custom-call | flops 1000 | bytes 1000 | tf_op jit(solution)/shard_map/project/pallas_call | solution.py:341
  46.0 2.0 %collective-permute-done.9.refs_2_ = bf16[128,1536]{1,0:T(8,128)(2,1)S(1)} collective-permute-done((bf16[128,1536]{1,0:T(8,128)(2,1)S(1)}, bf16[128,1536]{1,0:T(8,128)(2,1)S(1)}, u32[]{:S(2)}, u32[]{:S(2)}) %collective-permute-start.9) | collective-permute-done | bytes 393248 | tf_op jit(solution)/shard_map/ppermute | solution.py:55
  50.4 5.1 %grad_products.4 = (f32[512,1024]{1,0:T(8,128)S(1)}, bf16[1024,4096]{1,0:T(8,128)(2,1)}) custom-call(s32[4]{0:T(128)S(1)} %pad_add_fusion.sources_ref, bf16[128,1536]{1,0:T(8,128)(2,1)S(1)} %collective-permute-done.4.refs_0_, bf16[128,1536]{1,0:T(8,128)(2,1)S(1)} %collective-permute-done.12.refs_1_, ...), custom_call_target="tpu_custom_call", output_to_operand_aliasing={{1}: (8, {})} | custom-call | flops 1000 | bytes 1000 | tf_op jit(solution)/shard_map/grad_products/pallas_call | solution.py:293
  55.5 2.0 %collective-permute-done.16.attn_ref = bf16[4,80,1024]{2,1,0:T(8,128)(2,1)S(1)} collective-permute-done((bf16[4,80,1024]{2,1,0:T(8,128)(2,1)}, bf16[4,80,1024]{2,1,0:T(8,128)(2,1)S(1)}, u32[]{:S(2)}, u32[]{:S(2)}) %collective-permute-start.16) | collective-permute-done | bytes 655392 | tf_op jit(solution)/shard_map/ppermute | solution.py:45
  57.6 2.9 %project.3 = (bf16[1,80,2048]{2,1,0:T(8,128)(2,1)S(1)}, bf16[1,80,2048]{2,1,0:T(8,128)(2,1)S(1)}, bf16[80,4096]{1,0:T(8,128)(2,1)S(1)}, bf16[2,80,4096]{2,1,0:T(8,128)(2,1)S(1)}) custom-call(s32[1]{0:T(128)} %bitcast.1.place_ref, bf16[4,80,1024]{2,1,0:T(8,128)(2,1)S(1)} %collective-permute-done.16.attn_ref, bf16[1024,4096]{1,0:T(8,128)(2,1)S(1)} %bitcast.19), custom_call_target="tpu_custom_call" | custom-call | flops 1000 | bytes 1000 | tf_op jit(solution)/shard_map/project/pallas_call | solution.py:341
  61.1 1.0 %collective-permute-done.19.refs_0_ = bf16[1,80,2048]{2,1,0:T(8,128)(2,1)S(1)} collective-permute-done((bf16[1,80,2048]{2,1,0:T(8,128)(2,1)S(1)}, bf16[1,80,2048]{2,1,0:T(8,128)(2,1)S(1)}, u32[]{:S(2)}, u32[]{:S(2)}) %collective-permute-start.19) | collective-permute-done | bytes 327712 | tf_op jit(solution)/shard_map/ppermute | solution.py:50
  62.8 1.5 %collective-permute-start.22 = (bf16[80,4096]{1,0:T(8,128)(2,1)S(1)}, bf16[80,4096]{1,0:T(8,128)(2,1)S(1)}, u32[]{:S(2)}, u32[]{:S(2)}) collective-permute-start(bf16[80,4096]{1,0:T(8,128)(2,1)S(1)} %pair_sum.3), channel_id=1, source_target_pairs={{0,2},{1,3},{2,0},{3,1},{4,6},{5,7},{6,4},{7,5},{8,10},{9,11},{10,... | collective-permute-start | bytes 1966088 | tf_op jit(solution)/shard_map/ppermute | solution.py:55
  64.3 1.7 %collective-permute-done.21.refs_3_ = bf16[128,1536]{1,0:T(8,128)(2,1)S(1)} collective-permute-done((bf16[128,1536]{1,0:T(8,128)(2,1)S(1)}, bf16[128,1536]{1,0:T(8,128)(2,1)S(1)}, u32[]{:S(2)}, u32[]{:S(2)}) %collective-permute-start.21) | collective-permute-done | bytes 393248 | tf_op jit(solution)/shard_map/ppermute | solution.py:50
  66.1 5.1 %grad_products.5 = (bf16[512,1024]{1,0:T(8,128)(2,1)S(1)}, bf16[1024,4096]{1,0:T(8,128)(2,1)}) custom-call(s32[4]{0:T(128)S(1)} %pad_add_fusion.sources_ref, bf16[128,1536]{1,0:T(8,128)(2,1)S(1)} %collective-permute-done.3.refs_0_, bf16[128,1536]{1,0:T(8,128)(2,1)S(1)} %collective-permute-done.15.refs_1_, ...), custom_call_target="tpu_custom_call", output_to_operand_aliasing={{1}: (8, {})} | custom-call | flops 1000 | bytes 1000 | tf_op jit(solution)/shard_map/grad_products/pallas_call | solution.py:293
  71.2 5.0 %backward_attention.1 = (bf16[512,1024]{1,0:T(8,128)(2,1)}, bf16[2,512,256]{2,1,0:T(8,128)(2,1)}) custom-call(bf16[512,1024]{1,0:T(8,128)(2,1)S(1)} %bitcast.22, bf16[2,512,256]{2,1,0:T(8,128)(2,1)S(1)} %bitcast.24, bf16[512,1024]{1,0:T(8,128)(2,1)S(1)} %get-tuple-element.76.grad_ref, bf16[2,4,512,512]{3,2,1,0:T(8,128)(2,1)S(1)} %copy-done.2), custom_call_target="tpu_custom_call" | custom-call | flops 1000 | bytes 1000 | tf_op jit(solution)/shard_map/backward_attention/pallas_call | solution.py:230
  76.2 3.1 %collective-permute-done.8.resid_ref = bf16[128,4096]{1,0:T(8,128)(2,1)S(1)} collective-permute-done((bf16[128,4096]{1,0:T(8,128)(2,1)S(1)}, bf16[128,4096]{1,0:T(8,128)(2,1)S(1)}, u32[]{:S(2)}, u32[]{:S(2)}) %collective-permute-start.8) | collective-permute-done | bytes 1048608 | tf_op jit(solution)/shard_map/ppermute | solution.py:45
  79.6 1.2 %finish.1 = bf16[128,4096]{1,0:T(8,128)(2,1)} custom-call(bf16[128,4096]{1,0:T(8,128)(2,1)S(1)} %collective-permute-done.8.resid_ref, bf16[2,48,4096]{2,1,0:T(8,128)(2,1)S(1)} %get-tuple-element.54.keep_ref.refs_0_, bf16[48,4096]{1,0:T(8,128)(2,1)S(1)} %collective-permute-done.14.refs_1_, bf16[48,4096]{1,0:T(8,128)(2,1)S(1)} %collective-permute-done.18.refs_2_, ...), custom_call_target="tpu_custom_call" | custom-call | flops 1000 | bytes 1000 | tf_op jit(solution)/shard_map/finish/pallas_call | solution.py:419
  (52 shorter events, 8.3 us)
Async XLA Ops:
  2.3 17.5 %collective-permute-start = (bf16[128,1152]{1,0:T(8,128)(2,1)S(1)}, bf16[128,1152]{1,0:T(8,128)(2,1)S(1)}, u32[]{:S(2)}, u32[]{:S(2)}) collective-permute-start(bf16[128,1152]{1,0:T(8,128)(2,1)S(1)} %slice_select_fusion), channel_id=1, source_target_pairs={{0,28},{4,0},{8,4},{12,8},{16,12},{20,16},{24,20},{28,24},{1,29},{... | collective-permute-start | bytes 884744 | tf_op jit(solution)/shard_map/ppermute | solution.py:45
  9.5 18.6 %collective-permute-start.4 = (bf16[128,1536]{1,0:T(8,128)(2,1)S(1)}, bf16[128,1536]{1,0:T(8,128)(2,1)S(1)}, u32[]{:S(2)}, u32[]{:S(2)}) collective-permute-start(bf16[128,1536]{1,0:T(8,128)(2,1)S(1)} %get-tuple-element.82), channel_id=1, source_target_pairs={{0,28},{4,0},{8,4},{12,8},{16,12},{20,16},{24,20},{28,24},{1,29},{... | collective-permute-start | bytes 1179656 | tf_op jit(solution)/shard_map/ppermute | solution.py:45
  10.1 21.4 %collective-permute-start.3 = (bf16[128,1536]{1,0:T(8,128)(2,1)S(1)}, bf16[128,1536]{1,0:T(8,128)(2,1)S(1)}, u32[]{:S(2)}, u32[]{:S(2)}) collective-permute-start(bf16[128,1536]{1,0:T(8,128)(2,1)S(1)} %get-tuple-element.83), channel_id=1, source_target_pairs={{0,28},{4,0},{8,4},{12,8},{16,12},{20,16},{24,20},{28,24},{1,29},{... | collective-permute-start | bytes 1179656 | tf_op jit(solution)/shard_map/ppermute | solution.py:45
  19.8 11.6 %collective-permute-start.2 = (bf16[128,1152]{1,0:T(8,128)(2,1)S(1)}, bf16[128,1152]{1,0:T(8,128)(2,1)}, u32[]{:S(2)}, u32[]{:S(2)}) collective-permute-start(bf16[128,1152]{1,0:T(8,128)(2,1)S(1)} %collective-permute-done.micro_ref.refs_0_), channel_id=1, source_target_pairs={{0,2},{1,3},{2,0},{3,1},{4,6},{5,7},{6,4},{7,5},{8,10},{9,11},{10,... | collective-permute-start | bytes 884744 | tf_op jit(solution)/shard_map/ppermute | solution.py:55
  21.3 11.7 %collective-permute-start.1 = (bf16[128,1152]{1,0:T(8,128)(2,1)S(1)}, bf16[128,1152]{1,0:T(8,128)(2,1)}, u32[]{:S(2)}, u32[]{:S(2)}) collective-permute-start(bf16[128,1152]{1,0:T(8,128)(2,1)S(1)} %collective-permute-done.micro_ref.refs_0_), channel_id=1, source_target_pairs={{0,1},{1,0},{2,3},{3,2},{4,5},{5,4},{6,7},{7,6},{8,9},{9,8},{10,11... | collective-permute-start | bytes 884744 | tf_op jit(solution)/shard_map/ppermute | solution.py:50
  28.1 13.4 %collective-permute-start.6 = (bf16[128,1536]{1,0:T(8,128)(2,1)S(1)}, bf16[128,1536]{1,0:T(8,128)(2,1)S(1)}, u32[]{:S(2)}, u32[]{:S(2)}) collective-permute-start(bf16[128,1536]{1,0:T(8,128)(2,1)S(1)} %collective-permute-done.4.refs_0_), channel_id=1, source_target_pairs={{0,2},{1,3},{2,0},{3,1},{4,6},{5,7},{6,4},{7,5},{8,10},{9,11},{10,... | collective-permute-start | bytes 1179656 | tf_op jit(solution)/shard_map/ppermute | solution.py:55
  28.7 14.9 %collective-permute-start.7 = (bf16[4,48,1024]{2,1,0:T(8,128)(2,1)}, bf16[4,48,1024]{2,1,0:T(8,128)(2,1)S(1)}, u32[]{:S(2)}, u32[]{:S(2)}) collective-permute-start(bf16[4,48,1024]{2,1,0:T(8,128)(2,1)} %get-tuple-element.53), channel_id=1, source_target_pairs={{0,4},{4,8},{8,12},{12,16},{16,20},{20,24},{24,28},{28,0},{1,5},{5... | collective-permute-start | bytes 1179656 | tf_op jit(solution)/shard_map/ppermute | solution.py:45
  31.5 1.9 %collective-permute-start.5 = (bf16[128,1152]{1,0:T(8,128)(2,1)}, bf16[128,1152]{1,0:T(8,128)(2,1)}, u32[]{:S(2)}, u32[]{:S(2)}) collective-permute-start(bf16[128,1152]{1,0:T(8,128)(2,1)} %collective-permute-done.2.refs_2_), channel_id=1, source_target_pairs={{0,1},{1,0},{2,3},{3,2},{4,5},{5,4},{6,7},{7,6},{8,9},{9,8},{10,11... | collective-permute-start | bytes 884744 | tf_op jit(solution)/shard_map/ppermute | solution.py:50
  31.5 16.6 %collective-permute-start.9 = (bf16[128,1536]{1,0:T(8,128)(2,1)S(1)}, bf16[128,1536]{1,0:T(8,128)(2,1)S(1)}, u32[]{:S(2)}, u32[]{:S(2)}) collective-permute-start(bf16[128,1536]{1,0:T(8,128)(2,1)S(1)} %collective-permute-done.3.refs_0_), channel_id=1, source_target_pairs={{0,2},{1,3},{2,0},{3,1},{4,6},{5,7},{6,4},{7,5},{8,10},{9,11},{10,... | collective-permute-start | bytes 1179656 | tf_op jit(solution)/shard_map/ppermute | solution.py:55
  33.0 24.6 %collective-permute-start.16 = (bf16[4,80,1024]{2,1,0:T(8,128)(2,1)}, bf16[4,80,1024]{2,1,0:T(8,128)(2,1)S(1)}, u32[]{:S(2)}, u32[]{:S(2)}) collective-permute-start(bf16[4,80,1024]{2,1,0:T(8,128)(2,1)} %copy-done.6), channel_id=1, source_target_pairs={{0,4},{4,8},{8,12},{12,16},{16,20},{20,24},{24,28},{28,0},{1,5},{5... | collective-permute-start | bytes 1966088 | tf_op jit(solution)/shard_map/ppermute | solution.py:45
  36.8 13.0 %copy-start.7 = (bf16[1,128,4096]{2,1,0:T(8,128)(2,1)S(1)}, bf16[1,128,4096]{2,1,0:T(8,128)(2,1)}, u32[]{:S(2)}) copy-start(bf16[1,128,4096]{2,1,0:T(8,128)(2,1)} %param.10) | copy-start | bytes 3145732
  45.4 2.7 %collective-permute-start.10 = (bf16[1,48,2048]{2,1,0:T(8,128)(2,1)S(1)}, bf16[1,48,2048]{2,1,0:T(8,128)(2,1)S(1)}, u32[]{:S(2)}, u32[]{:S(2)}) collective-permute-start(bf16[1,48,2048]{2,1,0:T(8,128)(2,1)S(1)} %get-tuple-element.57), channel_id=1, source_target_pairs={{0,1},{1,0},{2,3},{3,2},{4,5},{5,4},{6,7},{7,6},{8,9},{9,8},{10,11... | collective-permute-start | bytes 589832 | tf_op jit(solution)/shard_map/ppermute | solution.py:50
  45.5 3.1 %collective-permute-start.11 = (bf16[1,48,2048]{2,1,0:T(8,128)(2,1)S(1)}, bf16[1,48,2048]{2,1,0:T(8,128)(2,1)S(1)}, u32[]{:S(2)}, u32[]{:S(2)}) collective-permute-start(bf16[1,48,2048]{2,1,0:T(8,128)(2,1)S(1)} %get-tuple-element.58), channel_id=1, source_target_pairs={{0,1},{1,0},{2,3},{3,2},{4,5},{5,4},{6,7},{7,6},{8,9},{9,8},{10,11... | collective-permute-start | bytes 589832 | tf_op jit(solution)/shard_map/ppermute | solution.py:50
  45.9 2.8 %collective-permute-start.12 = (bf16[128,1536]{1,0:T(8,128)(2,1)S(1)}, bf16[128,1536]{1,0:T(8,128)(2,1)S(1)}, u32[]{:S(2)}, u32[]{:S(2)}) collective-permute-start(bf16[128,1536]{1,0:T(8,128)(2,1)S(1)} %collective-permute-done.4.refs_0_), channel_id=1, source_target_pairs={{0,1},{1,0},{2,3},{3,2},{4,5},{5,4},{6,7},{7,6},{8,9},{9,8},{10,11... | collective-permute-start | bytes 1179656 | tf_op jit(solution)/shard_map/ppermute | solution.py:50
  48.1 1.7 %collective-permute-start.13 = (bf16[128,1536]{1,0:T(8,128)(2,1)S(1)}, bf16[128,1536]{1,0:T(8,128)(2,1)S(1)}, u32[]{:S(2)}, u32[]{:S(2)}) collective-permute-start(bf16[128,1536]{1,0:T(8,128)(2,1)S(1)} %collective-permute-done.6.refs_2_), channel_id=1, source_target_pairs={{0,1},{1,0},{2,3},{3,2},{4,5},{5,4},{6,7},{7,6},{8,9},{9,8},{10,11... | collective-permute-start | bytes 1179656 | tf_op jit(solution)/shard_map/ppermute | solution.py:50
  48.1 7.4 %collective-permute-start.15 = (bf16[128,1536]{1,0:T(8,128)(2,1)S(1)}, bf16[128,1536]{1,0:T(8,128)(2,1)S(1)}, u32[]{:S(2)}, u32[]{:S(2)}) collective-permute-start(bf16[128,1536]{1,0:T(8,128)(2,1)S(1)} %collective-permute-done.3.refs_0_), channel_id=1, source_target_pairs={{0,1},{1,0},{2,3},{3,2},{4,5},{5,4},{6,7},{7,6},{8,9},{9,8},{10,11... | collective-permute-start | bytes 1179656 | tf_op jit(solution)/shard_map/ppermute | solution.py:50
  48.6 6.9 %collective-permute-start.14 = (bf16[48,4096]{1,0:T(8,128)(2,1)S(1)}, bf16[48,4096]{1,0:T(8,128)(2,1)S(1)}, u32[]{:S(2)}, u32[]{:S(2)}) collective-permute-start(bf16[48,4096]{1,0:T(8,128)(2,1)S(1)} %get-tuple-element.63), channel_id=1, source_target_pairs={{0,1},{1,0},{2,3},{3,2},{4,5},{5,4},{6,7},{7,6},{8,9},{9,8},{10,11... | collective-permute-start | bytes 1179656 | tf_op jit(solution)/shard_map/ppermute | solution.py:50
  48.8 12.4 %collective-permute-start.18 = (bf16[48,4096]{1,0:T(8,128)(2,1)S(1)}, bf16[48,4096]{1,0:T(8,128)(2,1)S(1)}, u32[]{:S(2)}, u32[]{:S(2)}) collective-permute-start(bf16[48,4096]{1,0:T(8,128)(2,1)S(1)} %pair_sum.2), channel_id=1, source_target_pairs={{0,2},{1,3},{2,0},{3,1},{4,6},{5,7},{6,4},{7,5},{8,10},{9,11},{10,... | collective-permute-start | bytes 1179656 | tf_op jit(solution)/shard_map/ppermute | solution.py:55
  49.8 29.5 %collective-permute-start.8 = (bf16[128,4096]{1,0:T(8,128)(2,1)S(1)}, bf16[128,4096]{1,0:T(8,128)(2,1)S(1)}, u32[]{:S(2)}, u32[]{:S(2)}) collective-permute-start(bf16[128,4096]{1,0:T(8,128)(2,1)S(1)} %bitcast.31), channel_id=1, source_target_pairs={{0,4},{4,8},{8,12},{12,16},{16,20},{20,24},{24,28},{28,0},{1,5},{5... | collective-permute-start | bytes 3145736 | tf_op jit(solution)/shard_map/ppermute | solution.py:45
  60.5 1.7 %collective-permute-start.19 = (bf16[1,80,2048]{2,1,0:T(8,128)(2,1)S(1)}, bf16[1,80,2048]{2,1,0:T(8,128)(2,1)S(1)}, u32[]{:S(2)}, u32[]{:S(2)}) collective-permute-start(bf16[1,80,2048]{2,1,0:T(8,128)(2,1)S(1)} %get-tuple-element.71), channel_id=1, source_target_pairs={{0,1},{1,0},{2,3},{3,2},{4,5},{5,4},{6,7},{7,6},{8,9},{9,8},{10,11... | collective-permute-start | bytes 983048 | tf_op jit(solution)/shard_map/ppermute | solution.py:50
  60.6 2.1 %collective-permute-start.20 = (bf16[1,80,2048]{2,1,0:T(8,128)(2,1)S(1)}, bf16[1,80,2048]{2,1,0:T(8,128)(2,1)S(1)}, u32[]{:S(2)}, u32[]{:S(2)}) collective-permute-start(bf16[1,80,2048]{2,1,0:T(8,128)(2,1)S(1)} %get-tuple-element.72), channel_id=1, source_target_pairs={{0,1},{1,0},{2,3},{3,2},{4,5},{5,4},{6,7},{7,6},{8,9},{9,8},{10,11... | collective-permute-start | bytes 983048 | tf_op jit(solution)/shard_map/ppermute | solution.py:50
  61.1 10.1 %collective-permute-start.17 = (bf16[80,4096]{1,0:T(8,128)(2,1)S(1)}, bf16[80,4096]{1,0:T(8,128)(2,1)S(1)}, u32[]{:S(2)}, u32[]{:S(2)}) collective-permute-start(bf16[80,4096]{1,0:T(8,128)(2,1)S(1)} %get-tuple-element.67), channel_id=1, source_target_pairs={{0,1},{1,0},{2,3},{3,2},{4,5},{5,4},{6,7},{7,6},{8,9},{9,8},{10,11... | collective-permute-start | bytes 1966088 | tf_op jit(solution)/shard_map/ppermute | solution.py:50
  62.8 16.8 %collective-permute-start.22 = (bf16[80,4096]{1,0:T(8,128)(2,1)S(1)}, bf16[80,4096]{1,0:T(8,128)(2,1)S(1)}, u32[]{:S(2)}, u32[]{:S(2)}) collective-permute-start(bf16[80,4096]{1,0:T(8,128)(2,1)S(1)} %pair_sum.3), channel_id=1, source_target_pairs={{0,2},{1,3},{2,0},{3,1},{4,6},{5,7},{6,4},{7,5},{8,10},{9,11},{10,... | collective-permute-start | bytes 1966088 | tf_op jit(solution)/shard_map/ppermute | solution.py:55
  64.3 1.7 %collective-permute-start.21 = (bf16[128,1536]{1,0:T(8,128)(2,1)S(1)}, bf16[128,1536]{1,0:T(8,128)(2,1)S(1)}, u32[]{:S(2)}, u32[]{:S(2)}) collective-permute-start(bf16[128,1536]{1,0:T(8,128)(2,1)S(1)} %collective-permute-done.9.refs_2_), channel_id=1, source_target_pairs={{0,1},{1,0},{2,3},{3,2},{4,5},{5,4},{6,7},{7,6},{8,9},{9,8},{10,11... | collective-permute-start | bytes 1179656 | tf_op jit(solution)/shard_map/ppermute | solution.py:50
  (7 other events, 27.0 us)
